TPU v7x, 32 devices: a whole 2x2x4 slice. The times are simulated.
32 devices in a mesh: tm: 8 (over z, x), sensor: 4 (over y, core).
Axes of the slice: x: 2, y: 2, z: 4, core: 2. Of those that a mesh axis runs over, the one named last changes fastest.
Arguments:
- state_tiles: bfloat16 [8192, 4096], P('sensor', 'tm'), may hold values from -6 to 6
- sketch: bfloat16 [1024, 128], replicated, may hold values from -0.1875 to 0.1875
- probe_cell: int32 [4, 4, 128], P('sensor'), may hold values from 0 to 2047
- probe_row: int32 [4, 4, 128], P('sensor'), may hold values from -1 to 255, as said below
Outputs:
- hankel_sketch: float32 [256, 1024, 128], P('tm', 'sensor')
- column_image: float32 [1024, 128], P(('tm', 'sensor'))
Inputs may be any that keep to these rules, and one draw needn't show every extreme that they name: `probe_row`: every sensor row of every owner is filled by exactly one slot over all tiles; for each owner, the tiles that feed it fill all 128 of their slots to it and the other tiles none, and exactly half of the tiles feed each owner.
All inputs are finite; a program needn't handle non-finite values.
Results may differ from a plain program's by a relative error of at most 0.0003.
Values may be sent and summed in bfloat16 or wider, within the bound.
No kernel may reach another device: no remote copies, remote signals or barrier semaphores. Data moves between devices by JAX's collectives and lax.ppermute only.
A program may use at most 64 MiB of HBM per device.

v0:
```python
import math

import jax
import jax.numpy as jnp
from jax import lax
from jax.sharding import PartitionSpec as P

INPUTS = 16
SENS_DEV = 256


def shifted(x, axis, by):
    count = lax.axis_size(axis)
    pairs = [(i, i + by) for i in range(count) if 0 <= i + by < count]
    return lax.ppermute(x, axis, pairs)


def local(state_tiles, sketch, probe_cell, probe_row):
    n_tiles = lax.axis_size("sensor")
    cells_here = state_tiles.shape[0]
    width = state_tiles.shape[1]
    steps_here = width // INPUTS
    capacity = probe_cell.shape[2]
    cell_index = probe_cell[0].reshape(-1)
    onehot = (cell_index[:, None] == jnp.arange(cells_here, dtype=jnp.int32)[None, :]).astype(
        jnp.bfloat16
    )
    picked = jnp.dot(onehot, state_tiles, preferred_element_type=jnp.float32).astype(jnp.bfloat16)
    picked = picked.reshape(n_tiles, capacity, width)
    arrived = lax.all_to_all(picked, "sensor", split_axis=0, concat_axis=0, tiled=True)
    row_index = probe_row[0].reshape(-1)
    placement = (row_index[None, :] == jnp.arange(SENS_DEV, dtype=jnp.int32)[:, None]).astype(
        jnp.bfloat16
    )
    own_block = jnp.dot(
        placement, arrived.reshape(n_tiles * capacity, width), preferred_element_type=jnp.float32
    ).astype(jnp.bfloat16)
    next_one = shifted(own_block, "tm", -1)
    next_two = shifted(own_block, "tm", -2)
    extended = jnp.concatenate([own_block, next_one, next_two], axis=1)
    span = sketch.shape[0]
    group_size = math.gcd(steps_here, 8)
    total = jnp.zeros((span, sketch.shape[1]), jnp.float32)
    pieces = []
    for block in range(steps_here // group_size):
        windows = jnp.stack(
            [
                extended[
                    :,
                    (block * group_size + offset) * INPUTS : (block * group_size + offset) * INPUTS
                    + span,
                ]
                for offset in range(group_size)
            ]
        )
        image = jnp.einsum("isk,kc->isc", windows, sketch, preferred_element_type=jnp.float32)
        image_bf = image.astype(jnp.bfloat16)
        total = total + jnp.einsum(
            "isk,isc->kc", windows, image_bf, preferred_element_type=jnp.float32
        )
        pieces.append(image)
    hankel_sketch = jnp.concatenate(pieces, axis=0)
    norm_scale = 1.0 / math.sqrt(SENS_DEV * n_tiles * steps_here * lax.axis_size("tm"))
    total = total * norm_scale
    column_image = lax.psum_scatter(total, ("tm", "sensor"), scatter_dimension=0, tiled=True)
    return (hankel_sketch, column_image)


def solution(mesh):
    placed = (P("sensor", "tm"), P(), P("sensor", None, None), P("sensor", None, None))
    return jax.shard_map(
        local,
        mesh=mesh,
        in_specs=placed,
        out_specs=(P("tm", "sensor", None), P(("tm", "sensor"), None)),
        check_vma=False,
    )
```

profile of v0, /device:TPU:0, one launch (start us, length us, event | category | flops | bytes accessed | tf_op | source)
XLA Modules:
  0.0 200.4 jit_solution(9799325964802012517)
XLA Ops:
  7.2 0.0 copy-start
  7.2 0.0 reduce-scatter.2.cloned.1.call-start
  7.2 1.5 copy-done
  8.8 2.0 fusion.2
  10.8 12.9 %all_to_all.5 = bf16[4,128,512]{2,1,0:T(8,128)(2,1)S(1)} all-to-all(bf16[4,128,512]{2,1,0:T(8,128)(2,1)S(1)} %bitcast.168), channel_id=1, replica_groups=mesh['tm'=8,'sensor'=4] {'sensor'}, dimensions={0} | all-to-all | bytes 1048576 | tf_op jit(solution)/shard_map/all_to_all | solution.py:30
  23.6 0.3 convolution_convert_fusion
  24.0 1.3 collective-permute-start.1
  25.3 1.3 collective-permute-start
  26.6 8.5 %collective-permute-done.1 = bf16[256,512]{1,0:T(8,128)(2,1)S(1)} collective-permute-done((bf16[256,512]{1,0:T(8,128)(2,1)S(1)}, bf16[256,512]{1,0:T(8,128)(2,1)S(1)}, u32[]{:S(2)}, u32[]{:S(2)}) %collective-permute-start.1) | collective-permute-done | bytes 262176 | tf_op jit(solution)/shard_map/ppermute | solution.py:15
  35.1 0.0 collective-permute-done
  35.1 0.1 pad_maximum_fusion.1
  35.2 0.2 fusion.30
  35.3 0.1 fusion.38
  35.4 1.0 fusion.37
  36.4 1.0 fusion.36
  37.3 1.0 fusion.35
  38.3 1.0 fusion.34
  39.3 1.0 fusion.33
  40.3 0.0 copy-start.3
  40.3 1.0 fusion.32
  41.3 1.0 fusion.31
  42.2 1.3 fusion.49
  43.5 1.3 fusion.43
  44.8 1.3 convolution_bitcast_fusion
  46.1 1.3 fusion.45
  47.4 1.5 convolution_bitcast_fusion.1
  48.9 2.3 %fusion.47 = f32[8,256,128]{2,1,0:T(8,128)} fusion(bf16[8,256,1024]{2,1,0:T(8,128)(2,1)S(1)} %get-tuple-element.5, bf16[1024,128]{1,0:T(8,128)(2,1)S(1)} %copy-done.3), kind=kOutput, calls=%fused_computation.88 | convolution fusion | flops 536870912 | bytes 5505024 | tf_op jit(solution)/shard_map/isk,kc->isc/dot_general | solution.py:56
  51.2 2.5 %convolution_bitcast_fusion.2 = f32[1024,128]{1,0:T(8,128)S(1)} fusion(bf16[8,256,1024]{2,1,0:T(8,128)(2,1)S(1)} %get-tuple-element.5, f32[8,256,128]{2,1,0:T(8,128)} %fusion.47), kind=kOutput, calls=%fused_computation.7 | convolution fusion | flops 537133056 | bytes 5767168 | tf_op jit(solution)/shard_map/isk,isc->kc/dot_general | solution.py:58
  53.7 2.2 %fusion.6 = f32[1024,128]{1,0:T(8,128)} fusion(f32[1024,128]{1,0:T(8,128)S(1)} %convolution_bitcast_fusion, f32[1024,128]{1,0:T(8,128)S(1)} %convolution_bitcast_fusion.1, f32[1024,128]{1,0:T(8,128)S(1)} %convolution_bitcast_fusion.2, bf16[8,256,1024]{2,1,0:T(8,128)(2,1)S(1)} %get-tuple-element.2, f32[8,256,128]{2,1,0:T(8,128)S(1)} %fusion.49), kind=kOutput, calls=%fused_computation.12 | convolution fusion | flops 537657344 | bytes 7340032 | tf_op jit(solution)/shard_map/isk,isc->kc/dot_general | solution.py:58
  55.9 0.0 reduce-scatter.2.cloned.1.call-update
  55.9 4.3 %pad_maximum_fusion = f32[32,256,128]{2,1,0:T(8,128)} fusion(f32[8,256,128]{2,1,0:T(8,128)} %copy-done.1, f32[8,256,128]{2,1,0:T(8,128)} %copy-done.2, f32[8,256,128]{2,1,0:T(8,128)} %fusion.47, f32[8,256,128]{2,1,0:T(8,128)S(1)} %fusion.49), kind=kLoop, calls=%fused_computation | loop fusion | flops 3145728 | bytes 8388608 | tf_op jit(solution)/shard_map/concatenate | solution.py:62
  60.2 133.4 %reduce-scatter.2.cloned.1.call-done = f32[32,128]{1,0:T(8,128)} async-done(((f32[1024,128]{1,0:T(8,128)}), f32[32,128]{1,0:T(8,128)}) %reduce-scatter.2.cloned.1.call-update) | async-done | bytes 16400 | tf_op jit(solution)/shard_map/reduce_scatter | solution.py:65
  (7 shorter events, 0.0 us)
Async XLA Ops:
  7.2 1.6 copy-start
  7.2 186.4 %reduce-scatter.2.cloned.1.call-start = ((), (), s32[]{:S(2)}) async-start(), calls=%async_computation.2 | async-start | bytes 540672 | tf_op jit(solution)/shard_map/reduce_scatter | solution.py:65
  8.8 14.9 %copy-start.4 = (s32[1,4,128]{2,1,0:T(4,128)S(1)}, s32[1,4,128]{2,1,0:T(4,128)}, u32[]{:S(2)}) copy-start(s32[1,4,128]{2,1,0:T(4,128)} %param.7) | copy-start | bytes 6148
  24.0 11.1 %collective-permute-start.1 = (bf16[256,512]{1,0:T(8,128)(2,1)S(1)}, bf16[256,512]{1,0:T(8,128)(2,1)S(1)}, u32[]{:S(2)}, u32[]{:S(2)}) collective-permute-start(bf16[256,512]{1,0:T(8,128)(2,1)S(1)} %convolution_convert_fusion), channel_id=1, source_target_pairs={{8,0},{12,4},{16,8},{20,12},{24,16},{28,20},{9,1},{13,5},{17,9},{2... | collective-permute-start | bytes 786440 | tf_op jit(solution)/shard_map/ppermute | solution.py:15
  25.3 9.8 %collective-permute-start = (bf16[256,512]{1,0:T(8,128)(2,1)S(1)}, bf16[256,512]{1,0:T(8,128)(2,1)S(1)}, u32[]{:S(2)}, u32[]{:S(2)}) collective-permute-start(bf16[256,512]{1,0:T(8,128)(2,1)S(1)} %convolution_convert_fusion), channel_id=1, source_target_pairs={{4,0},{8,4},{12,8},{16,12},{20,16},{24,20},{28,24},{5,1},{9,5},{13... | collective-permute-start | bytes 786440 | tf_op jit(solution)/shard_map/ppermute | solution.py:15
  40.3 2.0 copy-start.3
  44.8 4.1 %copy-start.1 = (f32[8,256,128]{2,1,0:T(8,128)}, f32[8,256,128]{2,1,0:T(8,128)S(1)}, u32[]{:S(2)}) copy-start(f32[8,256,128]{2,1,0:T(8,128)S(1)} %fusion.43) | copy-start | bytes 3145732
  47.4 1.5 copy-start.2
Sparse Core Ops, SparseCore 0:
  56.0 137.5 reduce-scatter.1
where the time goes:
time: 201 us; the launch traced here: 200 us
  waiting for transfers between devices  142 us (71%)
  matrix products  15.9 us (8%)
  between operations  14.2 us (7%)
  blocking collectives  12.9 us (6%)
  local copies, waits for them, and re-layouts  8.49 us (4%)
  other arithmetic  4.43 us (2%)
  starting transfers between devices  2.62 us (1%)
    reduce_scatter x1, waiting for transfers between devices, local(): lax.psum_scatter(total, ('tm', 'sensor'), scatter_dimension=0, tiled=True)  133 us
    all_to_all x1, blocking collectives, local(): lax.all_to_all(picked, 'sensor', split_axis=0, concat_axis=0, tiled=True)  12.9 us
    ppermute x2, waiting for transfers between devices, shifted(): return lax.ppermute(x, axis, pairs)  8.54 us
    unnamed x17, local copies, waits for them, and re-layouts  7.52 us
    dot_general x4, matrix products, local(): jnp.einsum('isk,isc->kc', windows, image_bf, preferred_element_type=jnp.f...  7.52 us
    dot_general x4, matrix products, local(): jnp.einsum('isk,kc->isc', windows, sketch, preferred_element_type=jnp.flo...  6.03 us
    concatenate x1, other arithmetic, local(): hankel_sketch = jnp.concatenate(pieces, axis=0)  4.33 us
  transfers between devices with their start and end apart: 3, of which 2 were waited for; matrix products, arithmetic and copies ran while one was open for 2% of the time, Pallas kernels for 0%

commit v1 on v0

v1 whole, which is shorter than its diff:
```python
import math

import jax
import jax.numpy as jnp
from jax import lax
from jax.experimental import pallas as pl
from jax.experimental.pallas import tpu as pltpu
from jax.sharding import PartitionSpec as P

INPUTS = 16
SENS_DEV = 256
LANES = 128


def shifted(x, axis, by):
    count = lax.axis_size(axis)
    pairs = [(i, i + by) for i in range(count) if 0 <= i + by < count]
    return lax.ppermute(x, axis, pairs)


def crossed(x, axes, mask):
    count = math.prod(lax.axis_size(a) for a in axes)
    return lax.ppermute(x, axes, [(i, i ^ mask) for i in range(count)])


def exchange(parts, axis):
    count = lax.axis_size(axis)
    me = lax.axis_index(axis)
    got = [lax.dynamic_index_in_dim(parts, me, 0, keepdims=False)]
    for mask in range(1, count):
        got.append(crossed(lax.dynamic_index_in_dim(parts, me ^ mask, 0, keepdims=False), (axis,), mask))
    return got


def reduce_scatter(total, axes, rounds):
    count = math.prod(lax.axis_size(a) for a in axes)
    me = jnp.int32(0)
    for a in axes:
        me = me * lax.axis_size(a) + lax.axis_index(a)
    bits = int(math.log2(count))
    value = total.reshape((2,) * bits + (total.shape[0] // count, total.shape[1]))
    left = list(range(bits))
    for bunch in rounds:
        dims = [left.index(b) for b in bunch]
        value = jnp.moveaxis(value, dims, range(len(bunch)))
        rest = value.shape[len(bunch):]
        value = value.reshape((2 ** len(bunch),) + rest)
        mine = jnp.int32(0)
        for b in bunch:
            mine = mine * 2 + ((me >> (bits - 1 - b)) & 1)
        acc = lax.dynamic_index_in_dim(value, mine, 0, keepdims=False)
        for mask in range(1, 2 ** len(bunch)):
            flip = 0
            for place, b in enumerate(bunch):
                if (mask >> (len(bunch) - 1 - place)) & 1:
                    flip |= 1 << (bits - 1 - b)
            acc = acc + crossed(lax.dynamic_index_in_dim(value, mine ^ mask, 0, keepdims=False), axes, flip)
        value = acc
        for b in bunch:
            left.remove(b)
    return value


def products(blocks, wide, span, scale):
    rows, width = blocks[0].shape
    columns = wide.shape[1] // (LANES // INPUTS)
    group = LANES // INPUTS
    groups = width // LANES
    reach = wide.shape[0]
    n_blocks = len(blocks)

    def kernel(*refs):
        block_refs = refs[:n_blocks]
        wide_ref, out_ref, image_ref, ext, turned, rounded = refs[n_blocks:]
        g = pl.program_id(0)

        @pl.when(g == 0)
        def _():
            for b in range(n_blocks):
                ext[:, b * width : (b + 1) * width] = block_refs[b][...]

        window = ext[:, pl.ds(pl.multiple_of(g * LANES, LANES), reach)]
        image = jnp.dot(window, wide_ref[...], preferred_element_type=jnp.float32)
        at = pl.ds(pl.multiple_of(g * rows, rows), rows)
        rounded[at, :] = image.astype(jnp.bfloat16)
        for o in range(group):
            out_ref[o] = image[:, o * columns : (o + 1) * columns]
        turned[:, at] = window.T

        @pl.when(g == groups - 1)
        def _():
            image_ref[...] = jnp.zeros_like(image_ref)

            def pair(p, carry):
                first = pl.multiple_of(p * 2 * INPUTS, 2 * INPUTS)
                part = jnp.dot(
                    turned[pl.ds(first, span + INPUTS), :],
                    rounded[:, pl.ds(pl.multiple_of(p * 2 * columns, 2 * columns), 2 * columns)],
                    preferred_element_type=jnp.float32,
                )
                image_ref[...] += part[:span, :columns] + part[INPUTS:, columns:]
                return carry

            lax.fori_loop(0, group // 2, pair, 0)
            image_ref[...] *= scale

    return pl.pallas_call(
        kernel,
        grid=(groups,),
        in_specs=[pl.BlockSpec((rows, width), lambda g: (0, 0))] * n_blocks
        + [pl.BlockSpec(wide.shape, lambda g: (0, 0))],
        out_specs=[
            pl.BlockSpec((group, rows, columns), lambda g: (g, 0, 0)),
            pl.BlockSpec((span, columns), lambda g: (0, 0)),
        ],
        out_shape=[
            jax.ShapeDtypeStruct((groups * group, rows, columns), jnp.float32),
            jax.ShapeDtypeStruct((span, columns), jnp.float32),
        ],
        scratch_shapes=[
            pltpu.VMEM((rows, n_blocks * width), jnp.bfloat16),
            pltpu.VMEM((reach, groups * rows), jnp.bfloat16),
            pltpu.VMEM((groups * rows, group * columns), jnp.bfloat16),
        ],
        compiler_params=pltpu.CompilerParams(vmem_limit_bytes=48 * 1024 * 1024),
    )(*blocks, wide)


def local(state_tiles, sketch, probe_cell, probe_row):
    n_tiles = lax.axis_size("sensor")
    cells_here, width = state_tiles.shape
    steps_here = width // INPUTS
    capacity = probe_cell.shape[2]
    span, columns = sketch.shape
    cell_index = probe_cell[0].reshape(-1)
    onehot = (cell_index[:, None] == jnp.arange(cells_here, dtype=jnp.int32)[None, :]).astype(
        jnp.bfloat16
    )
    picked = jnp.dot(onehot, state_tiles, preferred_element_type=jnp.float32).astype(jnp.bfloat16)
    arrived = exchange(picked.reshape(n_tiles, capacity, width), "sensor")
    me = lax.axis_index("sensor")
    own_block = 0
    for mask in range(n_tiles):
        row_index = lax.dynamic_index_in_dim(probe_row[0], me ^ mask, 0, keepdims=False)
        placement = (row_index[None, :] == jnp.arange(SENS_DEV, dtype=jnp.int32)[:, None]).astype(
            jnp.bfloat16
        )
        own_block = own_block + jnp.dot(placement, arrived[mask], preferred_element_type=jnp.float32)
    own_block = own_block.astype(jnp.bfloat16)
    halos = -(-(span // INPUTS - 1) // steps_here)
    blocks = [own_block] + [shifted(own_block, "tm", -k) for k in range(1, halos + 1)]
    group = LANES // INPUTS
    wide = jnp.stack(
        [jnp.pad(sketch, ((o * INPUTS, LANES - o * INPUTS), (0, 0))) for o in range(group)], axis=1
    ).reshape(span + LANES, group * columns)
    scale = 1.0 / math.sqrt(SENS_DEV * n_tiles * steps_here * lax.axis_size("tm"))
    hankel_sketch, total = products(blocks, wide, span, scale)
    tm_bits = int(math.log2(lax.axis_size("tm")))
    sensor_bits = int(math.log2(n_tiles))
    last = tm_bits + sensor_bits - 1
    rounds = [[last], list(range(tm_bits - 1, last)), list(range(tm_bits - 1))]
    column_image = reduce_scatter(total, ("tm", "sensor"), rounds)
    return (hankel_sketch, column_image)


def solution(mesh):
    placed = (P("sensor", "tm"), P(), P("sensor", None, None), P("sensor", None, None))
    return jax.shard_map(
        local,
        mesh=mesh,
        in_specs=placed,
        out_specs=(P("tm", "sensor", None), P(("tm", "sensor"), None)),
        check_vma=False,
    )
```

time: 201 us -> 59 us (0.29)
  waiting for transfers between devices: 142 us -> 27 us
  between operations: 14.2 us -> 0.87 us
  blocking collectives: 12.9 us -> 0 us
  matrix products: 15.9 us -> 3.77 us
  starting transfers between devices: 2.62 us -> 13.4 us
  Pallas kernels: 0 us -> 7.6 us
  other arithmetic: 4.43 us -> 0.67 us
  local copies, waits for them, and re-layouts: 8.49 us -> 5.4 us
    reduce_scatter x1 -> x0, waiting for transfers between devices: 133 us -> none  [local(): lax.psum_scatter(total, ('tm', 'sensor'), scatter_dimension=0, tiled=True)]
    ppermute x0 -> x10, waiting for transfers between devices: none -> 15 us  [crossed(): return lax.ppermute(x, axes, [(i, i ^ mask) for i in range(count)])]
    all_to_all x1 -> x0, blocking collectives: 12.9 us -> none  [local(): lax.all_to_all(picked, 'sensor', split_axis=0, concat_axis=0, tiled=True)]
    dot_general x9 -> x4, matrix products: 13.9 us -> 1.76 us  [local(): jnp.dot(placement, arrived[mask], preferred_element_type=jnp.float32)]
    ppermute x0 -> x10, starting transfers between devices: none -> 10.8 us  [crossed(): return lax.ppermute(x, axes, [(i, i ^ mask) for i in range(count)])]
    pallas_call x0 -> x1, Pallas kernels: none -> 7.6 us  [products(): pl.pallas_call(kernel, grid=(groups,), in_specs=[pl.BlockSpec((rows, widt...]
    concatenate x2 -> x0, other arithmetic: 4.38 us -> none  [the longest x1 4.33 us: local(): hankel_sketch = jnp.concatenate(pieces, axis=0)]
    unnamed x17 -> x15, local copies, waits for them, and re-layouts: 7.52 us -> 3.51 us
  transfers between devices with their start and end apart: 3 -> 12, of which waited for: 2 -> 10; matrix products, arithmetic and copies ran while one was open for 2% -> 5% of each run, Pallas kernels for 0% -> 0%
where the time goes in v1:
time: 59 us; the launch traced here: 58.8 us
  waiting for transfers between devices  27 us (46%)
  starting transfers between devices  13.4 us (23%)
  Pallas kernels  7.6 us (13%)
  local copies, waits for them, and re-layouts  5.4 us (9%)
  matrix products  3.77 us (6%)
  between operations  0.87 us (1%)
  other arithmetic  0.67 us (1%)
    ppermute x10, waiting for transfers between devices, crossed(): return lax.ppermute(x, axes, [(i, i ^ mask) for i in range(count)])  15 us
    ppermute x2, waiting for transfers between devices, shifted(): return lax.ppermute(x, axis, pairs)  12 us
    ppermute x10, starting transfers between devices, crossed(): return lax.ppermute(x, axes, [(i, i ^ mask) for i in range(count)])  10.8 us
    pallas_call x1, Pallas kernels, products(): pl.pallas_call(kernel, grid=(groups,), in_specs=[pl.BlockSpec((rows, widt...  7.6 us
    unnamed x15, local copies, waits for them, and re-layouts  3.51 us
    ppermute x2, starting transfers between devices, shifted(): return lax.ppermute(x, axis, pairs)  2.58 us
    dot_general x1, matrix products, local(): jnp.dot(onehot, state_tiles, preferred_element_type=jnp.float32)  2.01 us
    dot_general x4, matrix products, local(): jnp.dot(placement, arrived[mask], preferred_element_type=jnp.float32)  1.76 us
  transfers between devices with their start and end apart: 12, of which 10 were waited for; matrix products, arithmetic and copies ran while one was open for 5% of the time, Pallas kernels for 0%

profile of v1, /device:TPU:0, one launch (start us, length us, event | category | flops | bytes accessed | tf_op | source)
XLA Modules:
  0.0 58.8 jit_solution(3190443929962898910)
XLA Ops:
  0.6 0.0 copy-start
  0.7 1.6 %copy-done = bf16[2048,512]{1,0:T(8,128)(2,1)S(1)} copy-done((bf16[2048,512]{1,0:T(8,128)(2,1)S(1)}, bf16[2048,512]{1,0:T(8,128)(2,1)}, u32[]{:S(2)}) %copy-start) | copy-done | bytes 2097176
  2.2 2.0 %fusion.2 = bf16[512,512]{1,0:T(8,128)(2,1)S(1)} fusion(bf16[2048,512]{1,0:T(8,128)(2,1)S(1)} %copy-done, s32[512]{0:T(512)} %bitcast.85), kind=kOutput, calls=%fused_computation.4 | convolution fusion | flops 1075052544 | bytes 2623488 | tf_op jit(solution)/shard_map/dot_general | solution.py:139
  4.3 0.5 collective-permute-start
  4.8 2.6 %collective-permute-start.2 = (bf16[128,512]{1,0:T(8,128)(2,1)S(1)}, bf16[128,512]{1,0:T(8,128)(2,1)S(1)}, u32[]{:S(2)}, u32[]{:S(2)}) collective-permute-start(bf16[128,512]{1,0:T(8,128)(2,1)S(1)} %get-tuple-element.7), channel_id=1, source_target_pairs={{0,3},{1,2},{2,1},{3,0},{4,7},{5,6},{6,5},{7,4},{8,11},{9,10},{10,... | collective-permute-start | bytes 393224 | tf_op jit(solution)/shard_map/ppermute | solution.py:23
  7.5 0.0 collective-permute-start.1
  7.5 0.2 fusion.5
  8.1 0.2 convolution_add_fusion.1
  8.4 2.9 %collective-permute-done.2 = bf16[128,512]{1,0:T(8,128)(2,1)S(1)} collective-permute-done((bf16[128,512]{1,0:T(8,128)(2,1)S(1)}, bf16[128,512]{1,0:T(8,128)(2,1)S(1)}, u32[]{:S(2)}, u32[]{:S(2)}) %collective-permute-start.2) | collective-permute-done | bytes 131104 | tf_op jit(solution)/shard_map/ppermute | solution.py:23
  11.3 0.2 fusion.8
  11.5 2.9 %collective-permute-done.1 = bf16[128,512]{1,0:T(8,128)(2,1)} collective-permute-done((bf16[128,512]{1,0:T(8,128)(2,1)S(1)}, bf16[128,512]{1,0:T(8,128)(2,1)}, u32[]{:S(2)}, u32[]{:S(2)}) %collective-permute-start.1) | collective-permute-done | bytes 131104 | tf_op jit(solution)/shard_map/ppermute | solution.py:23
  14.4 1.1 %fusion.4.refs_0_ = bf16[256,512]{1,0:T(8,128)(2,1)S(1)} fusion(f32[256,512]{1,0:T(8,128)S(1)} %fusion.8, f32[256,512]{1,0:T(8,128)S(1)} %convolution_add_fusion.1, bf16[128,512]{1,0:T(8,128)(2,1)} %collective-permute-done.1, s32[128]{0:T(128)S(1)} %get-tuple-element.15), kind=kOutput, calls=%fused_computation.8 | convolution fusion | flops 33980416 | bytes 1442304 | tf_op jit(solution)/shard_map/dot_general | solution.py:148
  15.5 1.3 %collective-permute-start.3 = (bf16[256,512]{1,0:T(8,128)(2,1)S(1)}, bf16[256,512]{1,0:T(8,128)(2,1)S(1)}, u32[]{:S(2)}, u32[]{:S(2)}) collective-permute-start(bf16[256,512]{1,0:T(8,128)(2,1)S(1)} %fusion.4.refs_0_), channel_id=1, source_target_pairs={{4,0},{8,4},{12,8},{16,12},{20,16},{24,20},{28,24},{5,1},{9,5},{13... | collective-permute-start | bytes 786440 | tf_op jit(solution)/shard_map/ppermute | solution.py:18
  16.8 1.3 %collective-permute-start.4 = (bf16[256,512]{1,0:T(8,128)(2,1)S(1)}, bf16[256,512]{1,0:T(8,128)(2,1)S(1)}, u32[]{:S(2)}, u32[]{:S(2)}) collective-permute-start(bf16[256,512]{1,0:T(8,128)(2,1)S(1)} %fusion.4.refs_0_), channel_id=1, source_target_pairs={{8,0},{12,4},{16,8},{20,12},{24,16},{28,20},{9,1},{13,5},{17,9},{2... | collective-permute-start | bytes 786440 | tf_op jit(solution)/shard_map/ppermute | solution.py:18
  18.1 1.8 %copy_bitcast_fusion.refs_3_ = bf16[1152,1024]{1,0:T(8,128)(2,1)} fusion(bf16[1152,8,128]{2,0,1:T(8,128)(2,1)S(1)} %bitcast_dynamic-update-slice_fusion), kind=kLoop, calls=%fused_computation.2 | loop fusion | bytes 4718592 | tf_op jit(solution)/shard_map/reshape | solution.py:155
  19.9 5.6 %collective-permute-done.3.refs_1_ = bf16[256,512]{1,0:T(8,128)(2,1)S(1)} collective-permute-done((bf16[256,512]{1,0:T(8,128)(2,1)S(1)}, bf16[256,512]{1,0:T(8,128)(2,1)S(1)}, u32[]{:S(2)}, u32[]{:S(2)}) %collective-permute-start.3) | collective-permute-done | bytes 262176 | tf_op jit(solution)/shard_map/ppermute | solution.py:18
  25.5 6.4 %collective-permute-done.4.refs_2_ = bf16[256,512]{1,0:T(8,128)(2,1)S(1)} collective-permute-done((bf16[256,512]{1,0:T(8,128)(2,1)S(1)}, bf16[256,512]{1,0:T(8,128)(2,1)S(1)}, u32[]{:S(2)}, u32[]{:S(2)}) %collective-permute-start.4) | collective-permute-done | bytes 262176 | tf_op jit(solution)/shard_map/ppermute | solution.py:18
  31.9 1.7 %copy-done.1 = bf16[1152,1024]{1,0:T(8,128)(2,1)S(1)} copy-done((bf16[1152,1024]{1,0:T(8,128)(2,1)S(1)}, bf16[1152,1024]{1,0:T(8,128)(2,1)}, u32[]{:S(2)}) %copy-start.1) | copy-done | bytes 2359320
  33.6 7.6 %shard_map.59 = (f32[32,256,128]{2,1,0:T(8,128)}, f32[1024,128]{1,0:T(8,128)S(1)}) custom-call(bf16[256,512]{1,0:T(8,128)(2,1)S(1)} %fusion.4.refs_0_, bf16[256,512]{1,0:T(8,128)(2,1)S(1)} %collective-permute-done.3.refs_1_, bf16[256,512]{1,0:T(8,128)(2,1)S(1)} %collective-permute-done.4.refs_2_, bf16[1152,1024]{1,0:T(8,128)(2,1)S(1)} %copy-done.1), custom_call_target="tpu_custom_call" | custom-call | tf_op jit(solution)/shard_map/pallas_call | solution.py:107
  41.2 0.1 collective-permute-start.5
  41.3 1.5 %collective-permute-done.5 = f32[2,2,2,2,32,128]{5,4,3,2,1,0:T(8,128)S(1)} collective-permute-done((f32[2,2,2,2,32,128]{5,4,3,2,1,0:T(8,128)S(1)}, f32[2,2,2,2,32,128]{5,4,3,2,1,0:T(8,128)S(1)}, u32[]{:S(2)}, u32[]{:S(2)}) %collective-permute-start.5) | collective-permute-done | bytes 262176 | tf_op jit(solution)/shard_map/ppermute | solution.py:23
  42.9 1.6 %collective-permute-start.6 = (f32[2,2,32,128]{3,2,1,0:T(8,128)S(1)}, f32[2,2,32,128]{3,2,1,0:T(8,128)S(1)}, u32[]{:S(2)}, u32[]{:S(2)}) collective-permute-start(f32[2,2,32,128]{3,2,1,0:T(8,128)S(1)} %get-tuple-element.9), channel_id=1, source_target_pairs={{0,2},{1,3},{2,0},{3,1},{4,6},{5,7},{6,4},{7,5},{8,10},{9,11},{10,... | collective-permute-start | bytes 196616 | tf_op jit(solution)/shard_map/ppermute | solution.py:23
  44.5 0.0 collective-permute-start.7
  44.5 2.0 %collective-permute-start.8 = (f32[2,2,32,128]{3,2,1,0:T(8,128)S(1)}, f32[2,2,32,128]{3,2,1,0:T(8,128)S(1)}, u32[]{:S(2)}, u32[]{:S(2)}) collective-permute-start(f32[2,2,32,128]{3,2,1,0:T(8,128)S(1)} %get-tuple-element.10), channel_id=1, source_target_pairs={{0,6},{1,7},{2,4},{3,5},{4,2},{5,3},{6,0},{7,1},{8,14},{9,15},{10,... | collective-permute-start | bytes 196616 | tf_op jit(solution)/shard_map/ppermute | solution.py:23
  46.4 0.8 %collective-permute-done.6 = f32[2,2,32,128]{3,2,1,0:T(8,128)S(1)} collective-permute-done((f32[2,2,32,128]{3,2,1,0:T(8,128)S(1)}, f32[2,2,32,128]{3,2,1,0:T(8,128)S(1)}, u32[]{:S(2)}, u32[]{:S(2)}) %collective-permute-start.6) | collective-permute-done | bytes 65568 | tf_op jit(solution)/shard_map/ppermute | solution.py:23
  47.2 1.8 %collective-permute-done.7 = f32[2,2,32,128]{3,2,1,0:T(8,128)S(1)} collective-permute-done((f32[2,2,32,128]{3,2,1,0:T(8,128)S(1)}, f32[2,2,32,128]{3,2,1,0:T(8,128)S(1)}, u32[]{:S(2)}, u32[]{:S(2)}) %collective-permute-start.7) | collective-permute-done | bytes 65568 | tf_op jit(solution)/shard_map/ppermute | solution.py:23
  49.0 0.9 %collective-permute-done.8 = f32[2,2,32,128]{3,2,1,0:T(8,128)S(1)} collective-permute-done((f32[2,2,32,128]{3,2,1,0:T(8,128)S(1)}, f32[2,2,32,128]{3,2,1,0:T(8,128)S(1)}, u32[]{:S(2)}, u32[]{:S(2)}) %collective-permute-start.8) | collective-permute-done | bytes 65568 | tf_op jit(solution)/shard_map/ppermute | solution.py:23
  50.0 2.7 %collective-permute-start.10 = (f32[32,128]{1,0:T(8,128)S(1)}, f32[32,128]{1,0:T(8,128)S(1)}, u32[]{:S(2)}, u32[]{:S(2)}) collective-permute-start(f32[32,128]{1,0:T(8,128)S(1)} %get-tuple-element.14), channel_id=1, source_target_pairs={{0,16},{1,17},{2,18},{3,19},{4,20},{5,21},{6,22},{7,23},{8,24},{9,... | collective-permute-start | bytes 49160 | tf_op jit(solution)/shard_map/ppermute | solution.py:23
  52.6 1.3 %collective-permute-start.11 = (f32[32,128]{1,0:T(8,128)S(1)}, f32[32,128]{1,0:T(8,128)S(1)}, u32[]{:S(2)}, u32[]{:S(2)}) collective-permute-start(f32[32,128]{1,0:T(8,128)S(1)} %get-tuple-element.13), channel_id=1, source_target_pairs={{0,24},{1,25},{2,26},{3,27},{4,28},{5,29},{6,30},{7,31},{8,16},{9,... | collective-permute-start | bytes 49160 | tf_op jit(solution)/shard_map/ppermute | solution.py:23
  54.0 0.7 %collective-permute-done.10 = f32[32,128]{1,0:T(8,128)S(1)} collective-permute-done((f32[32,128]{1,0:T(8,128)S(1)}, f32[32,128]{1,0:T(8,128)S(1)}, u32[]{:S(2)}, u32[]{:S(2)}) %collective-permute-start.10) | collective-permute-done | bytes 16416 | tf_op jit(solution)/shard_map/ppermute | solution.py:23
  54.7 3.5 %collective-permute-done.11 = f32[32,128]{1,0:T(8,128)S(1)} collective-permute-done((f32[32,128]{1,0:T(8,128)S(1)}, f32[32,128]{1,0:T(8,128)S(1)}, u32[]{:S(2)}, u32[]{:S(2)}) %collective-permute-start.11) | collective-permute-done | bytes 16416 | tf_op jit(solution)/shard_map/ppermute | solution.py:23
  58.2 0.6 %fusion.16 = f32[32,128]{1,0:T(8,128)} fusion(f32[32,128]{1,0:T(8,128)S(1)} %collective-permute-done.11, f32[32,128]{1,0:T(8,128)S(1)} %collective-permute-done.10, f32[32,128]{1,0:T(8,128)S(1)} %collective-permute-done.9, f32[4,32,128]{2,1,0:T(8,128)S(1)} %bitcast.84, s32[]{:T(128)S(6)} %select_n.61), kind=kLoop, calls=%fused_computation.42 | loop fusion | flops 12288 | bytes 81924 | tf_op jit(solution)/shard_map/add | solution.py:57
  (23 shorter events, 0.5 us)
Async XLA Ops:
  0.6 1.6 %copy-start = (bf16[2048,512]{1,0:T(8,128)(2,1)S(1)}, bf16[2048,512]{1,0:T(8,128)(2,1)}, u32[]{:S(2)}) copy-start(bf16[2048,512]{1,0:T(8,128)(2,1)} %param.4) | copy-start | bytes 6291460
  2.2 5.3 %copy-start.3 = (s32[1,4,128]{2,1,0:T(4,128)S(1)}, s32[1,4,128]{2,1,0:T(4,128)}, u32[]{:S(2)}) copy-start(s32[1,4,128]{2,1,0:T(4,128)} %param.7) | copy-start | bytes 6148
  2.2 5.5 %copy-start.2 = (bf16[1024,128]{1,0:T(8,128)(2,1)S(1)}, bf16[1024,128]{1,0:T(8,128)(2,1)}, u32[]{:S(2)}) copy-start(bf16[1024,128]{1,0:T(8,128)(2,1)} %param.5) | copy-start | bytes 786436
  4.3 3.8 %collective-permute-start = (bf16[128,512]{1,0:T(8,128)(2,1)S(1)}, bf16[128,512]{1,0:T(8,128)(2,1)S(1)}, u32[]{:S(2)}, u32[]{:S(2)}) collective-permute-start(bf16[128,512]{1,0:T(8,128)(2,1)S(1)} %get-tuple-element.8), channel_id=1, source_target_pairs={{0,1},{1,0},{2,3},{3,2},{4,5},{5,4},{6,7},{7,6},{8,9},{9,8},{10,11... | collective-permute-start | bytes 393224 | tf_op jit(solution)/shard_map/ppermute | solution.py:23
  4.8 6.5 %collective-permute-start.2 = (bf16[128,512]{1,0:T(8,128)(2,1)S(1)}, bf16[128,512]{1,0:T(8,128)(2,1)S(1)}, u32[]{:S(2)}, u32[]{:S(2)}) collective-permute-start(bf16[128,512]{1,0:T(8,128)(2,1)S(1)} %get-tuple-element.7), channel_id=1, source_target_pairs={{0,3},{1,2},{2,1},{3,0},{4,7},{5,6},{6,5},{7,4},{8,11},{9,10},{10,... | collective-permute-start | bytes 393224 | tf_op jit(solution)/shard_map/ppermute | solution.py:23
  7.5 7.0 %collective-permute-start.1 = (bf16[128,512]{1,0:T(8,128)(2,1)S(1)}, bf16[128,512]{1,0:T(8,128)(2,1)}, u32[]{:S(2)}, u32[]{:S(2)}) collective-permute-start(bf16[128,512]{1,0:T(8,128)(2,1)S(1)} %get-tuple-element.6), channel_id=1, source_target_pairs={{0,2},{1,3},{2,0},{3,1},{4,6},{5,7},{6,4},{7,5},{8,10},{9,11},{10,... | collective-permute-start | bytes 393224 | tf_op jit(solution)/shard_map/ppermute | solution.py:23
  15.5 10.0 %collective-permute-start.3 = (bf16[256,512]{1,0:T(8,128)(2,1)S(1)}, bf16[256,512]{1,0:T(8,128)(2,1)S(1)}, u32[]{:S(2)}, u32[]{:S(2)}) collective-permute-start(bf16[256,512]{1,0:T(8,128)(2,1)S(1)} %fusion.4.refs_0_), channel_id=1, source_target_pairs={{4,0},{8,4},{12,8},{16,12},{20,16},{24,20},{28,24},{5,1},{9,5},{13... | collective-permute-start | bytes 786440 | tf_op jit(solution)/shard_map/ppermute | solution.py:18
  16.8 15.1 %collective-permute-start.4 = (bf16[256,512]{1,0:T(8,128)(2,1)S(1)}, bf16[256,512]{1,0:T(8,128)(2,1)S(1)}, u32[]{:S(2)}, u32[]{:S(2)}) collective-permute-start(bf16[256,512]{1,0:T(8,128)(2,1)S(1)} %fusion.4.refs_0_), channel_id=1, source_target_pairs={{8,0},{12,4},{16,8},{20,12},{24,16},{28,20},{9,1},{13,5},{17,9},{2... | collective-permute-start | bytes 786440 | tf_op jit(solution)/shard_map/ppermute | solution.py:18
  31.9 1.7 %copy-start.1 = (bf16[1152,1024]{1,0:T(8,128)(2,1)S(1)}, bf16[1152,1024]{1,0:T(8,128)(2,1)}, u32[]{:S(2)}) copy-start(bf16[1152,1024]{1,0:T(8,128)(2,1)} %copy_bitcast_fusion.refs_3_) | copy-start | bytes 7077892
  41.2 1.6 %collective-permute-start.5 = (f32[2,2,2,2,32,128]{5,4,3,2,1,0:T(8,128)S(1)}, f32[2,2,2,2,32,128]{5,4,3,2,1,0:T(8,128)S(1)}, u32[]{:S(2)}, u32[]{:S(2)}) collective-permute-start(f32[2,2,2,2,32,128]{5,4,3,2,1,0:T(8,128)S(1)} %dynamic-slice_bitcast_fusion), channel_id=1, source_target_pairs={{0,1},{1,0},{2,3},{3,2},{4,5},{5,4},{6,7},{7,6},{8,9},{9,8},{10,11... | collective-permute-start | bytes 786440 | tf_op jit(solution)/shard_map/ppermute | solution.py:23
  42.9 4.3 %collective-permute-start.6 = (f32[2,2,32,128]{3,2,1,0:T(8,128)S(1)}, f32[2,2,32,128]{3,2,1,0:T(8,128)S(1)}, u32[]{:S(2)}, u32[]{:S(2)}) collective-permute-start(f32[2,2,32,128]{3,2,1,0:T(8,128)S(1)} %get-tuple-element.9), channel_id=1, source_target_pairs={{0,2},{1,3},{2,0},{3,1},{4,6},{5,7},{6,4},{7,5},{8,10},{9,11},{10,... | collective-permute-start | bytes 196616 | tf_op jit(solution)/shard_map/ppermute | solution.py:23
  44.5 4.6 %collective-permute-start.7 = (f32[2,2,32,128]{3,2,1,0:T(8,128)S(1)}, f32[2,2,32,128]{3,2,1,0:T(8,128)S(1)}, u32[]{:S(2)}, u32[]{:S(2)}) collective-permute-start(f32[2,2,32,128]{3,2,1,0:T(8,128)S(1)} %get-tuple-element.11), channel_id=1, source_target_pairs={{0,4},{1,5},{2,6},{3,7},{4,0},{5,1},{6,2},{7,3},{8,12},{9,13},{10,... | collective-permute-start | bytes 196616 | tf_op jit(solution)/shard_map/ppermute | solution.py:23
  44.5 5.5 %collective-permute-start.8 = (f32[2,2,32,128]{3,2,1,0:T(8,128)S(1)}, f32[2,2,32,128]{3,2,1,0:T(8,128)S(1)}, u32[]{:S(2)}, u32[]{:S(2)}) collective-permute-start(f32[2,2,32,128]{3,2,1,0:T(8,128)S(1)} %get-tuple-element.10), channel_id=1, source_target_pairs={{0,6},{1,7},{2,4},{3,5},{4,2},{5,3},{6,0},{7,1},{8,14},{9,15},{10,... | collective-permute-start | bytes 196616 | tf_op jit(solution)/shard_map/ppermute | solution.py:23
  50.0 4.7 %collective-permute-start.10 = (f32[32,128]{1,0:T(8,128)S(1)}, f32[32,128]{1,0:T(8,128)S(1)}, u32[]{:S(2)}, u32[]{:S(2)}) collective-permute-start(f32[32,128]{1,0:T(8,128)S(1)} %get-tuple-element.14), channel_id=1, source_target_pairs={{0,16},{1,17},{2,18},{3,19},{4,20},{5,21},{6,22},{7,23},{8,24},{9,... | collective-permute-start | bytes 49160 | tf_op jit(solution)/shard_map/ppermute | solution.py:23
  52.6 5.5 %collective-permute-start.11 = (f32[32,128]{1,0:T(8,128)S(1)}, f32[32,128]{1,0:T(8,128)S(1)}, u32[]{:S(2)}, u32[]{:S(2)}) collective-permute-start(f32[32,128]{1,0:T(8,128)S(1)} %get-tuple-element.13), channel_id=1, source_target_pairs={{0,24},{1,25},{2,26},{3,27},{4,28},{5,29},{6,30},{7,31},{8,16},{9,... | collective-permute-start | bytes 49160 | tf_op jit(solution)/shard_map/ppermute | solution.py:23
  54.0 4.2 %collective-permute-start.9 = (f32[32,128]{1,0:T(8,128)S(1)}, f32[32,128]{1,0:T(8,128)S(1)}, u32[]{:S(2)}, u32[]{:S(2)}) collective-permute-start(f32[32,128]{1,0:T(8,128)S(1)} %get-tuple-element.12), channel_id=1, source_target_pairs={{0,8},{1,9},{2,10},{3,11},{4,12},{5,13},{6,14},{7,15},{8,0},{9,1},... | collective-permute-start | bytes 49160 | tf_op jit(solution)/shard_map/ppermute | solution.py:23

commit v2 on v0

v2 whole, which is shorter than its diff:
```python
import math

import jax
import jax.numpy as jnp
from jax import lax
from jax.experimental import pallas as pl
from jax.experimental.pallas import tpu as pltpu
from jax.sharding import PartitionSpec as P

INPUTS = 16
SENS_DEV = 256
LANES = 128
TAIL = 16
MIB = 1024 * 1024
F32 = jnp.float32
BF16 = jnp.bfloat16


def shifted(x, axis, by):
    count = lax.axis_size(axis)
    pairs = [(i, i + by) for i in range(count) if 0 <= i + by < count]
    return lax.ppermute(x, axis, pairs)


def crossed(x, axes, mask):
    count = math.prod(lax.axis_size(a) for a in axes)
    return lax.ppermute(x, axes, [(i, i ^ mask) for i in range(count)])


def pick_rows(state_tiles, probe_cell, probe_row):
    cells_here, width = state_tiles.shape
    tiles, capacity = probe_cell.shape
    rows = tiles * capacity
    half = rows // 2
    steps = 4
    chunk = cells_here // steps

    def kernel(cell_ref, row_ref, state_ref, *refs):
        parts = refs[:tiles]
        first, second, swap, slot, total = refs[tiles:]
        k = pl.program_id(0)
        me = lax.axis_index("sensor")

        @pl.when(k == 0)
        def _():
            for m in range(tiles):
                line = cell_ref[pl.ds(me ^ m, 1), :]
                slot[m * capacity : (m + 1) * capacity, :] = jnp.broadcast_to(line, (LANES, capacity)).T
            total[...] = jnp.zeros_like(total)

        lane = lax.broadcasted_iota(jnp.int32, (rows, LANES), 1) + k * chunk
        wanted = slot[...]
        chosen = jnp.concatenate(
            [jnp.where(wanted == lane + c, 1.0, 0.0).astype(BF16) for c in range(0, chunk, LANES)], axis=1
        )
        total[...] += jnp.dot(chosen, state_ref[...], preferred_element_type=F32)

        @pl.when(k == steps - 1)
        def _():
            odd = lax.rem(lax.axis_index("tm"), 2)
            got = total[...].astype(BF16)
            first[...] = got[:half]
            second[...] = got[half:]

            @pl.when(odd == 0)
            def _():
                swap[...] = got[:half]

            @pl.when(odd == 1)
            def _():
                swap[...] = got[half:]

            for m in range(tiles):
                parts[m][:capacity, :] = got[m * capacity : (m + 1) * capacity]
                filled = jnp.broadcast_to(row_ref[pl.ds(me ^ m, 1), :1], (TAIL, width)) >= 0
                parts[m][capacity:, :] = jnp.where(filled, 1.0, 0.0).astype(BF16)

    whole = lambda shape: pl.BlockSpec(shape, lambda k: (0,) * len(shape))
    shapes = [(capacity + TAIL, width)] * tiles + [(half, width)] * 3
    return pl.pallas_call(
        kernel,
        grid=(steps,),
        in_specs=[whole(probe_cell.shape), whole(probe_row.shape), pl.BlockSpec((chunk, width), lambda k: (k, 0))],
        out_specs=[whole(s) for s in shapes],
        out_shape=[jax.ShapeDtypeStruct(s, BF16) for s in shapes],
        scratch_shapes=[pltpu.VMEM((rows, LANES), jnp.int32), pltpu.VMEM((rows, width), F32)],
        compiler_params=pltpu.CompilerParams(vmem_limit_bytes=24 * MIB),
    )(probe_cell, probe_row, state_tiles)


def place_rows(probe_row, parts):
    tiles, capacity = probe_row.shape
    width = parts[0].shape[1]

    def kernel(row_ref, *refs):
        out_ref = refs[tiles]
        me = lax.axis_index("sensor")
        sensor = lax.broadcasted_iota(jnp.int32, (SENS_DEV, capacity), 0)
        total = jnp.zeros((SENS_DEV, width), F32)
        for m in range(tiles):
            chosen = jnp.where(row_ref[pl.ds(me ^ m, 1), :] == sensor, 1.0, 0.0).astype(BF16)
            total += jnp.dot(chosen, refs[m][:capacity, :], preferred_element_type=F32)
        out_ref[...] = total.astype(BF16)

    return pl.pallas_call(
        kernel,
        out_shape=jax.ShapeDtypeStruct((SENS_DEV, width), BF16),
        compiler_params=pltpu.CompilerParams(vmem_limit_bytes=16 * MIB),
    )(probe_row, *parts)


def widen(sketch):
    span, columns = sketch.shape
    group = LANES // INPUTS

    def kernel(sketch_ref, out_ref):
        out_ref[...] = jnp.zeros_like(out_ref)
        for o in range(group):
            out_ref[o * INPUTS : o * INPUTS + span, o * columns : (o + 1) * columns] = sketch_ref[...]

    return pl.pallas_call(
        kernel,
        out_shape=jax.ShapeDtypeStruct((span + LANES, group * columns), BF16),
        compiler_params=pltpu.CompilerParams(vmem_limit_bytes=16 * MIB),
    )(sketch)


def hankel_times(blocks, wide):
    rows, width = blocks[0].shape
    group = LANES // INPUTS
    columns = wide.shape[1] // group
    groups = width // LANES
    reach = wide.shape[0]
    n_blocks = len(blocks)

    def kernel(*refs):
        wide_ref, out_ref, ext = refs[n_blocks:]
        g = pl.program_id(0)

        @pl.when(g == 0)
        def _():
            for b in range(n_blocks):
                ext[:, b * width : (b + 1) * width] = refs[b][...]

        window = ext[:, pl.ds(pl.multiple_of(g * LANES, LANES), reach)]
        image = jnp.dot(window, wide_ref[...], preferred_element_type=F32)
        for o in range(group):
            out_ref[o] = image[:, o * columns : (o + 1) * columns]

    return pl.pallas_call(
        kernel,
        grid=(groups,),
        in_specs=[pl.BlockSpec((rows, width), lambda g: (0, 0))] * n_blocks
        + [pl.BlockSpec(wide.shape, lambda g: (0, 0))],
        out_specs=pl.BlockSpec((group, rows, columns), lambda g: (g, 0, 0)),
        out_shape=jax.ShapeDtypeStruct((groups * group, rows, columns), F32),
        scratch_shapes=[pltpu.VMEM((rows, n_blocks * width), BF16)],
        compiler_params=pltpu.CompilerParams(vmem_limit_bytes=20 * MIB),
    )(*blocks, wide)


def across(a, b):
    return lax.dot_general(a, b, (((0,), (0,)), ((), ())), preferred_element_type=F32)


def gram_image(place, first, second, back, ahead, swap, parts, sketch, scale):
    half, width = first.shape
    span, columns = sketch.shape
    tiles = len(parts)
    capacity = 2 * half // tiles
    group = LANES // INPUTS
    pair = 2 * LANES
    groups = span // LANES

    def kernel(place_ref, first_ref, second_ref, back_ref, ahead_ref, swap_ref, *refs):
        part_refs = refs[:tiles]
        sketch_ref, image_ref, own, left, right, lag, early, full, turned = refs[tiles:]
        spot = place_ref[0]
        odd = lax.rem(spot, 2)
        for m in range(tiles):
            at = slice(m * capacity, (m + 1) * capacity)
            source, base = (first_ref, 0) if m < tiles // 2 else (second_ref, half)
            keep = part_refs[m][capacity : capacity + TAIL, :][:1]
            own[at, :] = source[m * capacity - base : (m + 1) * capacity - base, :] * keep

        @pl.when(odd == 0)
        def _():
            for m in range(tiles // 2, tiles):
                at = slice(m * capacity - half, (m + 1) * capacity - half)
                keep = part_refs[m][capacity : capacity + TAIL, :][:1]
                mine = swap_ref[at, :] * keep
                right[at, :] = mine
                left[half + m * capacity - half : half + (m + 1) * capacity - half, :] = mine
            left[:half, :] = own[half:, :]
            right[half : 2 * half, :] = ahead_ref[...]

        @pl.when(odd == 1)
        def _():
            for m in range(tiles // 2):
                at = slice(m * capacity, (m + 1) * capacity)
                keep = part_refs[m][capacity : capacity + TAIL, :][:1]
                mine = swap_ref[at, :] * keep
                left[at, :] = mine
                right[half + m * capacity : half + (m + 1) * capacity, :] = mine
            right[:half, :] = own[:half, :]
            left[half : 2 * half, :] = back_ref[...]

        left[2 * half : 3 * half, :] = back_ref[...]
        left[3 * half :, :] = own[half:, :]
        right[2 * half : 3 * half, :] = own[:half, :]
        right[3 * half :, :] = ahead_ref[...]
        lag[...] = jnp.zeros_like(lag)

        @pl.when(spot < 2)
        def _():
            early[...] = jnp.zeros_like(early)

        for q in range(width // pair):
            at = slice(q * pair, (q + 1) * pair)
            low = q * pair
            same = across(own[:, at], own[:, low:])
            n = width - low
            lag[:, :n] += same[:LANES]
            lag[:, : n - LANES] += same[LANES:, LANES:]
            near = across(left[:half, at], right[:half, :])
            one = near + across(left[half : 2 * half, at], right[half : 2 * half, :])
            lag[:, n : n + width] += one[:LANES]
            lag[:, n - LANES : n - LANES + width] += one[LANES:]
            two = across(left[2 * half :, at], right[2 * half :, : low + pair])
            lag[:, n + width :] += two[:LANES, : low + LANES]
            lag[:, n + width - LANES :] += two[LANES:, :]

            @pl.when(spot == 0)
            def _():
                early[at, low:width] = same
                early[at, width : 2 * width] = near

            @pl.when(spot == 1)
            def _():
                early[width + low : width + low + pair, width + low : 2 * width] = same
                early[at, width : 2 * width] = near

        strip = lag[:INPUTS, :span]
        for o in range(1, group):
            strip += pltpu.roll(lag[o * INPUTS : (o + 1) * INPUTS, :], span + LANES - o * INPUTS, 1)[:, :span]
        lane = lax.broadcasted_iota(jnp.int32, strip.shape, 1)
        strip = jnp.where(lane < INPUTS, 0.5 * strip, strip)
        for o in range(group):
            moved = strip if o == 0 else jnp.where(lane < o * INPUTS, 0.0, pltpu.roll(strip, o * INPUTS, 1))
            lag[o * INPUTS : (o + 1) * INPUTS, :span] = moved
        for j in range(groups):
            full[j * LANES : (j + 1) * LANES, j * LANES :] = lag[:, : span - j * LANES]
            if j % 2:
                full[j * LANES : (j + 1) * LANES, (j - 1) * LANES : j * LANES] = jnp.zeros((LANES, LANES), F32)

        @pl.when(spot < 2)
        def _():
            r = lax.broadcasted_iota(jnp.int32, (LANES, LANES), 0) // INPUTS
            c = lax.broadcasted_iota(jnp.int32, (LANES, LANES), 1) // INPUTS
            weight = jnp.where(c > r, 1.0, jnp.where(c == r, 0.5, 0.0))
            for j in range(groups):
                at = slice(j * LANES, (j + 1) * LANES)
                early[at, at] = early[at, at] * weight
                full[at, at] += early[at, at]
                if j + 1 < groups:
                    rest = slice((j + 1) * LANES, span)
                    full[at, rest] += early[at, rest]
            by = 1
            while by < group:
                step = by * INPUTS
                for j in reversed(range(groups)):
                    at = slice(j * LANES, (j + 1) * LANES)
                    if j:
                        source = early[j * LANES - step : (j + 1) * LANES - step, (j - 1) * LANES :]
                        early[at, j * LANES :] += pltpu.roll(source, step, 1)[:, LANES:]
                    else:
                        source = early[: LANES - step, :]
                        early[step:LANES, :] += pltpu.roll(source, step, 1)
                by *= 2
            by = 1
            while by < groups:
                for j in reversed(range(by, groups)):
                    early[j * LANES : (j + 1) * LANES, j * LANES :] += early[
                        (j - by) * LANES : (j - by + 1) * LANES, (j - by) * LANES : span - by * LANES
                    ]
                by *= 2
            for j in range(groups):
                at = slice(j * LANES, (j + 1) * LANES)
                full[at, at] -= jnp.where(c >= r, early[at, at], 0.0)
                if j + 1 < groups:
                    rest = slice((j + 1) * LANES, span)
                    full[at, rest] -= early[at, rest]

        for q in range(span // pair):
            at = slice(q * pair, (q + 1) * pair)
            value = full[at, q * pair :]
            high = value.astype(BF16)
            low = (value - high.astype(F32)).astype(BF16)
            below = sketch_ref[q * pair :, :]
            image_ref[at, :] = jnp.dot(high, below, preferred_element_type=F32) + jnp.dot(
                low, below, preferred_element_type=F32
            )
            tall = sketch_ref[at, :]
            down = across(tall, high) + across(tall, low)
            if q == 0:
                turned[...] = down
            else:
                turned[:, q * pair :] += down
        image_ref[...] = (image_ref[...] + turned[...].T) * scale

    vmem = pl.BlockSpec(memory_space=pltpu.VMEM)
    smem = pl.BlockSpec(memory_space=pltpu.SMEM)
    return pl.pallas_call(
        kernel,
        in_specs=[smem] + [vmem] * (6 + tiles),
        out_specs=vmem,
        out_shape=jax.ShapeDtypeStruct((span, columns), F32),
        scratch_shapes=[
            pltpu.VMEM((2 * half, width), BF16),
            pltpu.VMEM((4 * half, width), BF16),
            pltpu.VMEM((4 * half, width), BF16),
            pltpu.VMEM((LANES, span + LANES), F32),
            pltpu.VMEM((span, span), F32),
            pltpu.VMEM((span, span), F32),
            pltpu.VMEM((columns, span), F32),
        ],
        compiler_params=pltpu.CompilerParams(vmem_limit_bytes=28 * MIB),
    )(place, first, second, back, ahead, swap, *parts, sketch)


def reduce_scatter(total, axes, rounds):
    count = math.prod(lax.axis_size(a) for a in axes)
    me = jnp.int32(0)
    for a in axes:
        me = me * lax.axis_size(a) + lax.axis_index(a)
    bits = int(math.log2(count))
    value = total.reshape((2,) * bits + (total.shape[0] // count, total.shape[1]))
    left = list(range(bits))
    for bunch in rounds:
        dims = [left.index(b) for b in bunch]
        value = jnp.moveaxis(value, dims, range(len(bunch)))
        rest = value.shape[len(bunch):]
        value = value.reshape((2 ** len(bunch),) + rest)
        mine = jnp.int32(0)
        for b in bunch:
            mine = mine * 2 + ((me >> (bits - 1 - b)) & 1)
        acc = lax.dynamic_index_in_dim(value, mine, 0, keepdims=False)
        for mask in range(1, 2 ** len(bunch)):
            flip = 0
            for place, b in enumerate(bunch):
                if (mask >> (len(bunch) - 1 - place)) & 1:
                    flip |= 1 << (bits - 1 - b)
            acc = acc + crossed(lax.dynamic_index_in_dim(value, mine ^ mask, 0, keepdims=False), axes, flip)
        value = acc
        for b in bunch:
            left.remove(b)
    return value


def local(state_tiles, sketch, probe_cell, probe_row):
    n_tiles = lax.axis_size("sensor")
    width = state_tiles.shape[1]
    steps_here = width // INPUTS
    probe_row = probe_row[0]
    *parts, first, second, swap = pick_rows(state_tiles, probe_cell[0], probe_row)
    arrived = [parts[0]] + [crossed(parts[m], ("sensor",), m) for m in range(1, n_tiles)]
    swapped = crossed(swap, ("tm",), 1)
    back = shifted(first, "tm", 2)
    ahead = shifted(second, "tm", -2)
    own_block = place_rows(probe_row, arrived)
    blocks = [own_block, shifted(own_block, "tm", -1), shifted(own_block, "tm", -2)]
    scale = 1.0 / math.sqrt(SENS_DEV * n_tiles * steps_here * lax.axis_size("tm"))
    place = lax.axis_index("tm").astype(jnp.int32).reshape(1)
    total = gram_image(place, first, second, back, ahead, swapped, arrived, sketch, scale)
    hankel_sketch = hankel_times(blocks, widen(sketch))
    tm_bits = int(math.log2(lax.axis_size("tm")))
    sensor_bits = int(math.log2(n_tiles))
    last = tm_bits + sensor_bits - 1
    rounds = [[last], list(range(tm_bits - 1, last)), list(range(tm_bits - 1))]
    column_image = reduce_scatter(total, ("tm", "sensor"), rounds)
    return (hankel_sketch, column_image)


def solution(mesh):
    placed = (P("sensor", "tm"), P(), P("sensor", None, None), P("sensor", None, None))
    return jax.shard_map(
        local,
        mesh=mesh,
        in_specs=placed,
        out_specs=(P("tm", "sensor", None), P(("tm", "sensor"), None)),
        check_vma=False,
    )
```

time: 201 us -> 55.6 us (0.28)
  the two profiles are of different devices: /device:TPU:0 before, /device:TPU:2 now
where the time goes in v2:
time: 55.6 us; the launch traced here: 55.2 us
  starting transfers between devices  19.7 us (35%)
  waiting for transfers between devices  15.9 us (29%)
  Pallas kernels  13.5 us (24%)
  local copies, waits for them, and re-layouts  3.97 us (7%)
  other arithmetic  1.4 us (3%)
  between operations  0.8 us (1%)
    ppermute x4, starting transfers between devices, shifted(): return lax.ppermute(x, axis, pairs)  9.93 us
    ppermute x11, starting transfers between devices, crossed(): return lax.ppermute(x, axes, [(i, i ^ mask) for i in range(count)])  9.73 us
    ppermute x4, waiting for transfers between devices, shifted(): return lax.ppermute(x, axis, pairs)  8.12 us
    ppermute x11, waiting for transfers between devices, crossed(): return lax.ppermute(x, axes, [(i, i ^ mask) for i in range(count)])  7.74 us
    pallas_call x1, Pallas kernels, gram_image(): pl.pallas_call(kernel, in_specs=[smem] + [vmem] * (6 + tiles), out_specs=...  6.01 us
    pallas_call x1, Pallas kernels, hankel_times(): pl.pallas_call(kernel, grid=(groups,), in_specs=[pl.BlockSpec((rows, widt...  4.58 us
    unnamed x12, local copies, waits for them, and re-layouts  3.91 us
    pallas_call x1, Pallas kernels, pick_rows(): pl.pallas_call(kernel, grid=(steps,), in_specs=[whole(probe_cell.shape),...  2.1 us
  transfers between devices with their start and end apart: 15, of which 6 were waited for; matrix products, arithmetic and copies ran while one was open for 0% of the time, Pallas kernels for 10%

profile of v2, /device:TPU:2, one launch (start us, length us, event | category | flops | bytes accessed | tf_op | source)
XLA Modules:
  0.0 55.2 jit_solution(13888164439497022347)
XLA Ops:
  0.6 1.6 %copy-done = bf16[2048,512]{1,0:T(8,128)(2,1)S(1)} copy-done((bf16[2048,512]{1,0:T(8,128)(2,1)S(1)}, bf16[2048,512]{1,0:T(8,128)(2,1)}, u32[]{:S(2)}) %copy-start) | copy-done | bytes 2097176
  2.2 0.7 %copy-done.3 = s32[1,4,128]{2,1,0:T(4,128)S(1)} copy-done((s32[1,4,128]{2,1,0:T(4,128)S(1)}, s32[1,4,128]{2,1,0:T(4,128)}, u32[]{:S(2)}) %copy-start.3) | copy-done | bytes 2072
  2.9 0.7 %copy-done.5 = s32[1,4,128]{2,1,0:T(4,128)S(1)} copy-done((s32[1,4,128]{2,1,0:T(4,128)S(1)}, s32[1,4,128]{2,1,0:T(4,128)}, u32[]{:S(2)}) %copy-start.5) | copy-done | bytes 2072
  3.6 2.1 %shard_map.59 = (bf16[144,512]{1,0:T(8,128)(2,1)S(1)}, bf16[144,512]{1,0:T(8,128)(2,1)S(1)}, bf16[144,512]{1,0:T(8,128)(2,1)S(1)}, bf16[144,512]{1,0:T(8,128)(2,...) custom-call(s32[4,128]{1,0:T(4,128)S(1)} %bitcast.40, ...), custom_call_target="tpu_custom_call" | custom-call | tf_op jit(solution)/shard_map/pallas_call | solution.py:80
  5.7 0.0 copy-start.4
  5.7 0.1 collective-permute-start
  5.8 0.1 collective-permute-start.7
  5.9 4.0 %collective-permute-start.5 = (bf16[256,512]{1,0:T(8,128)(2,1)S(1)}, bf16[256,512]{1,0:T(8,128)(2,1)S(1)}, u32[]{:S(2)}, u32[]{:S(2)}) collective-permute-start(bf16[256,512]{1,0:T(8,128)(2,1)S(1)} %get-tuple-element.13.first_ref), channel_id=1, source_target_pairs={{0,8},{4,12},{8,16},{12,20},{16,24},{20,28},{1,9},{5,13},{9,17},{1... | collective-permute-start | bytes 786440 | tf_op jit(solution)/shard_map/ppermute | solution.py:22
  9.9 1.3 %collective-permute-start.6 = (bf16[256,512]{1,0:T(8,128)(2,1)S(1)}, bf16[256,512]{1,0:T(8,128)(2,1)S(1)}, u32[]{:S(2)}, u32[]{:S(2)}) collective-permute-start(bf16[256,512]{1,0:T(8,128)(2,1)S(1)} %get-tuple-element.14.second_ref), channel_id=1, source_target_pairs={{8,0},{12,4},{16,8},{20,12},{24,16},{28,20},{9,1},{13,5},{17,9},{2... | collective-permute-start | bytes 786440 | tf_op jit(solution)/shard_map/ppermute | solution.py:22
  11.2 1.6 %collective-permute-start.1 = (bf16[144,512]{1,0:T(8,128)(2,1)S(1)}, bf16[144,512]{1,0:T(8,128)(2,1)S(1)}, u32[]{:S(2)}, u32[]{:S(2)}) collective-permute-start(bf16[144,512]{1,0:T(8,128)(2,1)S(1)} %get-tuple-element.11), channel_id=1, source_target_pairs={{0,2},{1,3},{2,0},{3,1},{4,6},{5,7},{6,4},{7,5},{8,10},{9,11},{10,... | collective-permute-start | bytes 442376 | tf_op jit(solution)/shard_map/ppermute | solution.py:27
  12.8 5.2 %collective-permute-done.1.refs_2_ = bf16[144,512]{1,0:T(8,128)(2,1)S(1)} collective-permute-done((bf16[144,512]{1,0:T(8,128)(2,1)S(1)}, bf16[144,512]{1,0:T(8,128)(2,1)S(1)}, u32[]{:S(2)}, u32[]{:S(2)}) %collective-permute-start.1) | collective-permute-done | bytes 147488 | tf_op jit(solution)/shard_map/ppermute | solution.py:27
  18.0 1.1 %collective-permute-done.2.refs_3_ = bf16[144,512]{1,0:T(8,128)(2,1)S(1)} collective-permute-done((bf16[144,512]{1,0:T(8,128)(2,1)S(1)}, bf16[144,512]{1,0:T(8,128)(2,1)S(1)}, u32[]{:S(2)}, u32[]{:S(2)}) %collective-permute-start.2) | collective-permute-done | bytes 147488 | tf_op jit(solution)/shard_map/ppermute | solution.py:27
  19.1 0.8 %collective-permute-done.6.ahead_ref = bf16[256,512]{1,0:T(8,128)(2,1)S(1)} collective-permute-done((bf16[256,512]{1,0:T(8,128)(2,1)S(1)}, bf16[256,512]{1,0:T(8,128)(2,1)S(1)}, u32[]{:S(2)}, u32[]{:S(2)}) %collective-permute-start.6) | collective-permute-done | bytes 262176 | tf_op jit(solution)/shard_map/ppermute | solution.py:22
  19.9 0.9 %copy-done.1 = bf16[1024,128]{1,0:T(8,128)(2,1)S(1)} copy-done((bf16[1024,128]{1,0:T(8,128)(2,1)S(1)}, bf16[1024,128]{1,0:T(8,128)(2,1)}, u32[]{:S(2)}) %copy-start.1) | copy-done | bytes 262168
  20.8 6.0 %shard_map.63 = f32[1024,128]{1,0:T(8,128)S(1)} custom-call(s32[1]{0:T(128)} %bitcast.2.place_ref, bf16[256,512]{1,0:T(8,128)(2,1)S(1)} %get-tuple-element.13.first_ref, bf16[256,512]{1,0:T(8,128)(2,1)S(1)} %get-tuple-element.14.second_ref, bf16[256,512]{1,0:T(8,128)(2,1)S(1)} %collective-permute-done.5.back_ref, ...), custom_call_target="tpu_custom_call" | custom-call | tf_op jit(solution)/shard_map/pallas_call | solution.py:313
  26.9 0.2 collective-permute-start.8
  27.1 1.4 %collective-permute-done.8 = f32[2,2,2,2,32,128]{5,4,3,2,1,0:T(8,128)S(1)} collective-permute-done((f32[2,2,2,2,32,128]{5,4,3,2,1,0:T(8,128)S(1)}, f32[2,2,2,2,32,128]{5,4,3,2,1,0:T(8,128)S(1)}, u32[]{:S(2)}, u32[]{:S(2)}) %collective-permute-start.8) | collective-permute-done | bytes 262176 | tf_op jit(solution)/shard_map/ppermute | solution.py:27
  28.5 1.6 %collective-permute-start.9 = (f32[2,2,32,128]{3,2,1,0:T(8,128)S(1)}, f32[2,2,32,128]{3,2,1,0:T(8,128)S(1)}, u32[]{:S(2)}, u32[]{:S(2)}) collective-permute-start(f32[2,2,32,128]{3,2,1,0:T(8,128)S(1)} %get-tuple-element.16), channel_id=1, source_target_pairs={{0,2},{1,3},{2,0},{3,1},{4,6},{5,7},{6,4},{7,5},{8,10},{9,11},{10,... | collective-permute-start | bytes 196616 | tf_op jit(solution)/shard_map/ppermute | solution.py:27
  30.1 1.4 %collective-permute-start.11 = (f32[2,2,32,128]{3,2,1,0:T(8,128)S(1)}, f32[2,2,32,128]{3,2,1,0:T(8,128)S(1)}, u32[]{:S(2)}, u32[]{:S(2)}) collective-permute-start(f32[2,2,32,128]{3,2,1,0:T(8,128)S(1)} %get-tuple-element.17), channel_id=1, source_target_pairs={{0,6},{1,7},{2,4},{3,5},{4,2},{5,3},{6,0},{7,1},{8,14},{9,15},{10,... | collective-permute-start | bytes 196616 | tf_op jit(solution)/shard_map/ppermute | solution.py:27
  31.5 0.6 %collective-permute-start.10 = (f32[2,2,32,128]{3,2,1,0:T(8,128)S(1)}, f32[2,2,32,128]{3,2,1,0:T(8,128)S(1)}, u32[]{:S(2)}, u32[]{:S(2)}) collective-permute-start(f32[2,2,32,128]{3,2,1,0:T(8,128)S(1)} %get-tuple-element.18), channel_id=1, source_target_pairs={{0,4},{1,5},{2,6},{3,7},{4,0},{5,1},{6,2},{7,3},{8,12},{9,13},{10,... | collective-permute-start | bytes 196616 | tf_op jit(solution)/shard_map/ppermute | solution.py:27
  32.1 0.4 shard_map.60.refs_0_
  32.5 1.3 %collective-permute-start.4 = (bf16[256,512]{1,0:T(8,128)(2,1)S(1)}, bf16[256,512]{1,0:T(8,128)(2,1)S(1)}, u32[]{:S(2)}, u32[]{:S(2)}) collective-permute-start(bf16[256,512]{1,0:T(8,128)(2,1)S(1)} %shard_map.60.refs_0_), channel_id=1, source_target_pairs={{8,0},{12,4},{16,8},{20,12},{24,16},{28,20},{9,1},{13,5},{17,9},{2... | collective-permute-start | bytes 786440 | tf_op jit(solution)/shard_map/ppermute | solution.py:22
  33.8 3.3 %collective-permute-start.3 = (bf16[256,512]{1,0:T(8,128)(2,1)S(1)}, bf16[256,512]{1,0:T(8,128)(2,1)S(1)}, u32[]{:S(2)}, u32[]{:S(2)}) collective-permute-start(bf16[256,512]{1,0:T(8,128)(2,1)S(1)} %shard_map.60.refs_0_), channel_id=1, source_target_pairs={{4,0},{8,4},{12,8},{16,12},{20,16},{24,20},{28,24},{5,1},{9,5},{13... | collective-permute-start | bytes 786440 | tf_op jit(solution)/shard_map/ppermute | solution.py:22
  37.2 0.0 collective-permute-done.11
  37.2 2.7 %collective-permute-start.12 = (f32[32,128]{1,0:T(8,128)S(1)}, f32[32,128]{1,0:T(8,128)S(1)}, u32[]{:S(2)}, u32[]{:S(2)}) collective-permute-start(f32[32,128]{1,0:T(8,128)S(1)} %get-tuple-element.19), channel_id=1, source_target_pairs={{0,8},{1,9},{2,10},{3,11},{4,12},{5,13},{6,14},{7,15},{8,0},{9,1},... | collective-permute-start | bytes 49160 | tf_op jit(solution)/shard_map/ppermute | solution.py:27
  40.0 0.0 collective-permute-start.14
  40.0 1.5 %collective-permute-start.13 = (f32[32,128]{1,0:T(8,128)S(1)}, f32[32,128]{1,0:T(8,128)}, u32[]{:S(2)}, u32[]{:S(2)}) collective-permute-start(f32[32,128]{1,0:T(8,128)S(1)} %get-tuple-element.21), channel_id=1, source_target_pairs={{0,16},{1,17},{2,18},{3,19},{4,20},{5,21},{6,22},{7,23},{8,24},{9,... | collective-permute-start | bytes 49160 | tf_op jit(solution)/shard_map/ppermute | solution.py:27
  41.5 0.4 shard_map.61.refs_3_
  41.9 0.3 collective-permute-done.4.refs_2_
  42.3 7.0 %collective-permute-done.3.refs_1_ = bf16[256,512]{1,0:T(8,128)(2,1)S(1)} collective-permute-done((bf16[256,512]{1,0:T(8,128)(2,1)S(1)}, bf16[256,512]{1,0:T(8,128)(2,1)S(1)}, u32[]{:S(2)}, u32[]{:S(2)}) %collective-permute-start.3) | collective-permute-done | bytes 262176 | tf_op jit(solution)/shard_map/ppermute | solution.py:22
  49.3 4.6 %shard_map.62 = f32[32,256,128]{2,1,0:T(8,128)} custom-call(bf16[256,512]{1,0:T(8,128)(2,1)S(1)} %shard_map.60.refs_0_, bf16[256,512]{1,0:T(8,128)(2,1)S(1)} %collective-permute-done.3.refs_1_, bf16[256,512]{1,0:T(8,128)(2,1)S(1)} %collective-permute-done.4.refs_2_, bf16[1152,1024]{1,0:T(8,128)(2,1)S(1)} %shard_map.61.refs_3_), custom_call_target="tpu_custom_call" | custom-call | tf_op jit(solution)/shard_map/pallas_call | solution.py:150
  53.9 1.3 %fusion.3 = f32[32,128]{1,0:T(8,128)} fusion(f32[32,128]{1,0:T(8,128)S(1)} %collective-permute-done.14, f32[32,128]{1,0:T(8,128)} %collective-permute-done.13, f32[32,128]{1,0:T(8,128)S(1)} %collective-permute-done.12, f32[4,32,128]{2,1,0:T(8,128)S(1)} %bitcast.44, s32[]{:T(128)S(6)} %select_n.39), kind=kLoop, calls=%fused_computation.10 | loop fusion | flops 12288 | bytes 81924 | tf_op jit(solution)/shard_map/add | solution.py:353
  (21 shorter events, 0.2 us)
Async XLA Ops:
  0.6 1.6 %copy-start = (bf16[2048,512]{1,0:T(8,128)(2,1)S(1)}, bf16[2048,512]{1,0:T(8,128)(2,1)}, u32[]{:S(2)}) copy-start(bf16[2048,512]{1,0:T(8,128)(2,1)} %state_ref.1) | copy-start | bytes 6291460
  2.2 0.7 %copy-start.3 = (s32[1,4,128]{2,1,0:T(4,128)S(1)}, s32[1,4,128]{2,1,0:T(4,128)}, u32[]{:S(2)}) copy-start(s32[1,4,128]{2,1,0:T(4,128)} %param.7) | copy-start | bytes 6148
  2.9 0.7 %copy-start.5 = (s32[1,4,128]{2,1,0:T(4,128)S(1)}, s32[1,4,128]{2,1,0:T(4,128)}, u32[]{:S(2)}) copy-start(s32[1,4,128]{2,1,0:T(4,128)} %param.6) | copy-start | bytes 6148
  5.7 26.4 %copy-start.4 = (s32[1,4,128]{2,1,0:T(4,128)S(1)}, s32[1,4,128]{2,1,0:T(4,128)}, u32[]{:S(2)}) copy-start(s32[1,4,128]{2,1,0:T(4,128)} %param.7) | copy-start | bytes 6148
  5.7 7.1 %collective-permute-start = (bf16[144,512]{1,0:T(8,128)(2,1)S(1)}, bf16[144,512]{1,0:T(8,128)(2,1)S(1)}, u32[]{:S(2)}, u32[]{:S(2)}) collective-permute-start(bf16[144,512]{1,0:T(8,128)(2,1)S(1)} %get-tuple-element.10), channel_id=1, source_target_pairs={{0,1},{1,0},{2,3},{3,2},{4,5},{5,4},{6,7},{7,6},{8,9},{9,8},{10,11... | collective-permute-start | bytes 442376 | tf_op jit(solution)/shard_map/ppermute | solution.py:27
  5.8 13.3 %collective-permute-start.7 = (bf16[256,512]{1,0:T(8,128)(2,1)S(1)}, bf16[256,512]{1,0:T(8,128)(2,1)S(1)}, u32[]{:S(2)}, u32[]{:S(2)}) collective-permute-start(bf16[256,512]{1,0:T(8,128)(2,1)S(1)} %get-tuple-element.15), channel_id=1, source_target_pairs={{0,4},{4,0},{8,12},{12,8},{16,20},{20,16},{24,28},{28,24},{1,5},{5... | collective-permute-start | bytes 786440 | tf_op jit(solution)/shard_map/ppermute | solution.py:27
  5.9 13.2 %collective-permute-start.5 = (bf16[256,512]{1,0:T(8,128)(2,1)S(1)}, bf16[256,512]{1,0:T(8,128)(2,1)S(1)}, u32[]{:S(2)}, u32[]{:S(2)}) collective-permute-start(bf16[256,512]{1,0:T(8,128)(2,1)S(1)} %get-tuple-element.13.first_ref), channel_id=1, source_target_pairs={{0,8},{4,12},{8,16},{12,20},{16,24},{20,28},{1,9},{5,13},{9,17},{1... | collective-permute-start | bytes 786440 | tf_op jit(solution)/shard_map/ppermute | solution.py:22
  9.9 10.0 %collective-permute-start.6 = (bf16[256,512]{1,0:T(8,128)(2,1)S(1)}, bf16[256,512]{1,0:T(8,128)(2,1)S(1)}, u32[]{:S(2)}, u32[]{:S(2)}) collective-permute-start(bf16[256,512]{1,0:T(8,128)(2,1)S(1)} %get-tuple-element.14.second_ref), channel_id=1, source_target_pairs={{8,0},{12,4},{16,8},{20,12},{24,16},{28,20},{9,1},{13,5},{17,9},{2... | collective-permute-start | bytes 786440 | tf_op jit(solution)/shard_map/ppermute | solution.py:22
  11.2 6.8 %collective-permute-start.1 = (bf16[144,512]{1,0:T(8,128)(2,1)S(1)}, bf16[144,512]{1,0:T(8,128)(2,1)S(1)}, u32[]{:S(2)}, u32[]{:S(2)}) collective-permute-start(bf16[144,512]{1,0:T(8,128)(2,1)S(1)} %get-tuple-element.11), channel_id=1, source_target_pairs={{0,2},{1,3},{2,0},{3,1},{4,6},{5,7},{6,4},{7,5},{8,10},{9,11},{10,... | collective-permute-start | bytes 442376 | tf_op jit(solution)/shard_map/ppermute | solution.py:27
  12.8 6.3 %collective-permute-start.2 = (bf16[144,512]{1,0:T(8,128)(2,1)S(1)}, bf16[144,512]{1,0:T(8,128)(2,1)S(1)}, u32[]{:S(2)}, u32[]{:S(2)}) collective-permute-start(bf16[144,512]{1,0:T(8,128)(2,1)S(1)} %get-tuple-element.12), channel_id=1, source_target_pairs={{0,3},{1,2},{2,1},{3,0},{4,7},{5,6},{6,5},{7,4},{8,11},{9,10},{10,... | collective-permute-start | bytes 442376 | tf_op jit(solution)/shard_map/ppermute | solution.py:27
  19.9 1.0 %copy-start.1 = (bf16[1024,128]{1,0:T(8,128)(2,1)S(1)}, bf16[1024,128]{1,0:T(8,128)(2,1)}, u32[]{:S(2)}) copy-start(bf16[1024,128]{1,0:T(8,128)(2,1)} %refs_4_.1) | copy-start | bytes 786436
  20.8 20.7 %copy-start.2 = (bf16[1024,128]{1,0:T(8,128)(2,1)S(1)}, bf16[1024,128]{1,0:T(8,128)(2,1)}, u32[]{:S(2)}) copy-start(bf16[1024,128]{1,0:T(8,128)(2,1)} %refs_4_.1) | copy-start | bytes 786436
  26.9 1.6 %collective-permute-start.8 = (f32[2,2,2,2,32,128]{5,4,3,2,1,0:T(8,128)S(1)}, f32[2,2,2,2,32,128]{5,4,3,2,1,0:T(8,128)S(1)}, u32[]{:S(2)}, u32[]{:S(2)}) collective-permute-start(f32[2,2,2,2,32,128]{5,4,3,2,1,0:T(8,128)S(1)} %dynamic-slice_bitcast_fusion), channel_id=1, source_target_pairs={{0,1},{1,0},{2,3},{3,2},{4,5},{5,4},{6,7},{7,6},{8,9},{9,8},{10,11... | collective-permute-start | bytes 786440 | tf_op jit(solution)/shard_map/ppermute | solution.py:27
  28.5 8.6 %collective-permute-start.9 = (f32[2,2,32,128]{3,2,1,0:T(8,128)S(1)}, f32[2,2,32,128]{3,2,1,0:T(8,128)S(1)}, u32[]{:S(2)}, u32[]{:S(2)}) collective-permute-start(f32[2,2,32,128]{3,2,1,0:T(8,128)S(1)} %get-tuple-element.16), channel_id=1, source_target_pairs={{0,2},{1,3},{2,0},{3,1},{4,6},{5,7},{6,4},{7,5},{8,10},{9,11},{10,... | collective-permute-start | bytes 196616 | tf_op jit(solution)/shard_map/ppermute | solution.py:27
  30.1 7.1 %collective-permute-start.11 = (f32[2,2,32,128]{3,2,1,0:T(8,128)S(1)}, f32[2,2,32,128]{3,2,1,0:T(8,128)S(1)}, u32[]{:S(2)}, u32[]{:S(2)}) collective-permute-start(f32[2,2,32,128]{3,2,1,0:T(8,128)S(1)} %get-tuple-element.17), channel_id=1, source_target_pairs={{0,6},{1,7},{2,4},{3,5},{4,2},{5,3},{6,0},{7,1},{8,14},{9,15},{10,... | collective-permute-start | bytes 196616 | tf_op jit(solution)/shard_map/ppermute | solution.py:27
  31.5 5.7 %collective-permute-start.10 = (f32[2,2,32,128]{3,2,1,0:T(8,128)S(1)}, f32[2,2,32,128]{3,2,1,0:T(8,128)S(1)}, u32[]{:S(2)}, u32[]{:S(2)}) collective-permute-start(f32[2,2,32,128]{3,2,1,0:T(8,128)S(1)} %get-tuple-element.18), channel_id=1, source_target_pairs={{0,4},{1,5},{2,6},{3,7},{4,0},{5,1},{6,2},{7,3},{8,12},{9,13},{10,... | collective-permute-start | bytes 196616 | tf_op jit(solution)/shard_map/ppermute | solution.py:27
  32.5 9.7 %collective-permute-start.4 = (bf16[256,512]{1,0:T(8,128)(2,1)S(1)}, bf16[256,512]{1,0:T(8,128)(2,1)S(1)}, u32[]{:S(2)}, u32[]{:S(2)}) collective-permute-start(bf16[256,512]{1,0:T(8,128)(2,1)S(1)} %shard_map.60.refs_0_), channel_id=1, source_target_pairs={{8,0},{12,4},{16,8},{20,12},{24,16},{28,20},{9,1},{13,5},{17,9},{2... | collective-permute-start | bytes 786440 | tf_op jit(solution)/shard_map/ppermute | solution.py:22
  33.8 15.5 %collective-permute-start.3 = (bf16[256,512]{1,0:T(8,128)(2,1)S(1)}, bf16[256,512]{1,0:T(8,128)(2,1)S(1)}, u32[]{:S(2)}, u32[]{:S(2)}) collective-permute-start(bf16[256,512]{1,0:T(8,128)(2,1)S(1)} %shard_map.60.refs_0_), channel_id=1, source_target_pairs={{4,0},{8,4},{12,8},{16,12},{20,16},{24,20},{28,24},{5,1},{9,5},{13... | collective-permute-start | bytes 786440 | tf_op jit(solution)/shard_map/ppermute | solution.py:22
  37.2 16.6 %collective-permute-start.12 = (f32[32,128]{1,0:T(8,128)S(1)}, f32[32,128]{1,0:T(8,128)S(1)}, u32[]{:S(2)}, u32[]{:S(2)}) collective-permute-start(f32[32,128]{1,0:T(8,128)S(1)} %get-tuple-element.19), channel_id=1, source_target_pairs={{0,8},{1,9},{2,10},{3,11},{4,12},{5,13},{6,14},{7,15},{8,0},{9,1},... | collective-permute-start | bytes 49160 | tf_op jit(solution)/shard_map/ppermute | solution.py:27
  40.0 13.9 %collective-permute-start.14 = (f32[32,128]{1,0:T(8,128)S(1)}, f32[32,128]{1,0:T(8,128)S(1)}, u32[]{:S(2)}, u32[]{:S(2)}) collective-permute-start(f32[32,128]{1,0:T(8,128)S(1)} %get-tuple-element.20), channel_id=1, source_target_pairs={{0,24},{1,25},{2,26},{3,27},{4,28},{5,29},{6,30},{7,31},{8,16},{9,... | collective-permute-start | bytes 49160 | tf_op jit(solution)/shard_map/ppermute | solution.py:27
  40.0 13.9 %collective-permute-start.13 = (f32[32,128]{1,0:T(8,128)S(1)}, f32[32,128]{1,0:T(8,128)}, u32[]{:S(2)}, u32[]{:S(2)}) collective-permute-start(f32[32,128]{1,0:T(8,128)S(1)} %get-tuple-element.21), channel_id=1, source_target_pairs={{0,16},{1,17},{2,18},{3,19},{4,20},{5,21},{6,22},{7,23},{8,24},{9,... | collective-permute-start | bytes 49160 | tf_op jit(solution)/shard_map/ppermute | solution.py:27

commit v3 on v2

--- a/solution.py
+++ b/solution.py
@@ -16,12 +16,22 @@
 BF16 = jnp.bfloat16
 
 
+def costs(flops, bytes_accessed=0):
+    return pl.CostEstimate(flops=int(flops), bytes_accessed=int(bytes_accessed), transcendentals=0)
+
+
 def shifted(x, axis, by):
     count = lax.axis_size(axis)
     pairs = [(i, i + by) for i in range(count) if 0 <= i + by < count]
     return lax.ppermute(x, axis, pairs)
 
 
+def paired(x, axis, by, odd):
+    count = lax.axis_size(axis)
+    low = [i for i in range(count - by) if (i // by) % 2 == odd]
+    return lax.ppermute(x, axis, [(i, i + by) for i in low] + [(i + by, i) for i in low])
+
+
 def crossed(x, axes, mask):
     count = math.prod(lax.axis_size(a) for a in axes)
     return lax.ppermute(x, axes, [(i, i ^ mask) for i in range(count)])
@@ -31,13 +41,12 @@
     cells_here, width = state_tiles.shape
     tiles, capacity = probe_cell.shape
     rows = tiles * capacity
-    half = rows // 2
     steps = 4
     chunk = cells_here // steps
 
     def kernel(cell_ref, row_ref, state_ref, *refs):
         parts = refs[:tiles]
-        first, second, swap, slot, total = refs[tiles:]
+        slot, total = refs[tiles:]
         k = pl.program_id(0)
         me = lax.axis_index("sensor")
 
@@ -57,26 +66,14 @@
 
         @pl.when(k == steps - 1)
         def _():
-            odd = lax.rem(lax.axis_index("tm"), 2)
             got = total[...].astype(BF16)
-            first[...] = got[:half]
-            second[...] = got[half:]
-
-            @pl.when(odd == 0)
-            def _():
-                swap[...] = got[:half]
-
-            @pl.when(odd == 1)
-            def _():
-                swap[...] = got[half:]
-
             for m in range(tiles):
                 parts[m][:capacity, :] = got[m * capacity : (m + 1) * capacity]
                 filled = jnp.broadcast_to(row_ref[pl.ds(me ^ m, 1), :1], (TAIL, width)) >= 0
                 parts[m][capacity:, :] = jnp.where(filled, 1.0, 0.0).astype(BF16)
 
     whole = lambda shape: pl.BlockSpec(shape, lambda k: (0,) * len(shape))
-    shapes = [(capacity + TAIL, width)] * tiles + [(half, width)] * 3
+    shapes = [(capacity + TAIL, width)] * tiles
     return pl.pallas_call(
         kernel,
         grid=(steps,),
@@ -84,7 +81,8 @@
         out_specs=[whole(s) for s in shapes],
         out_shape=[jax.ShapeDtypeStruct(s, BF16) for s in shapes],
         scratch_shapes=[pltpu.VMEM((rows, LANES), jnp.int32), pltpu.VMEM((rows, width), F32)],
-        compiler_params=pltpu.CompilerParams(vmem_limit_bytes=24 * MIB),
+        compiler_params=pltpu.CompilerParams(vmem_limit_bytes=10 * MIB),
+        cost_estimate=costs(2 * rows * cells_here * width, 2 * cells_here * width),
     )(probe_cell, probe_row, state_tiles)
 
 
@@ -105,45 +103,81 @@
     return pl.pallas_call(
         kernel,
         out_shape=jax.ShapeDtypeStruct((SENS_DEV, width), BF16),
-        compiler_params=pltpu.CompilerParams(vmem_limit_bytes=16 * MIB),
+        compiler_params=pltpu.CompilerParams(vmem_limit_bytes=8 * MIB),
+        cost_estimate=costs(2e10),
     )(probe_row, *parts)
 
 
-def widen(sketch):
+def prepare(parts):
+    tiles = len(parts)
+    capacity, width = parts[0].shape
+    capacity -= TAIL
+    half = tiles * capacity // 2
+
+    def kernel(*refs):
+        first, second, swap, even_pair, odd_pair = refs[tiles:]
+        spot = lax.axis_index("tm")
+        odd = lax.rem(spot, 2)
+        upper = lax.rem(spot // 2, 2)
+        for m in range(tiles):
+            base = 0 if m < tiles // 2 else half
+            at = slice(m * capacity - base, (m + 1) * capacity - base)
+            side = first if m < tiles // 2 else second
+            side[at, :] = refs[m][:capacity, :]
+
+        @pl.when(odd == 0)
+        def _():
+            swap[...] = first[...]
+
+        @pl.when(odd == 1)
+        def _():
+            swap[...] = second[...]
+
+        @pl.when(upper == 0)
+        def _():
+            even_pair[...] = first[...]
+            odd_pair[...] = second[...]
+
+        @pl.when(upper == 1)
+        def _():
+            even_pair[...] = second[...]
+            odd_pair[...] = first[...]
+
+    shapes = [(half, width)] * 5
+    return pl.pallas_call(
+        kernel,
+        out_shape=[jax.ShapeDtypeStruct(s, BF16) for s in shapes],
+        compiler_params=pltpu.CompilerParams(vmem_limit_bytes=8 * MIB),
+        cost_estimate=costs(5e8),
+    )(*parts)
+
+
+def hankel_times(blocks, sketch):
+    rows, width = blocks[0].shape
     span, columns = sketch.shape
     group = LANES // INPUTS
-
-    def kernel(sketch_ref, out_ref):
-        out_ref[...] = jnp.zeros_like(out_ref)
-        for o in range(group):
-            out_ref[o * INPUTS : o * INPUTS + span, o * columns : (o + 1) * columns] = sketch_ref[...]
-
-    return pl.pallas_call(
-        kernel,
-        out_shape=jax.ShapeDtypeStruct((span + LANES, group * columns), BF16),
-        compiler_params=pltpu.CompilerParams(vmem_limit_bytes=16 * MIB),
-    )(sketch)
-
-
-def hankel_times(blocks, wide):
-    rows, width = blocks[0].shape
-    group = LANES // INPUTS
-    columns = wide.shape[1] // group
     groups = width // LANES
-    reach = wide.shape[0]
+    reach = span + LANES
     n_blocks = len(blocks)
 
     def kernel(*refs):
-        wide_ref, out_ref, ext = refs[n_blocks:]
+        sketch_ref, out_ref, ext, wide = refs[n_blocks:]
         g = pl.program_id(0)
 
         @pl.when(g == 0)
         def _():
             for b in range(n_blocks):
                 ext[:, b * width : (b + 1) * width] = refs[b][...]
+            for o in range(group):
+                at = slice(o * columns, (o + 1) * columns)
+                top = o * INPUTS
+                wide[top : top + span, at] = sketch_ref[...]
+                if o:
+                    wide[:top, at] = jnp.zeros((top, columns), BF16)
+                wide[top + span :, at] = jnp.zeros((LANES - top, columns), BF16)
 
         window = ext[:, pl.ds(pl.multiple_of(g * LANES, LANES), reach)]
-        image = jnp.dot(window, wide_ref[...], preferred_element_type=F32)
+        image = jnp.dot(window, wide[...], preferred_element_type=F32)
         for o in range(group):
             out_ref[o] = image[:, o * columns : (o + 1) * columns]
 
@@ -151,19 +185,23 @@
         kernel,
         grid=(groups,),
         in_specs=[pl.BlockSpec((rows, width), lambda g: (0, 0))] * n_blocks
-        + [pl.BlockSpec(wide.shape, lambda g: (0, 0))],
+        + [pl.BlockSpec(sketch.shape, lambda g: (0, 0))],
         out_specs=pl.BlockSpec((group, rows, columns), lambda g: (g, 0, 0)),
         out_shape=jax.ShapeDtypeStruct((groups * group, rows, columns), F32),
-        scratch_shapes=[pltpu.VMEM((rows, n_blocks * width), BF16)],
-        compiler_params=pltpu.CompilerParams(vmem_limit_bytes=20 * MIB),
-    )(*blocks, wide)
+        scratch_shapes=[
+            pltpu.VMEM((rows, n_blocks * width), BF16),
+            pltpu.VMEM((reach, group * columns), BF16),
+        ],
+        compiler_params=pltpu.CompilerParams(vmem_limit_bytes=13 * MIB),
+        cost_estimate=costs(2 * groups * rows * reach * group * columns, 4 * groups * rows * group * columns),
+    )(*blocks, sketch)
 
 
 def across(a, b):
     return lax.dot_general(a, b, (((0,), (0,)), ((), ())), preferred_element_type=F32)
 
 
-def gram_image(place, first, second, back, ahead, swap, parts, sketch, scale):
+def gram_image(place, first, second, even_pair, odd_pair, swap, parts, sketch, scale):
     half, width = first.shape
     span, columns = sketch.shape
     tiles = len(parts)
@@ -172,7 +210,7 @@
     pair = 2 * LANES
     groups = span // LANES
 
-    def kernel(place_ref, first_ref, second_ref, back_ref, ahead_ref, swap_ref, *refs):
+    def kernel(place_ref, first_ref, second_ref, even_ref, odd_ref, swap_ref, *refs):
         part_refs = refs[:tiles]
         sketch_ref, image_ref, own, left, right, lag, early, full, turned = refs[tiles:]
         spot = place_ref[0]
@@ -183,6 +221,21 @@
             keep = part_refs[m][capacity : capacity + TAIL, :][:1]
             own[at, :] = source[m * capacity - base : (m + 1) * capacity - base, :] * keep
 
+        upper = lax.rem(spot // 2, 2)
+
+        @pl.when(upper == 0)
+        def _():
+            left[2 * half : 3 * half, :] = odd_ref[...]
+            right[3 * half :, :] = even_ref[...]
+
+        @pl.when(upper == 1)
+        def _():
+            left[2 * half : 3 * half, :] = even_ref[...]
+            right[3 * half :, :] = odd_ref[...]
+
+        left[3 * half :, :] = own[half:, :]
+        right[2 * half : 3 * half, :] = own[:half, :]
+
         @pl.when(odd == 0)
         def _():
             for m in range(tiles // 2, tiles):
@@ -192,7 +245,7 @@
                 right[at, :] = mine
                 left[half + m * capacity - half : half + (m + 1) * capacity - half, :] = mine
             left[:half, :] = own[half:, :]
-            right[half : 2 * half, :] = ahead_ref[...]
+            right[half : 2 * half, :] = right[3 * half :, :]
 
         @pl.when(odd == 1)
         def _():
@@ -203,12 +256,8 @@
                 left[at, :] = mine
                 right[half + m * capacity : half + (m + 1) * capacity, :] = mine
             right[:half, :] = own[:half, :]
-            left[half : 2 * half, :] = back_ref[...]
-
-        left[2 * half : 3 * half, :] = back_ref[...]
-        left[3 * half :, :] = own[half:, :]
-        right[2 * half : 3 * half, :] = own[:half, :]
-        right[3 * half :, :] = ahead_ref[...]
+            left[half : 2 * half, :] = left[2 * half : 3 * half, :]
+
         lag[...] = jnp.zeros_like(lag)
 
         @pl.when(spot < 2)
@@ -324,18 +373,21 @@
             pltpu.VMEM((span, span), F32),
             pltpu.VMEM((columns, span), F32),
         ],
-        compiler_params=pltpu.CompilerParams(vmem_limit_bytes=28 * MIB),
-    )(place, first, second, back, ahead, swap, *parts, sketch)
-
-
-def reduce_scatter(total, axes, rounds):
+        compiler_params=pltpu.CompilerParams(vmem_limit_bytes=18 * MIB),
+        cost_estimate=costs(5e9),
+    )(place, first, second, even_pair, odd_pair, swap, *parts, sketch)
+
+
+def reduce_scatter(total, axes, rounds, left=None, gate=None):
     count = math.prod(lax.axis_size(a) for a in axes)
     me = jnp.int32(0)
     for a in axes:
         me = me * lax.axis_size(a) + lax.axis_index(a)
     bits = int(math.log2(count))
-    value = total.reshape((2,) * bits + (total.shape[0] // count, total.shape[1]))
-    left = list(range(bits))
+    left = list(range(bits)) if left is None else left
+    value = total
+    if value.ndim == 2:
+        value = total.reshape((2,) * bits + (total.shape[0] // count, total.shape[1]))
     for bunch in rounds:
         dims = [left.index(b) for b in bunch]
         value = jnp.moveaxis(value, dims, range(len(bunch)))
@@ -345,16 +397,25 @@
         for b in bunch:
             mine = mine * 2 + ((me >> (bits - 1 - b)) & 1)
         acc = lax.dynamic_index_in_dim(value, mine, 0, keepdims=False)
+        came = []
         for mask in range(1, 2 ** len(bunch)):
             flip = 0
             for place, b in enumerate(bunch):
                 if (mask >> (len(bunch) - 1 - place)) & 1:
                     flip |= 1 << (bits - 1 - b)
-            acc = acc + crossed(lax.dynamic_index_in_dim(value, mine ^ mask, 0, keepdims=False), axes, flip)
+            piece = lax.dynamic_index_in_dim(value, mine ^ mask, 0, keepdims=False)
+            if len(bunch) == 1:
+                came.append(jnp.stack([crossed(part, axes, flip) for part in piece]))
+            else:
+                came.append(crossed(piece, axes, flip))
+        if gate is not None and len(left) == len(bunch):
+            came, gate = lax.optimization_barrier((came, gate))
+        for piece in came:
+            acc = acc + piece
         value = acc
         for b in bunch:
             left.remove(b)
-    return value
+    return value if gate is None else (value, gate)
 
 
 def local(state_tiles, sketch, probe_cell, probe_row):
@@ -362,22 +423,28 @@
     width = state_tiles.shape[1]
     steps_here = width // INPUTS
     probe_row = probe_row[0]
-    *parts, first, second, swap = pick_rows(state_tiles, probe_cell[0], probe_row)
+    parts = pick_rows(state_tiles, probe_cell[0], probe_row)
     arrived = [parts[0]] + [crossed(parts[m], ("sensor",), m) for m in range(1, n_tiles)]
+    first, second, swap, even_pair, odd_pair = prepare(parts)
     swapped = crossed(swap, ("tm",), 1)
-    back = shifted(first, "tm", 2)
-    ahead = shifted(second, "tm", -2)
+    even_pair = paired(even_pair, "tm", 2, 0)
+    odd_pair = paired(odd_pair, "tm", 2, 1)
     own_block = place_rows(probe_row, arrived)
-    blocks = [own_block, shifted(own_block, "tm", -1), shifted(own_block, "tm", -2)]
+    own_block, first = lax.optimization_barrier((own_block, first))
+    next_two = shifted(own_block, "tm", -2)
     scale = 1.0 / math.sqrt(SENS_DEV * n_tiles * steps_here * lax.axis_size("tm"))
     place = lax.axis_index("tm").astype(jnp.int32).reshape(1)
-    total = gram_image(place, first, second, back, ahead, swapped, arrived, sketch, scale)
-    hankel_sketch = hankel_times(blocks, widen(sketch))
+    total = gram_image(place, first, second, even_pair, odd_pair, swapped, arrived, sketch, scale)
     tm_bits = int(math.log2(lax.axis_size("tm")))
     sensor_bits = int(math.log2(n_tiles))
     last = tm_bits + sensor_bits - 1
-    rounds = [[last], list(range(tm_bits - 1, last)), list(range(tm_bits - 1))]
-    column_image = reduce_scatter(total, ("tm", "sensor"), rounds)
+    axes = ("tm", "sensor")
+    total = reduce_scatter(total, axes, [[last]])
+    total, next_two = lax.optimization_barrier((total, next_two))
+    next_one = crossed(jnp.where(lax.rem(place[0], 2) == 0, next_two, own_block), ("tm",), 1)
+    hankel_sketch = hankel_times([own_block, next_one, next_two], sketch)
+    rounds = [list(range(tm_bits - 1, last)), list(range(tm_bits - 1))]
+    column_image, hankel_sketch = reduce_scatter(total, axes, rounds, list(range(last)), hankel_sketch)
     return (hankel_sketch, column_image)
 
 

time: 55.6 us -> 46.1 us (0.83)
  the two profiles are of different devices: /device:TPU:2 before, /device:TPU:0 now
where the time goes in v3:
time: 46.1 us; the launch traced here: 45.9 us
  starting transfers between devices  18.7 us (41%)
  Pallas kernels  13.4 us (29%)
  waiting for transfers between devices  9.22 us (20%)
  local copies, waits for them, and re-layouts  3.05 us (7%)
  between operations  0.82 us (2%)
  other arithmetic  0.7 us (2%)
    ppermute x13, starting transfers between devices, crossed(): return lax.ppermute(x, axes, [(i, i ^ mask) for i in range(count)])  14.9 us
    ppermute x13, waiting for transfers between devices, crossed(): return lax.ppermute(x, axes, [(i, i ^ mask) for i in range(count)])  9.21 us
    pallas_call x1, Pallas kernels, gram_image(): pl.pallas_call(kernel, in_specs=[smem] + [vmem] * (6 + tiles), out_specs=...  5.96 us
    pallas_call x1, Pallas kernels, hankel_times(): pl.pallas_call(kernel, grid=(groups,), in_specs=[pl.BlockSpec((rows, widt...  4.91 us
    unnamed x10, local copies, waits for them, and re-layouts  2.96 us
    ppermute x2, starting transfers between devices, paired(): lax.ppermute(x, axis, [(i, i + by) for i in low] + [(i + by, i) for i in...  2.52 us
    pallas_call x1, Pallas kernels, pick_rows(): pl.pallas_call(kernel, grid=(steps,), in_specs=[whole(probe_cell.shape),...  2.03 us
    ppermute x1, starting transfers between devices, shifted(): return lax.ppermute(x, axis, pairs)  1.29 us
  transfers between devices with their start and end apart: 16, of which 8 were waited for; matrix products, arithmetic and copies ran while one was open for 0% of the time, Pallas kernels for 25%

profile of v3, /device:TPU:0, one launch (start us, length us, event | category | flops | bytes accessed | tf_op | source)
XLA Modules:
  0.0 45.9 jit_solution(1815158480928067483)
XLA Ops:
  0.6 1.6 %copy-done = bf16[2048,512]{1,0:T(8,128)(2,1)S(1)} copy-done((bf16[2048,512]{1,0:T(8,128)(2,1)S(1)}, bf16[2048,512]{1,0:T(8,128)(2,1)}, u32[]{:S(2)}) %copy-start) | copy-done | bytes 2097176
  2.2 0.7 %copy-done.2 = s32[1,4,128]{2,1,0:T(4,128)S(1)} copy-done((s32[1,4,128]{2,1,0:T(4,128)S(1)}, s32[1,4,128]{2,1,0:T(4,128)}, u32[]{:S(2)}) %copy-start.2) | copy-done | bytes 2072
  2.9 0.7 %copy-done.3 = s32[1,4,128]{2,1,0:T(4,128)S(1)} copy-done((s32[1,4,128]{2,1,0:T(4,128)S(1)}, s32[1,4,128]{2,1,0:T(4,128)}, u32[]{:S(2)}) %copy-start.3) | copy-done | bytes 2072
  3.6 2.0 %shard_map.59 = (bf16[144,512]{1,0:T(8,128)(2,1)S(1)}, bf16[144,512]{1,0:T(8,128)(2,1)S(1)}, bf16[144,512]{1,0:T(8,128)(2,1)S(1)}, bf16[144,512]{1,0:T(8,128)(2,1)S(1)}) custom-call(s32[4,128]{1,0:T(4,128)S(1)} %bitcast.44, s32[4,128]{1,0:T(4,128)S(1)} %bitcast.45, bf16[2048,512]{1,0:T(8,128)(2,1)S(1)} %copy-done), custom_call_target="tpu_custom_call" | custom-call | flops 1073741824 | bytes 2097152 | tf_op jit(solution)/shard_map/pallas_call | solution.py:77
  5.6 0.5 %collective-permute-start = (bf16[144,512]{1,0:T(8,128)(2,1)S(1)}, bf16[144,512]{1,0:T(8,128)(2,1)S(1)}, u32[]{:S(2)}, u32[]{:S(2)}) collective-permute-start(bf16[144,512]{1,0:T(8,128)(2,1)S(1)} %get-tuple-element.20.refs_1_), channel_id=1, source_target_pairs={{0,1},{1,0},{2,3},{3,2},{4,5},{5,4},{6,7},{7,6},{8,9},{9,8},{10,11... | collective-permute-start | bytes 442376 | tf_op jit(solution)/shard_map/ppermute | solution.py:37
  6.2 2.6 %collective-permute-start.1 = (bf16[144,512]{1,0:T(8,128)(2,1)S(1)}, bf16[144,512]{1,0:T(8,128)(2,1)S(1)}, u32[]{:S(2)}, u32[]{:S(2)}) collective-permute-start(bf16[144,512]{1,0:T(8,128)(2,1)S(1)} %get-tuple-element.21.refs_2_), channel_id=1, source_target_pairs={{0,2},{1,3},{2,0},{3,1},{4,6},{5,7},{6,4},{7,5},{8,10},{9,11},{10,... | collective-permute-start | bytes 442376 | tf_op jit(solution)/shard_map/ppermute | solution.py:37
  8.8 0.1 shard_map.61
  8.9 1.9 %collective-permute-start.3 = (bf16[256,512]{1,0:T(8,128)(2,1)S(1)}, bf16[256,512]{1,0:T(8,128)(2,1)S(1)}, u32[]{:S(2)}, u32[]{:S(2)}) collective-permute-start(bf16[256,512]{1,0:T(8,128)(2,1)S(1)} %get-tuple-element.26), channel_id=1, source_target_pairs={{0,8},{4,12},{16,24},{20,28},{8,0},{12,4},{24,16},{28,20},{1,9},{5... | collective-permute-start | bytes 786440 | tf_op jit(solution)/shard_map/ppermute | solution.py:32
  10.8 0.7 %collective-permute-start.4 = (bf16[256,512]{1,0:T(8,128)(2,1)S(1)}, bf16[256,512]{1,0:T(8,128)(2,1)S(1)}, u32[]{:S(2)}, u32[]{:S(2)}) collective-permute-start(bf16[256,512]{1,0:T(8,128)(2,1)S(1)} %get-tuple-element.27), channel_id=1, source_target_pairs={{8,16},{12,20},{16,8},{20,12},{9,17},{13,21},{17,9},{21,13},{10,18... | collective-permute-start | bytes 786440 | tf_op jit(solution)/shard_map/ppermute | solution.py:32
  11.5 1.6 %collective-permute-start.5 = (bf16[256,512]{1,0:T(8,128)(2,1)S(1)}, bf16[256,512]{1,0:T(8,128)(2,1)S(1)}, u32[]{:S(2)}, u32[]{:S(2)}) collective-permute-start(bf16[256,512]{1,0:T(8,128)(2,1)S(1)} %get-tuple-element.28), channel_id=1, source_target_pairs={{0,4},{4,0},{8,12},{12,8},{16,20},{20,16},{24,28},{28,24},{1,5},{5... | collective-permute-start | bytes 786440 | tf_op jit(solution)/shard_map/ppermute | solution.py:37
  13.0 0.4 collective-permute-done.1.refs_2_
  13.4 2.6 %collective-permute-done.2.refs_3_ = bf16[144,512]{1,0:T(8,128)(2,1)S(1)} collective-permute-done((bf16[144,512]{1,0:T(8,128)(2,1)S(1)}, bf16[144,512]{1,0:T(8,128)(2,1)S(1)}, u32[]{:S(2)}, u32[]{:S(2)}) %collective-permute-start.2) | collective-permute-done | bytes 147488 | tf_op jit(solution)/shard_map/ppermute | solution.py:37
  16.1 0.4 shard_map.60.refs_0_
  16.5 1.3 %collective-permute-start.8 = (bf16[256,512]{1,0:T(8,128)(2,1)S(1)}, bf16[256,512]{1,0:T(8,128)(2,1)S(1)}, u32[]{:S(2)}, u32[]{:S(2)}) collective-permute-start(bf16[256,512]{1,0:T(8,128)(2,1)S(1)} %shard_map.60.refs_0_), channel_id=1, source_target_pairs={{8,0},{12,4},{16,8},{20,12},{24,16},{28,20},{9,1},{13,5},{17,9},{2... | collective-permute-start | bytes 786440 | tf_op jit(solution)/shard_map/ppermute | solution.py:26
  17.8 2.0 %collective-permute-done.5.swap_ref = bf16[256,512]{1,0:T(8,128)(2,1)S(1)} collective-permute-done((bf16[256,512]{1,0:T(8,128)(2,1)S(1)}, bf16[256,512]{1,0:T(8,128)(2,1)S(1)}, u32[]{:S(2)}, u32[]{:S(2)}) %collective-permute-start.5) | collective-permute-done | bytes 262176 | tf_op jit(solution)/shard_map/ppermute | solution.py:37
  19.8 6.0 %shard_map.62 = f32[1024,128]{1,0:T(8,128)S(1)} custom-call(s32[1]{0:T(128)} %bitcast.place_ref, bf16[256,512]{1,0:T(8,128)(2,1)S(1)} %get-tuple-element.24.first_ref, bf16[256,512]{1,0:T(8,128)(2,1)S(1)} %get-tuple-element.25.second_ref, bf16[256,512]{1,0:T(8,128)(2,1)S(1)} %collective-permute-done.3.even_ref, ...), custom_call_target="tpu_custom_call" | custom-call | flops 5000000000 | tf_op jit(solution)/shard_map/pallas_call | solution.py:362
  25.9 0.1 collective-permute-start.6
  25.9 0.5 %collective-permute-start.7 = (f32[2,2,2,32,128]{4,3,2,1,0:T(8,128)S(1)}, f32[2,2,2,32,128]{4,3,2,1,0:T(8,128)S(1)}, u32[]{:S(2)}, u32[]{:S(2)}) collective-permute-start(f32[2,2,2,32,128]{4,3,2,1,0:T(8,128)S(1)} %get-tuple-element.40), channel_id=1, source_target_pairs={{0,1},{1,0},{2,3},{3,2},{4,5},{5,4},{6,7},{7,6},{8,9},{9,8},{10,11... | collective-permute-start | bytes 393224 | tf_op jit(solution)/shard_map/ppermute | solution.py:37
  26.4 0.8 %collective-permute-done.6 = f32[2,2,2,32,128]{4,3,2,1,0:T(8,128)S(1)} collective-permute-done((f32[2,2,2,32,128]{4,3,2,1,0:T(8,128)S(1)}, f32[2,2,2,32,128]{4,3,2,1,0:T(8,128)S(1)}, u32[]{:S(2)}, u32[]{:S(2)}) %collective-permute-start.6) | collective-permute-done | bytes 131104 | tf_op jit(solution)/shard_map/ppermute | solution.py:37
  27.3 0.2 collective-permute-done.7
  27.5 1.6 %collective-permute-start.9 = (f32[2,2,32,128]{3,2,1,0:T(8,128)S(1)}, f32[2,2,32,128]{3,2,1,0:T(8,128)S(1)}, u32[]{:S(2)}, u32[]{:S(2)}) collective-permute-start(f32[2,2,32,128]{3,2,1,0:T(8,128)S(1)} %get-tuple-element.36), channel_id=1, source_target_pairs={{0,2},{1,3},{2,0},{3,1},{4,6},{5,7},{6,4},{7,5},{8,10},{9,11},{10,... | collective-permute-start | bytes 196616 | tf_op jit(solution)/shard_map/ppermute | solution.py:37
  29.1 1.5 %collective-permute-start.11 = (f32[2,2,32,128]{3,2,1,0:T(8,128)S(1)}, f32[2,2,32,128]{3,2,1,0:T(8,128)S(1)}, u32[]{:S(2)}, u32[]{:S(2)}) collective-permute-start(f32[2,2,32,128]{3,2,1,0:T(8,128)S(1)} %get-tuple-element.37), channel_id=1, source_target_pairs={{0,6},{1,7},{2,4},{3,5},{4,2},{5,3},{6,0},{7,1},{8,14},{9,15},{10,... | collective-permute-start | bytes 196616 | tf_op jit(solution)/shard_map/ppermute | solution.py:37
  30.6 0.5 %collective-permute-start.10 = (f32[2,2,32,128]{3,2,1,0:T(8,128)S(1)}, f32[2,2,32,128]{3,2,1,0:T(8,128)S(1)}, u32[]{:S(2)}, u32[]{:S(2)}) collective-permute-start(f32[2,2,32,128]{3,2,1,0:T(8,128)S(1)} %get-tuple-element.38), channel_id=1, source_target_pairs={{0,4},{1,5},{2,6},{3,7},{4,0},{5,1},{6,2},{7,3},{8,12},{9,13},{10,... | collective-permute-start | bytes 196616 | tf_op jit(solution)/shard_map/ppermute | solution.py:37
  31.1 1.6 %collective-permute-start.15 = (bf16[256,512]{1,0:T(8,128)(2,1)S(1)}, bf16[256,512]{1,0:T(8,128)(2,1)S(1)}, u32[]{:S(2)}, u32[]{:S(2)}) collective-permute-start(bf16[256,512]{1,0:T(8,128)(2,1)S(1)} %broadcast_select_fusion), channel_id=1, source_target_pairs={{0,4},{4,0},{8,12},{12,8},{16,20},{20,16},{24,28},{28,24},{1,5},{5... | collective-permute-start | bytes 786440 | tf_op jit(solution)/shard_map/ppermute | solution.py:37
  32.7 1.9 %collective-permute-done.11 = f32[2,2,32,128]{3,2,1,0:T(8,128)S(1)} collective-permute-done((f32[2,2,32,128]{3,2,1,0:T(8,128)S(1)}, f32[2,2,32,128]{3,2,1,0:T(8,128)S(1)}, u32[]{:S(2)}, u32[]{:S(2)}) %collective-permute-start.11) | collective-permute-done | bytes 65568 | tf_op jit(solution)/shard_map/ppermute | solution.py:37
  34.7 0.9 %collective-permute-done.10 = f32[2,2,32,128]{3,2,1,0:T(8,128)S(1)} collective-permute-done((f32[2,2,32,128]{3,2,1,0:T(8,128)S(1)}, f32[2,2,32,128]{3,2,1,0:T(8,128)S(1)}, u32[]{:S(2)}, u32[]{:S(2)}) %collective-permute-start.10) | collective-permute-done | bytes 65568 | tf_op jit(solution)/shard_map/ppermute | solution.py:37
  35.6 1.3 %collective-permute-start.14 = (f32[32,128]{1,0:T(8,128)S(1)}, f32[32,128]{1,0:T(8,128)S(1)}, u32[]{:S(2)}, u32[]{:S(2)}) collective-permute-start(f32[32,128]{1,0:T(8,128)S(1)} %get-tuple-element.41), channel_id=1, source_target_pairs={{0,24},{1,25},{2,26},{3,27},{4,28},{5,29},{6,30},{7,31},{8,16},{9,... | collective-permute-start | bytes 49160 | tf_op jit(solution)/shard_map/ppermute | solution.py:37
  37.0 1.4 %collective-permute-start.13 = (f32[32,128]{1,0:T(8,128)S(1)}, f32[32,128]{1,0:T(8,128)S(1)}, u32[]{:S(2)}, u32[]{:S(2)}) collective-permute-start(f32[32,128]{1,0:T(8,128)S(1)} %get-tuple-element.42), channel_id=1, source_target_pairs={{0,16},{1,17},{2,18},{3,19},{4,20},{5,21},{6,22},{7,23},{8,24},{9,... | collective-permute-start | bytes 49160 | tf_op jit(solution)/shard_map/ppermute | solution.py:37
  38.4 1.7 %collective-permute-start.12 = (f32[32,128]{1,0:T(8,128)S(1)}, f32[32,128]{1,0:T(8,128)S(1)}, u32[]{:S(2)}, u32[]{:S(2)}) collective-permute-start(f32[32,128]{1,0:T(8,128)S(1)} %get-tuple-element.43), channel_id=1, source_target_pairs={{0,8},{1,9},{2,10},{3,11},{4,12},{5,13},{6,14},{7,15},{8,0},{9,1},... | collective-permute-start | bytes 49160 | tf_op jit(solution)/shard_map/ppermute | solution.py:37
  40.1 0.3 collective-permute-done.15.refs_1_
  40.4 4.9 %shard_map.63 = f32[32,256,128]{2,1,0:T(8,128)} custom-call(bf16[256,512]{1,0:T(8,128)(2,1)S(1)} %shard_map.60.refs_0_, bf16[256,512]{1,0:T(8,128)(2,1)S(1)} %collective-permute-done.15.refs_1_, bf16[256,512]{1,0:T(8,128)(2,1)S(1)} %collective-permute-done.8.refs_2_, bf16[1024,128]{1,0:T(8,128)(2,1)S(1)} %copy-done.1), custom_call_target="tpu_custom_call" | custom-call | flops 2415919104 | bytes 4194304 | tf_op jit(solution)/shard_map/pallas_call | solution.py:184
  45.3 0.6 %fusion.3 = f32[32,128]{1,0:T(8,128)} fusion(f32[32,128]{1,0:T(8,128)S(1)} %collective-permute-done.14, f32[32,128]{1,0:T(8,128)S(1)} %collective-permute-done.13, f32[32,128]{1,0:T(8,128)S(1)} %collective-permute-done.12, f32[4,32,128]{2,1,0:T(8,128)S(1)} %bitcast.50, s32[]{:T(128)S(6)} %select_n.52), kind=kLoop, calls=%fused_computation.13 | loop fusion | flops 12288 | bytes 81924 | tf_op jit(solution)/shard_map/add | solution.py:414
  (23 shorter events, 0.3 us)
Async XLA Ops:
  0.6 15.5 %copy-start.4 = (s32[1,4,128]{2,1,0:T(4,128)S(1)}, s32[1,4,128]{2,1,0:T(4,128)}, u32[]{:S(2)}) copy-start(s32[1,4,128]{2,1,0:T(4,128)} %param.7) | copy-start | bytes 6148
  0.6 1.6 %copy-start = (bf16[2048,512]{1,0:T(8,128)(2,1)S(1)}, bf16[2048,512]{1,0:T(8,128)(2,1)}, u32[]{:S(2)}) copy-start(bf16[2048,512]{1,0:T(8,128)(2,1)} %state_ref.1) | copy-start | bytes 6291460
  2.2 0.7 %copy-start.2 = (s32[1,4,128]{2,1,0:T(4,128)S(1)}, s32[1,4,128]{2,1,0:T(4,128)}, u32[]{:S(2)}) copy-start(s32[1,4,128]{2,1,0:T(4,128)} %param.6) | copy-start | bytes 6148
  2.9 0.7 %copy-start.3 = (s32[1,4,128]{2,1,0:T(4,128)S(1)}, s32[1,4,128]{2,1,0:T(4,128)}, u32[]{:S(2)}) copy-start(s32[1,4,128]{2,1,0:T(4,128)} %param.7) | copy-start | bytes 6148
  5.6 5.8 %collective-permute-start = (bf16[144,512]{1,0:T(8,128)(2,1)S(1)}, bf16[144,512]{1,0:T(8,128)(2,1)S(1)}, u32[]{:S(2)}, u32[]{:S(2)}) collective-permute-start(bf16[144,512]{1,0:T(8,128)(2,1)S(1)} %get-tuple-element.20.refs_1_), channel_id=1, source_target_pairs={{0,1},{1,0},{2,3},{3,2},{4,5},{5,4},{6,7},{7,6},{8,9},{9,8},{10,11... | collective-permute-start | bytes 442376 | tf_op jit(solution)/shard_map/ppermute | solution.py:37
  6.2 7.3 %collective-permute-start.1 = (bf16[144,512]{1,0:T(8,128)(2,1)S(1)}, bf16[144,512]{1,0:T(8,128)(2,1)S(1)}, u32[]{:S(2)}, u32[]{:S(2)}) collective-permute-start(bf16[144,512]{1,0:T(8,128)(2,1)S(1)} %get-tuple-element.21.refs_2_), channel_id=1, source_target_pairs={{0,2},{1,3},{2,0},{3,1},{4,6},{5,7},{6,4},{7,5},{8,10},{9,11},{10,... | collective-permute-start | bytes 442376 | tf_op jit(solution)/shard_map/ppermute | solution.py:37
  8.8 7.3 %collective-permute-start.2 = (bf16[144,512]{1,0:T(8,128)(2,1)S(1)}, bf16[144,512]{1,0:T(8,128)(2,1)S(1)}, u32[]{:S(2)}, u32[]{:S(2)}) collective-permute-start(bf16[144,512]{1,0:T(8,128)(2,1)S(1)} %get-tuple-element.22.refs_3_), channel_id=1, source_target_pairs={{0,3},{1,2},{2,1},{3,0},{4,7},{5,6},{6,5},{7,4},{8,11},{9,10},{10,... | collective-permute-start | bytes 442376 | tf_op jit(solution)/shard_map/ppermute | solution.py:37
  8.9 8.9 %collective-permute-start.3 = (bf16[256,512]{1,0:T(8,128)(2,1)S(1)}, bf16[256,512]{1,0:T(8,128)(2,1)S(1)}, u32[]{:S(2)}, u32[]{:S(2)}) collective-permute-start(bf16[256,512]{1,0:T(8,128)(2,1)S(1)} %get-tuple-element.26), channel_id=1, source_target_pairs={{0,8},{4,12},{16,24},{20,28},{8,0},{12,4},{24,16},{28,20},{1,9},{5... | collective-permute-start | bytes 786440 | tf_op jit(solution)/shard_map/ppermute | solution.py:32
  10.8 7.1 %collective-permute-start.4 = (bf16[256,512]{1,0:T(8,128)(2,1)S(1)}, bf16[256,512]{1,0:T(8,128)(2,1)S(1)}, u32[]{:S(2)}, u32[]{:S(2)}) collective-permute-start(bf16[256,512]{1,0:T(8,128)(2,1)S(1)} %get-tuple-element.27), channel_id=1, source_target_pairs={{8,16},{12,20},{16,8},{20,12},{9,17},{13,21},{17,9},{21,13},{10,18... | collective-permute-start | bytes 786440 | tf_op jit(solution)/shard_map/ppermute | solution.py:32
  11.5 8.4 %copy-start.1 = (bf16[1024,128]{1,0:T(8,128)(2,1)S(1)}, bf16[1024,128]{1,0:T(8,128)(2,1)}, u32[]{:S(2)}) copy-start(bf16[1024,128]{1,0:T(8,128)(2,1)} %refs_3_.1) | copy-start | bytes 786436
  11.5 8.3 %collective-permute-start.5 = (bf16[256,512]{1,0:T(8,128)(2,1)S(1)}, bf16[256,512]{1,0:T(8,128)(2,1)S(1)}, u32[]{:S(2)}, u32[]{:S(2)}) collective-permute-start(bf16[256,512]{1,0:T(8,128)(2,1)S(1)} %get-tuple-element.28), channel_id=1, source_target_pairs={{0,4},{4,0},{8,12},{12,8},{16,20},{20,16},{24,28},{28,24},{1,5},{5... | collective-permute-start | bytes 786440 | tf_op jit(solution)/shard_map/ppermute | solution.py:37
  16.5 11.0 %collective-permute-start.8 = (bf16[256,512]{1,0:T(8,128)(2,1)S(1)}, bf16[256,512]{1,0:T(8,128)(2,1)S(1)}, u32[]{:S(2)}, u32[]{:S(2)}) collective-permute-start(bf16[256,512]{1,0:T(8,128)(2,1)S(1)} %shard_map.60.refs_0_), channel_id=1, source_target_pairs={{8,0},{12,4},{16,8},{20,12},{24,16},{28,20},{9,1},{13,5},{17,9},{2... | collective-permute-start | bytes 786440 | tf_op jit(solution)/shard_map/ppermute | solution.py:26
  25.9 1.4 %collective-permute-start.6 = (f32[2,2,2,32,128]{4,3,2,1,0:T(8,128)S(1)}, f32[2,2,2,32,128]{4,3,2,1,0:T(8,128)S(1)}, u32[]{:S(2)}, u32[]{:S(2)}) collective-permute-start(f32[2,2,2,32,128]{4,3,2,1,0:T(8,128)S(1)} %get-tuple-element.39), channel_id=1, source_target_pairs={{0,1},{1,0},{2,3},{3,2},{4,5},{5,4},{6,7},{7,6},{8,9},{9,8},{10,11... | collective-permute-start | bytes 393224 | tf_op jit(solution)/shard_map/ppermute | solution.py:37
  25.9 1.5 %collective-permute-start.7 = (f32[2,2,2,32,128]{4,3,2,1,0:T(8,128)S(1)}, f32[2,2,2,32,128]{4,3,2,1,0:T(8,128)S(1)}, u32[]{:S(2)}, u32[]{:S(2)}) collective-permute-start(f32[2,2,2,32,128]{4,3,2,1,0:T(8,128)S(1)} %get-tuple-element.40), channel_id=1, source_target_pairs={{0,1},{1,0},{2,3},{3,2},{4,5},{5,4},{6,7},{7,6},{8,9},{9,8},{10,11... | collective-permute-start | bytes 393224 | tf_op jit(solution)/shard_map/ppermute | solution.py:37
  27.5 5.2 %collective-permute-start.9 = (f32[2,2,32,128]{3,2,1,0:T(8,128)S(1)}, f32[2,2,32,128]{3,2,1,0:T(8,128)S(1)}, u32[]{:S(2)}, u32[]{:S(2)}) collective-permute-start(f32[2,2,32,128]{3,2,1,0:T(8,128)S(1)} %get-tuple-element.36), channel_id=1, source_target_pairs={{0,2},{1,3},{2,0},{3,1},{4,6},{5,7},{6,4},{7,5},{8,10},{9,11},{10,... | collective-permute-start | bytes 196616 | tf_op jit(solution)/shard_map/ppermute | solution.py:37
  29.1 5.5 %collective-permute-start.11 = (f32[2,2,32,128]{3,2,1,0:T(8,128)S(1)}, f32[2,2,32,128]{3,2,1,0:T(8,128)S(1)}, u32[]{:S(2)}, u32[]{:S(2)}) collective-permute-start(f32[2,2,32,128]{3,2,1,0:T(8,128)S(1)} %get-tuple-element.37), channel_id=1, source_target_pairs={{0,6},{1,7},{2,4},{3,5},{4,2},{5,3},{6,0},{7,1},{8,14},{9,15},{10,... | collective-permute-start | bytes 196616 | tf_op jit(solution)/shard_map/ppermute | solution.py:37
  30.6 5.0 %collective-permute-start.10 = (f32[2,2,32,128]{3,2,1,0:T(8,128)S(1)}, f32[2,2,32,128]{3,2,1,0:T(8,128)S(1)}, u32[]{:S(2)}, u32[]{:S(2)}) collective-permute-start(f32[2,2,32,128]{3,2,1,0:T(8,128)S(1)} %get-tuple-element.38), channel_id=1, source_target_pairs={{0,4},{1,5},{2,6},{3,7},{4,0},{5,1},{6,2},{7,3},{8,12},{9,13},{10,... | collective-permute-start | bytes 196616 | tf_op jit(solution)/shard_map/ppermute | solution.py:37
  31.1 9.2 %collective-permute-start.15 = (bf16[256,512]{1,0:T(8,128)(2,1)S(1)}, bf16[256,512]{1,0:T(8,128)(2,1)S(1)}, u32[]{:S(2)}, u32[]{:S(2)}) collective-permute-start(bf16[256,512]{1,0:T(8,128)(2,1)S(1)} %broadcast_select_fusion), channel_id=1, source_target_pairs={{0,4},{4,0},{8,12},{12,8},{16,20},{20,16},{24,28},{28,24},{1,5},{5... | collective-permute-start | bytes 786440 | tf_op jit(solution)/shard_map/ppermute | solution.py:37
  35.6 9.6 %collective-permute-start.14 = (f32[32,128]{1,0:T(8,128)S(1)}, f32[32,128]{1,0:T(8,128)S(1)}, u32[]{:S(2)}, u32[]{:S(2)}) collective-permute-start(f32[32,128]{1,0:T(8,128)S(1)} %get-tuple-element.41), channel_id=1, source_target_pairs={{0,24},{1,25},{2,26},{3,27},{4,28},{5,29},{6,30},{7,31},{8,16},{9,... | collective-permute-start | bytes 49160 | tf_op jit(solution)/shard_map/ppermute | solution.py:37
  37.0 8.3 %collective-permute-start.13 = (f32[32,128]{1,0:T(8,128)S(1)}, f32[32,128]{1,0:T(8,128)S(1)}, u32[]{:S(2)}, u32[]{:S(2)}) collective-permute-start(f32[32,128]{1,0:T(8,128)S(1)} %get-tuple-element.42), channel_id=1, source_target_pairs={{0,16},{1,17},{2,18},{3,19},{4,20},{5,21},{6,22},{7,23},{8,24},{9,... | collective-permute-start | bytes 49160 | tf_op jit(solution)/shard_map/ppermute | solution.py:37
  38.4 6.9 %collective-permute-start.12 = (f32[32,128]{1,0:T(8,128)S(1)}, f32[32,128]{1,0:T(8,128)S(1)}, u32[]{:S(2)}, u32[]{:S(2)}) collective-permute-start(f32[32,128]{1,0:T(8,128)S(1)} %get-tuple-element.43), channel_id=1, source_target_pairs={{0,8},{1,9},{2,10},{3,11},{4,12},{5,13},{6,14},{7,15},{8,0},{9,1},... | collective-permute-start | bytes 49160 | tf_op jit(solution)/shard_map/ppermute | solution.py:37

commit v4 on v3

--- a/solution.py
+++ b/solution.py
@@ -26,10 +26,16 @@
     return lax.ppermute(x, axis, pairs)
 
 
-def paired(x, axis, by, odd):
-    count = lax.axis_size(axis)
+def paired(x, by, odd):
+    count, width = lax.axis_size("tm"), lax.axis_size("sensor")
     low = [i for i in range(count - by) if (i // by) % 2 == odd]
-    return lax.ppermute(x, axis, [(i, i + by) for i in low] + [(i + by, i) for i in low])
+    partner = {i: i + by for i in low} | {i + by: i for i in low}
+    pairs = []
+    for i in range(count):
+        for j in range(width):
+            target = partner[i] * width + j if i in partner else i * width + (j ^ 1)
+            pairs.append((i * width + j, target))
+    return lax.ppermute(x, ("tm", "sensor"), pairs)
 
 
 def crossed(x, axes, mask):
@@ -44,50 +50,61 @@
     steps = 4
     chunk = cells_here // steps
 
-    def kernel(cell_ref, row_ref, state_ref, *refs):
+    def kernel(cell_hbm, row_hbm, state_hbm, *refs):
         parts = refs[:tiles]
-        slot, total = refs[tiles:]
-        k = pl.program_id(0)
+        row_ref, cell_ref, slot, total, state, came = refs[tiles:]
         me = lax.axis_index("sensor")
-
-        @pl.when(k == 0)
-        def _():
-            for m in range(tiles):
-                line = cell_ref[pl.ds(me ^ m, 1), :]
-                slot[m * capacity : (m + 1) * capacity, :] = jnp.broadcast_to(line, (LANES, capacity)).T
-            total[...] = jnp.zeros_like(total)
-
-        lane = lax.broadcasted_iota(jnp.int32, (rows, LANES), 1) + k * chunk
-        wanted = slot[...]
-        chosen = jnp.concatenate(
-            [jnp.where(wanted == lane + c, 1.0, 0.0).astype(BF16) for c in range(0, chunk, LANES)], axis=1
-        )
-        total[...] += jnp.dot(chosen, state_ref[...], preferred_element_type=F32)
-
-        @pl.when(k == steps - 1)
-        def _():
-            got = total[...].astype(BF16)
-            for m in range(tiles):
-                parts[m][:capacity, :] = got[m * capacity : (m + 1) * capacity]
-                filled = jnp.broadcast_to(row_ref[pl.ds(me ^ m, 1), :1], (TAIL, width)) >= 0
-                parts[m][capacity:, :] = jnp.where(filled, 1.0, 0.0).astype(BF16)
-
-    whole = lambda shape: pl.BlockSpec(shape, lambda k: (0,) * len(shape))
+        copies = [pltpu.make_async_copy(cell_hbm, cell_ref, came.at[steps])]
+        copies.append(pltpu.make_async_copy(row_hbm, row_ref, came.at[steps + 1]))
+        for k in range(steps):
+            at = slice(k * chunk, (k + 1) * chunk)
+            copies.append(pltpu.make_async_copy(state_hbm.at[at, :], state.at[at, :], came.at[k]))
+        for copy in copies:
+            copy.start()
+        copies[0].wait()
+        copies[1].wait()
+        for m in range(tiles):
+            line = cell_ref[pl.ds(me ^ m, 1), :]
+            slot[m * capacity : (m + 1) * capacity, :] = jnp.broadcast_to(line, (LANES, capacity)).T
+        lane = lax.broadcasted_iota(jnp.int32, (rows, LANES), 1)
+        for k in range(steps):
+            wanted = slot[...]
+            chosen = jnp.concatenate(
+                [jnp.where(wanted == lane + c, 1.0, 0.0).astype(BF16) for c in range(k * chunk, (k + 1) * chunk, LANES)],
+                axis=1,
+            )
+            copies[2 + k].wait()
+            got = jnp.dot(chosen, state[k * chunk : (k + 1) * chunk, :], preferred_element_type=F32)
+            if k:
+                got += total[...]
+            if k < steps - 1:
+                total[...] = got
+        got = got.astype(BF16)
+        for m in range(tiles):
+            parts[m][:capacity, :] = got[m * capacity : (m + 1) * capacity]
+            filled = jnp.broadcast_to(row_ref[pl.ds(me ^ m, 1), :1], (TAIL, width)) >= 0
+            parts[m][capacity:, :] = jnp.where(filled, 1.0, 0.0).astype(BF16)
+
     shapes = [(capacity + TAIL, width)] * tiles
     return pl.pallas_call(
         kernel,
-        grid=(steps,),
-        in_specs=[whole(probe_cell.shape), whole(probe_row.shape), pl.BlockSpec((chunk, width), lambda k: (k, 0))],
-        out_specs=[whole(s) for s in shapes],
-        out_shape=[jax.ShapeDtypeStruct(s, BF16) for s in shapes],
-        scratch_shapes=[pltpu.VMEM((rows, LANES), jnp.int32), pltpu.VMEM((rows, width), F32)],
+        in_specs=[pl.BlockSpec(memory_space=pltpu.HBM)] * 3,
+        out_specs=[pl.BlockSpec(memory_space=pltpu.VMEM)] * (tiles + 1),
+        out_shape=[jax.ShapeDtypeStruct(s, BF16) for s in shapes] + [jax.ShapeDtypeStruct(probe_row.shape, jnp.int32)],
+        scratch_shapes=[
+            pltpu.VMEM(probe_cell.shape, jnp.int32),
+            pltpu.VMEM((rows, LANES), jnp.int32),
+            pltpu.VMEM((rows, width), F32),
+            pltpu.VMEM((cells_here, width), BF16),
+            pltpu.SemaphoreType.DMA((steps + 2,)),
+        ],
         compiler_params=pltpu.CompilerParams(vmem_limit_bytes=10 * MIB),
         cost_estimate=costs(2 * rows * cells_here * width, 2 * cells_here * width),
-    )(probe_cell, probe_row, state_tiles)
-
-
-def place_rows(probe_row, parts):
-    tiles, capacity = probe_row.shape
+    )(*[pltpu.with_memory_space_constraint(x, pltpu.HBM) for x in (probe_cell, probe_row, state_tiles)])
+
+
+def place_rows(wanted, parts):
+    tiles, capacity = wanted.shape
     width = parts[0].shape[1]
 
     def kernel(row_ref, *refs):
@@ -105,7 +122,7 @@
         out_shape=jax.ShapeDtypeStruct((SENS_DEV, width), BF16),
         compiler_params=pltpu.CompilerParams(vmem_limit_bytes=8 * MIB),
         cost_estimate=costs(2e10),
-    )(probe_row, *parts)
+    )(wanted, *parts)
 
 
 def prepare(parts):
@@ -152,49 +169,70 @@
     )(*parts)
 
 
-def hankel_times(blocks, sketch):
-    rows, width = blocks[0].shape
+def hankel_ends(first, last, sketch):
+    rows, width = first.shape
     span, columns = sketch.shape
     group = LANES // INPUTS
     groups = width // LANES
-    reach = span + LANES
-    n_blocks = len(blocks)
-
-    def kernel(*refs):
-        sketch_ref, out_ref, ext, wide = refs[n_blocks:]
-        g = pl.program_id(0)
-
-        @pl.when(g == 0)
-        def _():
-            for b in range(n_blocks):
-                ext[:, b * width : (b + 1) * width] = refs[b][...]
+
+    def kernel(first_ref, last_ref, sketch_ref, out_ref, wide):
+        for o in range(group):
+            at = slice(o * columns, (o + 1) * columns)
+            top = o * INPUTS
+            wide[top : top + span, at] = sketch_ref[...]
+            if o:
+                wide[:top, at] = jnp.zeros((top, columns), BF16)
+            wide[top + span :, at] = jnp.zeros((LANES - top, columns), BF16)
+        for g in range(groups):
+            shift = g * LANES
+            image = jnp.dot(first_ref[:, shift:], wide[: width - shift, :], preferred_element_type=F32)
+            image += jnp.dot(last_ref[:, : shift + LANES], wide[span - shift :, :], preferred_element_type=F32)
             for o in range(group):
-                at = slice(o * columns, (o + 1) * columns)
-                top = o * INPUTS
-                wide[top : top + span, at] = sketch_ref[...]
-                if o:
-                    wide[:top, at] = jnp.zeros((top, columns), BF16)
-                wide[top + span :, at] = jnp.zeros((LANES - top, columns), BF16)
-
-        window = ext[:, pl.ds(pl.multiple_of(g * LANES, LANES), reach)]
-        image = jnp.dot(window, wide[...], preferred_element_type=F32)
-        for o in range(group):
-            out_ref[o] = image[:, o * columns : (o + 1) * columns]
-
+                out_ref[g * group + o] = image[:, o * columns : (o + 1) * columns]
+
+    vmem = pl.BlockSpec(memory_space=pltpu.VMEM)
     return pl.pallas_call(
         kernel,
-        grid=(groups,),
-        in_specs=[pl.BlockSpec((rows, width), lambda g: (0, 0))] * n_blocks
-        + [pl.BlockSpec(sketch.shape, lambda g: (0, 0))],
-        out_specs=pl.BlockSpec((group, rows, columns), lambda g: (g, 0, 0)),
-        out_shape=jax.ShapeDtypeStruct((groups * group, rows, columns), F32),
-        scratch_shapes=[
-            pltpu.VMEM((rows, n_blocks * width), BF16),
-            pltpu.VMEM((reach, group * columns), BF16),
+        in_specs=[vmem] * 3,
+        out_specs=[vmem] * 2,
+        out_shape=[
+            jax.ShapeDtypeStruct((groups * group, rows, columns), F32),
+            jax.ShapeDtypeStruct((span + LANES, group * columns), BF16),
         ],
-        compiler_params=pltpu.CompilerParams(vmem_limit_bytes=13 * MIB),
-        cost_estimate=costs(2 * groups * rows * reach * group * columns, 4 * groups * rows * group * columns),
-    )(*blocks, sketch)
+        compiler_params=pltpu.CompilerParams(vmem_limit_bytes=8 * MIB),
+        cost_estimate=costs(2.5e9),
+    )(first, last, sketch)
+
+
+def hankel_middle(middle, wide, ends):
+    rows, width = middle.shape
+    group = LANES // INPUTS
+    groups = width // LANES
+    columns = ends.shape[2]
+
+    def kernel(middle_ref, wide_ref, ends_ref, out_hbm, result, sent):
+        copies = []
+        for g in range(groups):
+            at = slice(width - g * LANES, 2 * width - g * LANES)
+            image = jnp.dot(middle_ref[...], wide_ref[at, :], preferred_element_type=F32)
+            for o in range(group):
+                i = g * group + o
+                result[i] = image[:, o * columns : (o + 1) * columns] + ends_ref[i]
+                copies.append(pltpu.make_async_copy(result.at[i], out_hbm.at[i], sent.at[i]))
+                copies[-1].start()
+        for copy in copies:
+            copy.wait()
+
+    vmem = pl.BlockSpec(memory_space=pltpu.VMEM)
+    return pl.pallas_call(
+        kernel,
+        in_specs=[vmem] * 3,
+        out_specs=pl.BlockSpec(memory_space=pltpu.HBM),
+        out_shape=jax.ShapeDtypeStruct(ends.shape, F32),
+        scratch_shapes=[pltpu.VMEM(ends.shape, F32), pltpu.SemaphoreType.DMA((groups * group,))],
+        compiler_params=pltpu.CompilerParams(vmem_limit_bytes=8 * MIB),
+        cost_estimate=costs(2.5e9),
+    )(middle, wide, ends)
 
 
 def across(a, b):
@@ -206,6 +244,7 @@
     span, columns = sketch.shape
     tiles = len(parts)
     capacity = 2 * half // tiles
+    places = lax.axis_size("tm")
     group = LANES // INPUTS
     pair = 2 * LANES
     groups = span // LANES
@@ -233,6 +272,14 @@
             left[2 * half : 3 * half, :] = even_ref[...]
             right[3 * half :, :] = odd_ref[...]
 
+        @pl.when(spot < 2)
+        def _():
+            left[2 * half : 3 * half, :] = jnp.zeros((half, width), BF16)
+
+        @pl.when(spot >= places - 2)
+        def _():
+            right[3 * half :, :] = jnp.zeros((half, width), BF16)
+
         left[3 * half :, :] = own[half:, :]
         right[2 * half : 3 * half, :] = own[:half, :]
 
@@ -259,10 +306,6 @@
             left[half : 2 * half, :] = left[2 * half : 3 * half, :]
 
         lag[...] = jnp.zeros_like(lag)
-
-        @pl.when(spot < 2)
-        def _():
-            early[...] = jnp.zeros_like(early)
 
         for q in range(width // pair):
             at = slice(q * pair, (q + 1) * pair)
@@ -297,48 +340,59 @@
         for o in range(group):
             moved = strip if o == 0 else jnp.where(lane < o * INPUTS, 0.0, pltpu.roll(strip, o * INPUTS, 1))
             lag[o * INPUTS : (o + 1) * INPUTS, :span] = moved
-        for j in range(groups):
-            full[j * LANES : (j + 1) * LANES, j * LANES :] = lag[:, : span - j * LANES]
-            if j % 2:
-                full[j * LANES : (j + 1) * LANES, (j - 1) * LANES : j * LANES] = jnp.zeros((LANES, LANES), F32)
+        for j in range(1, groups, 2):
+            full[j * LANES : (j + 1) * LANES, (j - 1) * LANES : j * LANES] = jnp.zeros((LANES, LANES), F32)
+
+        @pl.when(spot >= 2)
+        def _():
+            for j in range(groups):
+                full[j * LANES : (j + 1) * LANES, j * LANES :] = lag[:, : span - j * LANES]
 
         @pl.when(spot < 2)
         def _():
             r = lax.broadcasted_iota(jnp.int32, (LANES, LANES), 0) // INPUTS
             c = lax.broadcasted_iota(jnp.int32, (LANES, LANES), 1) // INPUTS
             weight = jnp.where(c > r, 1.0, jnp.where(c == r, 0.5, 0.0))
+            blocks_here = width // LANES
+
+            @pl.when(spot == 0)
+            def _():
+                for j in range(blocks_here, 2 * blocks_here):
+                    at = slice(j * LANES, (j + 1) * LANES)
+                    early[at, j * LANES :] = jnp.zeros((LANES, span - j * LANES), F32)
+
+            @pl.when(spot == 1)
+            def _():
+                for j in range(blocks_here):
+                    at = slice(j * LANES, (j + 1) * LANES)
+                    early[at, j * LANES : width] = jnp.zeros((LANES, width - j * LANES), F32)
+
             for j in range(groups):
                 at = slice(j * LANES, (j + 1) * LANES)
                 early[at, at] = early[at, at] * weight
-                full[at, at] += early[at, at]
-                if j + 1 < groups:
-                    rest = slice((j + 1) * LANES, span)
-                    full[at, rest] += early[at, rest]
+                full[at, j * LANES :] = lag[:, : span - j * LANES] + early[at, j * LANES :]
+            for j in range(1, groups):
+                early[j * LANES : (j + 1) * LANES, j * LANES :] += early[
+                    (j - 1) * LANES : j * LANES, (j - 1) * LANES : span - LANES
+                ]
             by = 1
             while by < group:
                 step = by * INPUTS
+                by *= 2
                 for j in reversed(range(groups)):
                     at = slice(j * LANES, (j + 1) * LANES)
                     if j:
                         source = early[j * LANES - step : (j + 1) * LANES - step, (j - 1) * LANES :]
-                        early[at, j * LANES :] += pltpu.roll(source, step, 1)[:, LANES:]
+                        value = early[at, j * LANES :] + pltpu.roll(source, step, 1)[:, LANES:]
                     else:
-                        source = early[: LANES - step, :]
-                        early[step:LANES, :] += pltpu.roll(source, step, 1)
-                by *= 2
-            by = 1
-            while by < groups:
-                for j in reversed(range(by, groups)):
-                    early[j * LANES : (j + 1) * LANES, j * LANES :] += early[
-                        (j - by) * LANES : (j - by + 1) * LANES, (j - by) * LANES : span - by * LANES
-                    ]
-                by *= 2
-            for j in range(groups):
-                at = slice(j * LANES, (j + 1) * LANES)
-                full[at, at] -= jnp.where(c >= r, early[at, at], 0.0)
-                if j + 1 < groups:
-                    rest = slice((j + 1) * LANES, span)
-                    full[at, rest] -= early[at, rest]
+                        source = jnp.concatenate([jnp.zeros((step, span), F32), early[: LANES - step, :]], axis=0)
+                        value = early[at, :] + pltpu.roll(source, step, 1)
+                    if by < group:
+                        early[at, j * LANES :] = value
+                    else:
+                        full[at, at] -= jnp.where(c >= r, value[:, :LANES], 0.0)
+                        if j + 1 < groups:
+                            full[at, (j + 1) * LANES :] -= value[:, LANES:]
 
         for q in range(span // pair):
             at = slice(q * pair, (q + 1) * pair)
@@ -408,7 +462,7 @@
                 came.append(jnp.stack([crossed(part, axes, flip) for part in piece]))
             else:
                 came.append(crossed(piece, axes, flip))
-        if gate is not None and len(left) == len(bunch):
+        if gate is not None and bunch is rounds[-1]:
             came, gate = lax.optimization_barrier((came, gate))
         for piece in came:
             acc = acc + piece
@@ -422,14 +476,13 @@
     n_tiles = lax.axis_size("sensor")
     width = state_tiles.shape[1]
     steps_here = width // INPUTS
-    probe_row = probe_row[0]
-    parts = pick_rows(state_tiles, probe_cell[0], probe_row)
+    *parts, wanted = pick_rows(state_tiles, probe_cell[0], probe_row[0])
     arrived = [parts[0]] + [crossed(parts[m], ("sensor",), m) for m in range(1, n_tiles)]
     first, second, swap, even_pair, odd_pair = prepare(parts)
     swapped = crossed(swap, ("tm",), 1)
-    even_pair = paired(even_pair, "tm", 2, 0)
-    odd_pair = paired(odd_pair, "tm", 2, 1)
-    own_block = place_rows(probe_row, arrived)
+    odd_pair = paired(odd_pair, 2, 1)
+    even_pair = paired(even_pair, 2, 0)
+    own_block = place_rows(wanted, arrived)
     own_block, first = lax.optimization_barrier((own_block, first))
     next_two = shifted(own_block, "tm", -2)
     scale = 1.0 / math.sqrt(SENS_DEV * n_tiles * steps_here * lax.axis_size("tm"))
@@ -442,9 +495,12 @@
     total = reduce_scatter(total, axes, [[last]])
     total, next_two = lax.optimization_barrier((total, next_two))
     next_one = crossed(jnp.where(lax.rem(place[0], 2) == 0, next_two, own_block), ("tm",), 1)
-    hankel_sketch = hankel_times([own_block, next_one, next_two], sketch)
-    rounds = [list(range(tm_bits - 1, last)), list(range(tm_bits - 1))]
-    column_image, hankel_sketch = reduce_scatter(total, axes, rounds, list(range(last)), hankel_sketch)
+    ends, wide = hankel_ends(own_block, next_two, sketch)
+    left = list(range(last))
+    total, ends = reduce_scatter(total, axes, [list(range(tm_bits - 1, last))], left, ends)
+    hankel_sketch = hankel_middle(next_one, wide, ends)
+    left = list(range(tm_bits - 1))
+    column_image, hankel_sketch = reduce_scatter(total, axes, [left], list(left), hankel_sketch)
     return (hankel_sketch, column_image)
 
 

time: 46.1 us -> 41.4 us (0.90)
  local copies, waits for them, and re-layouts: 3.05 us -> 0.08 us
  waiting for transfers between devices: 9.22 us -> 8.04 us
  starting transfers between devices: 18.7 us -> 18.2 us
    unnamed x10 -> x2, local copies, waits for them, and re-layouts: 2.96 us -> 0.01 us
    ppermute x13, waiting for transfers between devices: 9.21 us -> 7.63 us  [crossed(): return lax.ppermute(x, axes, [(i, i ^ mask) for i in range(count)])]
    ppermute x2, starting transfers between devices: 2.52 us -> 1.92 us  [paired(): return lax.ppermute(x, ('tm', 'sensor'), pairs)]
    pallas_call x2 -> x3, Pallas kernels: 6.94 us -> 7.47 us  [the longest x1 2.81 us: pick_rows(): pl.pallas_call(kernel, in_specs=[pl.BlockSpec(memory_space=pltpu.HBM)] *...]
    pallas_call x1, Pallas kernels: 5.96 us -> 5.46 us  [gram_image(): pl.pallas_call(kernel, in_specs=[smem] + [vmem] * (6 + tiles), out_specs=...]
  transfers between devices with their start and end apart: 16 -> 16, of which waited for: 8 -> 8; matrix products, arithmetic and copies ran while one was open for 0% -> 0% of each run, Pallas kernels for 25% -> 26%
where the time goes in v4:
time: 41.4 us; the launch traced here: 41.2 us
  starting transfers between devices  18.2 us (44%)
  Pallas kernels  13.4 us (32%)
  waiting for transfers between devices  8.04 us (19%)
  between operations  0.78 us (2%)
  other arithmetic  0.7 us (2%)
    ppermute x13, starting transfers between devices, crossed(): return lax.ppermute(x, axes, [(i, i ^ mask) for i in range(count)])  15 us
    ppermute x13, waiting for transfers between devices, crossed(): return lax.ppermute(x, axes, [(i, i ^ mask) for i in range(count)])  7.63 us
    pallas_call x1, Pallas kernels, gram_image(): pl.pallas_call(kernel, in_specs=[smem] + [vmem] * (6 + tiles), out_specs=...  5.46 us
    pallas_call x1, Pallas kernels, pick_rows(): pl.pallas_call(kernel, in_specs=[pl.BlockSpec(memory_space=pltpu.HBM)] *...  2.81 us
    pallas_call x1, Pallas kernels, hankel_middle(): pl.pallas_call(kernel, in_specs=[vmem] * 3, out_specs=pl.BlockSpec(memory...  2.72 us
    pallas_call x1, Pallas kernels, hankel_ends(): pl.pallas_call(kernel, in_specs=[vmem] * 3, out_specs=[vmem] * 2, out_sha...  1.94 us
    ppermute x2, starting transfers between devices, paired(): return lax.ppermute(x, ('tm', 'sensor'), pairs)  1.92 us
    ppermute x1, starting transfers between devices, shifted(): return lax.ppermute(x, axis, pairs)  1.29 us
  transfers between devices with their start and end apart: 16, of which 8 were waited for; matrix products, arithmetic and copies ran while one was open for 0% of the time, Pallas kernels for 26%

profile of v4, /device:TPU:0, one launch (start us, length us, event | category | flops | bytes accessed | tf_op | source)
XLA Modules:
  0.0 41.2 jit_solution(10728788692213788556)
XLA Ops:
  0.6 2.8 %shard_map.59 = (bf16[144,512]{1,0:T(8,128)(2,1)S(1)}, bf16[144,512]{1,0:T(8,128)(2,1)S(1)}, bf16[144,512]{1,0:T(8,128)(2,1)S(1)}, bf16[144,512]{1,0:T(8,128)(2,1)S(1)}, s32[4,128]{1,0:T(4,128)S(1)}) custom-call(s32[4,128]{1,0:T(4,128)} %bitcast.50, s32[4,128]{1,0:T(4,128)} %bitcast.51, bf16[2048,512]{1,0:T(8,128)(2,1)} %state_hbm.1), custom_call_target="tpu_custom_call" | custom-call | flops 1073741824 | bytes 2097152 | tf_op jit(solution)/shard_map/pallas_call | solution.py:89
  3.4 0.5 %collective-permute-start = (bf16[144,512]{1,0:T(8,128)(2,1)S(1)}, bf16[144,512]{1,0:T(8,128)(2,1)S(1)}, u32[]{:S(2)}, u32[]{:S(2)}) collective-permute-start(bf16[144,512]{1,0:T(8,128)(2,1)S(1)} %get-tuple-element.28.refs_1_), channel_id=1, source_target_pairs={{0,1},{1,0},{2,3},{3,2},{4,5},{5,4},{6,7},{7,6},{8,9},{9,8},{10,11... | collective-permute-start | bytes 442376 | tf_op jit(solution)/shard_map/ppermute | solution.py:43
  4.0 2.6 %collective-permute-start.1 = (bf16[144,512]{1,0:T(8,128)(2,1)S(1)}, bf16[144,512]{1,0:T(8,128)(2,1)S(1)}, u32[]{:S(2)}, u32[]{:S(2)}) collective-permute-start(bf16[144,512]{1,0:T(8,128)(2,1)S(1)} %get-tuple-element.29.refs_2_), channel_id=1, source_target_pairs={{0,2},{1,3},{2,0},{3,1},{4,6},{5,7},{6,4},{7,5},{8,10},{9,11},{10,... | collective-permute-start | bytes 442376 | tf_op jit(solution)/shard_map/ppermute | solution.py:43
  6.6 0.1 collective-permute-start.2
  6.6 0.1 shard_map.61
  6.7 1.9 %collective-permute-start.3 = (bf16[256,512]{1,0:T(8,128)(2,1)S(1)}, bf16[256,512]{1,0:T(8,128)(2,1)S(1)}, u32[]{:S(2)}, u32[]{:S(2)}) collective-permute-start(bf16[256,512]{1,0:T(8,128)(2,1)S(1)} %get-tuple-element.34), channel_id=1, source_target_pairs={{0,8},{1,9},{2,10},{3,11},{4,12},{5,13},{6,14},{7,15},{8,0},{9,1},... | collective-permute-start | bytes 786440 | tf_op jit(solution)/shard_map/ppermute | solution.py:38
  8.6 0.1 collective-permute-start.4
  8.7 1.5 %collective-permute-start.5 = (bf16[256,512]{1,0:T(8,128)(2,1)S(1)}, bf16[256,512]{1,0:T(8,128)(2,1)S(1)}, u32[]{:S(2)}, u32[]{:S(2)}) collective-permute-start(bf16[256,512]{1,0:T(8,128)(2,1)S(1)} %get-tuple-element.36), channel_id=1, source_target_pairs={{0,4},{4,0},{8,12},{12,8},{16,20},{20,16},{24,28},{28,24},{1,5},{5... | collective-permute-start | bytes 786440 | tf_op jit(solution)/shard_map/ppermute | solution.py:43
  10.1 1.1 %collective-permute-done.1.refs_2_ = bf16[144,512]{1,0:T(8,128)(2,1)S(1)} collective-permute-done((bf16[144,512]{1,0:T(8,128)(2,1)S(1)}, bf16[144,512]{1,0:T(8,128)(2,1)S(1)}, u32[]{:S(2)}, u32[]{:S(2)}) %collective-permute-start.1) | collective-permute-done | bytes 147488 | tf_op jit(solution)/shard_map/ppermute | solution.py:43
  11.3 2.6 %collective-permute-done.2.refs_3_ = bf16[144,512]{1,0:T(8,128)(2,1)S(1)} collective-permute-done((bf16[144,512]{1,0:T(8,128)(2,1)S(1)}, bf16[144,512]{1,0:T(8,128)(2,1)S(1)}, u32[]{:S(2)}, u32[]{:S(2)}) %collective-permute-start.2) | collective-permute-done | bytes 147488 | tf_op jit(solution)/shard_map/ppermute | solution.py:43
  13.9 0.4 %shard_map.60.first_ref = bf16[256,512]{1,0:T(8,128)(2,1)S(1)} custom-call(s32[4,128]{1,0:T(4,128)S(1)} %get-tuple-element.26.row_ref, bf16[144,512]{1,0:T(8,128)(2,1)S(1)} %get-tuple-element.27.refs_0_, bf16[144,512]{1,0:T(8,128)(2,1)S(1)} %collective-permute-done.refs_1_, bf16[144,512]{1,0:T(8,128)(2,1)S(1)} %collective-permute-done.1.refs_2_, ...), custom_call_target="tpu_custom_call" | custom-call | flops 20000000000 | tf_op jit(solution)/shard_map/pallas_call | solution.py:120
  14.3 1.3 %collective-permute-start.8 = (bf16[256,512]{1,0:T(8,128)(2,1)S(1)}, bf16[256,512]{1,0:T(8,128)(2,1)S(1)}, u32[]{:S(2)}, u32[]{:S(2)}) collective-permute-start(bf16[256,512]{1,0:T(8,128)(2,1)S(1)} %shard_map.60.first_ref), channel_id=1, source_target_pairs={{8,0},{12,4},{16,8},{20,12},{24,16},{28,20},{9,1},{13,5},{17,9},{2... | collective-permute-start | bytes 786440 | tf_op jit(solution)/shard_map/ppermute | solution.py:26
  15.6 0.0 collective-permute-done.3.even_ref
  15.6 1.7 %collective-permute-done.5.swap_ref = bf16[256,512]{1,0:T(8,128)(2,1)S(1)} collective-permute-done((bf16[256,512]{1,0:T(8,128)(2,1)S(1)}, bf16[256,512]{1,0:T(8,128)(2,1)S(1)}, u32[]{:S(2)}, u32[]{:S(2)}) %collective-permute-start.5) | collective-permute-done | bytes 262176 | tf_op jit(solution)/shard_map/ppermute | solution.py:43
  17.3 5.5 %shard_map.62 = f32[1024,128]{1,0:T(8,128)S(1)} custom-call(s32[1]{0:T(128)} %bitcast.place_ref, bf16[256,512]{1,0:T(8,128)(2,1)S(1)} %get-tuple-element.32.first_ref, bf16[256,512]{1,0:T(8,128)(2,1)S(1)} %get-tuple-element.33.second_ref, bf16[256,512]{1,0:T(8,128)(2,1)S(1)} %collective-permute-done.3.even_ref, ...), custom_call_target="tpu_custom_call" | custom-call | flops 5000000000 | tf_op jit(solution)/shard_map/pallas_call | solution.py:416
  22.8 0.1 collective-permute-start.6
  22.9 0.5 %collective-permute-start.7 = (f32[2,2,2,32,128]{4,3,2,1,0:T(8,128)S(1)}, f32[2,2,2,32,128]{4,3,2,1,0:T(8,128)S(1)}, u32[]{:S(2)}, u32[]{:S(2)}) collective-permute-start(f32[2,2,2,32,128]{4,3,2,1,0:T(8,128)S(1)} %get-tuple-element.54), channel_id=1, source_target_pairs={{0,1},{1,0},{2,3},{3,2},{4,5},{5,4},{6,7},{7,6},{8,9},{9,8},{10,11... | collective-permute-start | bytes 393224 | tf_op jit(solution)/shard_map/ppermute | solution.py:43
  23.4 0.8 %collective-permute-done.6 = f32[2,2,2,32,128]{4,3,2,1,0:T(8,128)S(1)} collective-permute-done((f32[2,2,2,32,128]{4,3,2,1,0:T(8,128)S(1)}, f32[2,2,2,32,128]{4,3,2,1,0:T(8,128)S(1)}, u32[]{:S(2)}, u32[]{:S(2)}) %collective-permute-start.6) | collective-permute-done | bytes 131104 | tf_op jit(solution)/shard_map/ppermute | solution.py:43
  24.3 0.2 collective-permute-done.7
  24.5 0.4 collective-permute-done.8.last_ref
  24.9 2.7 %collective-permute-start.11 = (f32[2,2,32,128]{3,2,1,0:T(8,128)S(1)}, f32[2,2,32,128]{3,2,1,0:T(8,128)S(1)}, u32[]{:S(2)}, u32[]{:S(2)}) collective-permute-start(f32[2,2,32,128]{3,2,1,0:T(8,128)S(1)} %get-tuple-element.50), channel_id=1, source_target_pairs={{0,6},{1,7},{2,4},{3,5},{4,2},{5,3},{6,0},{7,1},{8,14},{9,15},{10,... | collective-permute-start | bytes 196616 | tf_op jit(solution)/shard_map/ppermute | solution.py:43
  27.6 0.5 %collective-permute-start.10 = (f32[2,2,32,128]{3,2,1,0:T(8,128)S(1)}, f32[2,2,32,128]{3,2,1,0:T(8,128)S(1)}, u32[]{:S(2)}, u32[]{:S(2)}) collective-permute-start(f32[2,2,32,128]{3,2,1,0:T(8,128)S(1)} %get-tuple-element.51), channel_id=1, source_target_pairs={{0,4},{1,5},{2,6},{3,7},{4,0},{5,1},{6,2},{7,3},{8,12},{9,13},{10,... | collective-permute-start | bytes 196616 | tf_op jit(solution)/shard_map/ppermute | solution.py:43
  28.1 0.4 collective-permute-start.9
  28.5 1.9 %shard_map.63 = (f32[32,256,128]{2,1,0:T(8,128)S(1)}, bf16[1152,1024]{1,0:T(8,128)(2,1)S(1)}) custom-call(bf16[256,512]{1,0:T(8,128)(2,1)S(1)} %shard_map.60.first_ref, bf16[256,512]{1,0:T(8,128)(2,1)S(1)} %collective-permute-done.8.last_ref, bf16[1024,128]{1,0:T(8,128)(2,1)S(1)} %copy-done), custom_call_target="tpu_custom_call" | custom-call | flops 2500000000 | tf_op jit(solution)/shard_map/pallas_call | solution.py:194
  30.4 1.7 %collective-permute-start.15 = (bf16[256,512]{1,0:T(8,128)(2,1)S(1)}, bf16[256,512]{1,0:T(8,128)(2,1)S(1)}, u32[]{:S(2)}, u32[]{:S(2)}) collective-permute-start(bf16[256,512]{1,0:T(8,128)(2,1)S(1)} %broadcast_select_fusion), channel_id=1, source_target_pairs={{0,4},{4,0},{8,12},{12,8},{16,20},{20,16},{24,28},{28,24},{1,5},{5... | collective-permute-start | bytes 786440 | tf_op jit(solution)/shard_map/ppermute | solution.py:43
  32.2 0.2 collective-permute-done.9
  32.4 1.6 %collective-permute-start.14 = (f32[32,128]{1,0:T(8,128)S(1)}, f32[32,128]{1,0:T(8,128)S(1)}, u32[]{:S(2)}, u32[]{:S(2)}) collective-permute-start(f32[32,128]{1,0:T(8,128)S(1)} %get-tuple-element.55), channel_id=1, source_target_pairs={{0,24},{1,25},{2,26},{3,27},{4,28},{5,29},{6,30},{7,31},{8,16},{9,... | collective-permute-start | bytes 49160 | tf_op jit(solution)/shard_map/ppermute | solution.py:43
  34.1 1.5 %collective-permute-start.13 = (f32[32,128]{1,0:T(8,128)S(1)}, f32[32,128]{1,0:T(8,128)S(1)}, u32[]{:S(2)}, u32[]{:S(2)}) collective-permute-start(f32[32,128]{1,0:T(8,128)S(1)} %get-tuple-element.56), channel_id=1, source_target_pairs={{0,16},{1,17},{2,18},{3,19},{4,20},{5,21},{6,22},{7,23},{8,24},{9,... | collective-permute-start | bytes 49160 | tf_op jit(solution)/shard_map/ppermute | solution.py:43
  35.5 1.3 %collective-permute-start.12 = (f32[32,128]{1,0:T(8,128)S(1)}, f32[32,128]{1,0:T(8,128)S(1)}, u32[]{:S(2)}, u32[]{:S(2)}) collective-permute-start(f32[32,128]{1,0:T(8,128)S(1)} %get-tuple-element.57), channel_id=1, source_target_pairs={{0,8},{1,9},{2,10},{3,11},{4,12},{5,13},{6,14},{7,15},{8,0},{9,1},... | collective-permute-start | bytes 49160 | tf_op jit(solution)/shard_map/ppermute | solution.py:43
  36.9 0.9 %collective-permute-done.15.middle_ref = bf16[256,512]{1,0:T(8,128)(2,1)S(1)} collective-permute-done((bf16[256,512]{1,0:T(8,128)(2,1)S(1)}, bf16[256,512]{1,0:T(8,128)(2,1)S(1)}, u32[]{:S(2)}, u32[]{:S(2)}) %collective-permute-start.15) | collective-permute-done | bytes 262176 | tf_op jit(solution)/shard_map/ppermute | solution.py:43
  37.8 2.7 %shard_map.64 = f32[32,256,128]{2,1,0:T(8,128)} custom-call(bf16[256,512]{1,0:T(8,128)(2,1)S(1)} %collective-permute-done.15.middle_ref, bf16[1152,1024]{1,0:T(8,128)(2,1)S(1)} %get-tuple-element.44.wide_ref, f32[32,256,128]{2,1,0:T(8,128)S(1)} %get-tuple-element.45.ends_ref), custom_call_target="tpu_custom_call" | custom-call | flops 2500000000 | tf_op jit(solution)/shard_map/pallas_call | solution.py:227
  40.6 0.6 %fusion.3 = f32[32,128]{1,0:T(8,128)} fusion(f32[32,128]{1,0:T(8,128)S(1)} %collective-permute-done.14, f32[32,128]{1,0:T(8,128)S(1)} %collective-permute-done.13, f32[32,128]{1,0:T(8,128)S(1)} %collective-permute-done.12, f32[4,32,128]{2,1,0:T(8,128)S(1)} %bitcast.47, s32[]{:T(128)S(6)} %select_n.52), kind=kLoop, calls=%fused_computation.13 | loop fusion | flops 12288 | bytes 81924 | tf_op jit(solution)/shard_map/add | solution.py:468
  (16 shorter events, 0.2 us)
Async XLA Ops:
  3.4 5.2 %collective-permute-start = (bf16[144,512]{1,0:T(8,128)(2,1)S(1)}, bf16[144,512]{1,0:T(8,128)(2,1)S(1)}, u32[]{:S(2)}, u32[]{:S(2)}) collective-permute-start(bf16[144,512]{1,0:T(8,128)(2,1)S(1)} %get-tuple-element.28.refs_1_), channel_id=1, source_target_pairs={{0,1},{1,0},{2,3},{3,2},{4,5},{5,4},{6,7},{7,6},{8,9},{9,8},{10,11... | collective-permute-start | bytes 442376 | tf_op jit(solution)/shard_map/ppermute | solution.py:43
  4.0 7.3 %collective-permute-start.1 = (bf16[144,512]{1,0:T(8,128)(2,1)S(1)}, bf16[144,512]{1,0:T(8,128)(2,1)S(1)}, u32[]{:S(2)}, u32[]{:S(2)}) collective-permute-start(bf16[144,512]{1,0:T(8,128)(2,1)S(1)} %get-tuple-element.29.refs_2_), channel_id=1, source_target_pairs={{0,2},{1,3},{2,0},{3,1},{4,6},{5,7},{6,4},{7,5},{8,10},{9,11},{10,... | collective-permute-start | bytes 442376 | tf_op jit(solution)/shard_map/ppermute | solution.py:43
  6.6 7.3 %collective-permute-start.2 = (bf16[144,512]{1,0:T(8,128)(2,1)S(1)}, bf16[144,512]{1,0:T(8,128)(2,1)S(1)}, u32[]{:S(2)}, u32[]{:S(2)}) collective-permute-start(bf16[144,512]{1,0:T(8,128)(2,1)S(1)} %get-tuple-element.30.refs_3_), channel_id=1, source_target_pairs={{0,3},{1,2},{2,1},{3,0},{4,7},{5,6},{6,5},{7,4},{8,11},{9,10},{10,... | collective-permute-start | bytes 442376 | tf_op jit(solution)/shard_map/ppermute | solution.py:43
  6.7 8.9 %collective-permute-start.3 = (bf16[256,512]{1,0:T(8,128)(2,1)S(1)}, bf16[256,512]{1,0:T(8,128)(2,1)S(1)}, u32[]{:S(2)}, u32[]{:S(2)}) collective-permute-start(bf16[256,512]{1,0:T(8,128)(2,1)S(1)} %get-tuple-element.34), channel_id=1, source_target_pairs={{0,8},{1,9},{2,10},{3,11},{4,12},{5,13},{6,14},{7,15},{8,0},{9,1},... | collective-permute-start | bytes 786440 | tf_op jit(solution)/shard_map/ppermute | solution.py:38
  8.6 7.1 %collective-permute-start.4 = (bf16[256,512]{1,0:T(8,128)(2,1)S(1)}, bf16[256,512]{1,0:T(8,128)(2,1)S(1)}, u32[]{:S(2)}, u32[]{:S(2)}) collective-permute-start(bf16[256,512]{1,0:T(8,128)(2,1)S(1)} %get-tuple-element.35), channel_id=1, source_target_pairs={{0,1},{1,0},{2,3},{3,2},{4,5},{5,4},{6,7},{7,6},{8,16},{9,17},{10,... | collective-permute-start | bytes 786440 | tf_op jit(solution)/shard_map/ppermute | solution.py:38
  8.7 8.7 %collective-permute-start.5 = (bf16[256,512]{1,0:T(8,128)(2,1)S(1)}, bf16[256,512]{1,0:T(8,128)(2,1)S(1)}, u32[]{:S(2)}, u32[]{:S(2)}) collective-permute-start(bf16[256,512]{1,0:T(8,128)(2,1)S(1)} %get-tuple-element.36), channel_id=1, source_target_pairs={{0,4},{4,0},{8,12},{12,8},{16,20},{20,16},{24,28},{28,24},{1,5},{5... | collective-permute-start | bytes 786440 | tf_op jit(solution)/shard_map/ppermute | solution.py:43
  13.9 3.4 %copy-start = (bf16[1024,128]{1,0:T(8,128)(2,1)S(1)}, bf16[1024,128]{1,0:T(8,128)(2,1)}, u32[]{:S(2)}) copy-start(bf16[1024,128]{1,0:T(8,128)(2,1)} %sketch_ref.1) | copy-start | bytes 786436
  14.3 10.6 %collective-permute-start.8 = (bf16[256,512]{1,0:T(8,128)(2,1)S(1)}, bf16[256,512]{1,0:T(8,128)(2,1)S(1)}, u32[]{:S(2)}, u32[]{:S(2)}) collective-permute-start(bf16[256,512]{1,0:T(8,128)(2,1)S(1)} %shard_map.60.first_ref), channel_id=1, source_target_pairs={{8,0},{12,4},{16,8},{20,12},{24,16},{28,20},{9,1},{13,5},{17,9},{2... | collective-permute-start | bytes 786440 | tf_op jit(solution)/shard_map/ppermute | solution.py:26
  22.8 1.4 %collective-permute-start.6 = (f32[2,2,2,32,128]{4,3,2,1,0:T(8,128)S(1)}, f32[2,2,2,32,128]{4,3,2,1,0:T(8,128)S(1)}, u32[]{:S(2)}, u32[]{:S(2)}) collective-permute-start(f32[2,2,2,32,128]{4,3,2,1,0:T(8,128)S(1)} %get-tuple-element.53), channel_id=1, source_target_pairs={{0,1},{1,0},{2,3},{3,2},{4,5},{5,4},{6,7},{7,6},{8,9},{9,8},{10,11... | collective-permute-start | bytes 393224 | tf_op jit(solution)/shard_map/ppermute | solution.py:43
  22.9 1.5 %collective-permute-start.7 = (f32[2,2,2,32,128]{4,3,2,1,0:T(8,128)S(1)}, f32[2,2,2,32,128]{4,3,2,1,0:T(8,128)S(1)}, u32[]{:S(2)}, u32[]{:S(2)}) collective-permute-start(f32[2,2,2,32,128]{4,3,2,1,0:T(8,128)S(1)} %get-tuple-element.54), channel_id=1, source_target_pairs={{0,1},{1,0},{2,3},{3,2},{4,5},{5,4},{6,7},{7,6},{8,9},{9,8},{10,11... | collective-permute-start | bytes 393224 | tf_op jit(solution)/shard_map/ppermute | solution.py:43
  24.9 7.2 %collective-permute-start.11 = (f32[2,2,32,128]{3,2,1,0:T(8,128)S(1)}, f32[2,2,32,128]{3,2,1,0:T(8,128)S(1)}, u32[]{:S(2)}, u32[]{:S(2)}) collective-permute-start(f32[2,2,32,128]{3,2,1,0:T(8,128)S(1)} %get-tuple-element.50), channel_id=1, source_target_pairs={{0,6},{1,7},{2,4},{3,5},{4,2},{5,3},{6,0},{7,1},{8,14},{9,15},{10,... | collective-permute-start | bytes 196616 | tf_op jit(solution)/shard_map/ppermute | solution.py:43
  27.6 4.6 %collective-permute-start.10 = (f32[2,2,32,128]{3,2,1,0:T(8,128)S(1)}, f32[2,2,32,128]{3,2,1,0:T(8,128)S(1)}, u32[]{:S(2)}, u32[]{:S(2)}) collective-permute-start(f32[2,2,32,128]{3,2,1,0:T(8,128)S(1)} %get-tuple-element.51), channel_id=1, source_target_pairs={{0,4},{1,5},{2,6},{3,7},{4,0},{5,1},{6,2},{7,3},{8,12},{9,13},{10,... | collective-permute-start | bytes 196616 | tf_op jit(solution)/shard_map/ppermute | solution.py:43
  28.1 4.3 %collective-permute-start.9 = (f32[2,2,32,128]{3,2,1,0:T(8,128)S(1)}, f32[2,2,32,128]{3,2,1,0:T(8,128)S(1)}, u32[]{:S(2)}, u32[]{:S(2)}) collective-permute-start(f32[2,2,32,128]{3,2,1,0:T(8,128)S(1)} %get-tuple-element.52), channel_id=1, source_target_pairs={{0,2},{1,3},{2,0},{3,1},{4,6},{5,7},{6,4},{7,5},{8,10},{9,11},{10,... | collective-permute-start | bytes 196616 | tf_op jit(solution)/shard_map/ppermute | solution.py:43
  30.4 7.4 %collective-permute-start.15 = (bf16[256,512]{1,0:T(8,128)(2,1)S(1)}, bf16[256,512]{1,0:T(8,128)(2,1)S(1)}, u32[]{:S(2)}, u32[]{:S(2)}) collective-permute-start(bf16[256,512]{1,0:T(8,128)(2,1)S(1)} %broadcast_select_fusion), channel_id=1, source_target_pairs={{0,4},{4,0},{8,12},{12,8},{16,20},{20,16},{24,28},{28,24},{1,5},{5... | collective-permute-start | bytes 786440 | tf_op jit(solution)/shard_map/ppermute | solution.py:43
  32.4 8.1 %collective-permute-start.14 = (f32[32,128]{1,0:T(8,128)S(1)}, f32[32,128]{1,0:T(8,128)S(1)}, u32[]{:S(2)}, u32[]{:S(2)}) collective-permute-start(f32[32,128]{1,0:T(8,128)S(1)} %get-tuple-element.55), channel_id=1, source_target_pairs={{0,24},{1,25},{2,26},{3,27},{4,28},{5,29},{6,30},{7,31},{8,16},{9,... | collective-permute-start | bytes 49160 | tf_op jit(solution)/shard_map/ppermute | solution.py:43
  34.1 6.5 %collective-permute-start.13 = (f32[32,128]{1,0:T(8,128)S(1)}, f32[32,128]{1,0:T(8,128)S(1)}, u32[]{:S(2)}, u32[]{:S(2)}) collective-permute-start(f32[32,128]{1,0:T(8,128)S(1)} %get-tuple-element.56), channel_id=1, source_target_pairs={{0,16},{1,17},{2,18},{3,19},{4,20},{5,21},{6,22},{7,23},{8,24},{9,... | collective-permute-start | bytes 49160 | tf_op jit(solution)/shard_map/ppermute | solution.py:43
  35.5 5.0 %collective-permute-start.12 = (f32[32,128]{1,0:T(8,128)S(1)}, f32[32,128]{1,0:T(8,128)S(1)}, u32[]{:S(2)}, u32[]{:S(2)}) collective-permute-start(f32[32,128]{1,0:T(8,128)S(1)} %get-tuple-element.57), channel_id=1, source_target_pairs={{0,8},{1,9},{2,10},{3,11},{4,12},{5,13},{6,14},{7,15},{8,0},{9,1},... | collective-permute-start | bytes 49160 | tf_op jit(solution)/shard_map/ppermute | solution.py:43

commit v5 on v4

--- a/solution.py
+++ b/solution.py
@@ -67,10 +67,13 @@
             line = cell_ref[pl.ds(me ^ m, 1), :]
             slot[m * capacity : (m + 1) * capacity, :] = jnp.broadcast_to(line, (LANES, capacity)).T
         lane = lax.broadcasted_iota(jnp.int32, (rows, LANES), 1)
+        wanted = slot[...]
+        tile = (wanted // LANES).astype(F32).astype(BF16)
+        within = jnp.where(lax.rem(wanted, LANES) == lane, 1.0, 0.0).astype(BF16)
+        none = jnp.zeros_like(within)
         for k in range(steps):
-            wanted = slot[...]
             chosen = jnp.concatenate(
-                [jnp.where(wanted == lane + c, 1.0, 0.0).astype(BF16) for c in range(k * chunk, (k + 1) * chunk, LANES)],
+                [jnp.where(tile == jnp.asarray(c, BF16), within, none) for c in range(k * chunk // LANES, (k + 1) * chunk // LANES)],
                 axis=1,
             )
             copies[2 + k].wait()
@@ -251,7 +254,7 @@
 
     def kernel(place_ref, first_ref, second_ref, even_ref, odd_ref, swap_ref, *refs):
         part_refs = refs[:tiles]
-        sketch_ref, image_ref, own, left, right, lag, early, full, turned = refs[tiles:]
+        sketch_ref, image_ref, own, left, right, lag, start, later, full, turned = refs[tiles:]
         spot = place_ref[0]
         odd = lax.rem(spot, 2)
         for m in range(tiles):
@@ -322,77 +325,98 @@
             lag[:, n + width :] += two[:LANES, : low + LANES]
             lag[:, n + width - LANES :] += two[LANES:, :]
 
-            @pl.when(spot == 0)
-            def _():
-                early[at, low:width] = same
-                early[at, width : 2 * width] = near
-
-            @pl.when(spot == 1)
-            def _():
-                early[width + low : width + low + pair, width + low : 2 * width] = same
-                early[at, width : 2 * width] = near
+            start[at, low:width] = same
+            start[at, width : 2 * width] = near
 
         strip = lag[:INPUTS, :span]
         for o in range(1, group):
             strip += pltpu.roll(lag[o * INPUTS : (o + 1) * INPUTS, :], span + LANES - o * INPUTS, 1)[:, :span]
         lane = lax.broadcasted_iota(jnp.int32, strip.shape, 1)
         strip = jnp.where(lane < INPUTS, 0.5 * strip, strip)
-        for o in range(group):
-            moved = strip if o == 0 else jnp.where(lane < o * INPUTS, 0.0, pltpu.roll(strip, o * INPUTS, 1))
-            lag[o * INPUTS : (o + 1) * INPUTS, :span] = moved
         for j in range(1, groups, 2):
             full[j * LANES : (j + 1) * LANES, (j - 1) * LANES : j * LANES] = jnp.zeros((LANES, LANES), F32)
 
+        tile_lane = lax.broadcasted_iota(jnp.int32, (INPUTS, LANES), 1)
+        half_first = jnp.where(tile_lane < INPUTS, 0.5, 1.0)
+        steps_here = width // INPUTS
+
+        def first_tile(value, change):
+            if value.shape[1] == LANES:
+                return change(value)
+            return jnp.concatenate([change(value[:, :LANES]), value[:, LANES:]], axis=1)
+
+        def place(step):
+            return slice(step * INPUTS, (step + 1) * INPUTS), step // group * LANES, step % group * INPUTS
+
+        def to_columns(steps):
+            for step in steps:
+                rows_of, first_lane, shift = place(step)
+                if shift:
+                    value = pltpu.roll(full[rows_of, first_lane:], shift, 1)
+                    full[rows_of, first_lane:] = first_tile(
+                        value, lambda tile: jnp.where(tile_lane < shift, 0.0, tile)
+                    )
+
+        def to_lags(last):
+            for step in range(steps_here):
+                rows_of, first_lane, shift = place(step)
+                value = start[rows_of, first_lane:last]
+                if shift:
+                    value = pltpu.roll(value, value.shape[1] - shift, 1)
+                start[rows_of, : last - first_lane] = first_tile(value, lambda tile: tile * half_first)
+
         @pl.when(spot >= 2)
         def _():
-            for j in range(groups):
-                full[j * LANES : (j + 1) * LANES, j * LANES :] = lag[:, : span - j * LANES]
-
-        @pl.when(spot < 2)
-        def _():
-            r = lax.broadcasted_iota(jnp.int32, (LANES, LANES), 0) // INPUTS
-            c = lax.broadcasted_iota(jnp.int32, (LANES, LANES), 1) // INPUTS
-            weight = jnp.where(c > r, 1.0, jnp.where(c == r, 0.5, 0.0))
-            blocks_here = width // LANES
-
-            @pl.when(spot == 0)
-            def _():
-                for j in range(blocks_here, 2 * blocks_here):
-                    at = slice(j * LANES, (j + 1) * LANES)
-                    early[at, j * LANES :] = jnp.zeros((LANES, span - j * LANES), F32)
-
-            @pl.when(spot == 1)
-            def _():
-                for j in range(blocks_here):
-                    at = slice(j * LANES, (j + 1) * LANES)
-                    early[at, j * LANES : width] = jnp.zeros((LANES, width - j * LANES), F32)
-
-            for j in range(groups):
-                at = slice(j * LANES, (j + 1) * LANES)
-                early[at, at] = early[at, at] * weight
-                full[at, j * LANES :] = lag[:, : span - j * LANES] + early[at, j * LANES :]
+            for o in range(group):
+                full[o * INPUTS : (o + 1) * INPUTS, :] = strip
+            to_columns(range(group))
             for j in range(1, groups):
-                early[j * LANES : (j + 1) * LANES, j * LANES :] += early[
-                    (j - 1) * LANES : j * LANES, (j - 1) * LANES : span - LANES
-                ]
-            by = 1
-            while by < group:
-                step = by * INPUTS
-                by *= 2
-                for j in reversed(range(groups)):
-                    at = slice(j * LANES, (j + 1) * LANES)
-                    if j:
-                        source = early[j * LANES - step : (j + 1) * LANES - step, (j - 1) * LANES :]
-                        value = early[at, j * LANES :] + pltpu.roll(source, step, 1)[:, LANES:]
-                    else:
-                        source = jnp.concatenate([jnp.zeros((step, span), F32), early[: LANES - step, :]], axis=0)
-                        value = early[at, :] + pltpu.roll(source, step, 1)
-                    if by < group:
-                        early[at, j * LANES :] = value
-                    else:
-                        full[at, at] -= jnp.where(c >= r, value[:, :LANES], 0.0)
-                        if j + 1 < groups:
-                            full[at, (j + 1) * LANES :] -= value[:, LANES:]
+                full[j * LANES : (j + 1) * LANES, j * LANES :] = full[:LANES, : span - j * LANES]
+
+        @pl.when(spot == 0)
+        def _():
+            to_lags(2 * width)
+            rest = strip
+            for step in range(steps_here):
+                rows_of, first_lane, _ = place(step)
+                rest = rest[:, : span - first_lane]
+                full[rows_of, first_lane:] = rest
+                rest -= start[rows_of, : 2 * width - first_lane]
+            rest = rest[:, : span - width]
+            for o in range(group):
+                full[width + o * INPUTS : width + (o + 1) * INPUTS, width:] = rest
+            to_columns(range(steps_here + group))
+            source = slice(width, width + LANES)
+            for j in range(width // LANES + 1, groups):
+                full[j * LANES : (j + 1) * LANES, j * LANES :] = full[source, width : span + width - j * LANES]
+
+        @pl.when(spot == 1)
+        def _():
+            blank = jnp.zeros((INPUTS, LANES), F32)
+            for step in range(steps_here):
+                rows_of, first_lane, shift = place(step)
+                value = start[rows_of, width : 2 * width]
+                if shift:
+                    value = jnp.concatenate([blank, value], axis=1)
+                    value = pltpu.roll(value, value.shape[1] - shift, 1)
+                later[rows_of, : value.shape[1]] = value
+            to_lags(width)
+            rest = strip
+            for step in range(steps_here):
+                rows_of, first_lane, shift = place(step)
+                rest = rest[:, : span - first_lane]
+                full[rows_of, first_lane:] = rest
+                length = width + (LANES if shift else 0)
+                before = span - first_lane - length
+                changed = rest[:, before:] - later[rows_of, :length]
+                rest = jnp.concatenate([rest[:, :before], changed], axis=1) if before else changed
+            rest = rest[:, : span - width]
+            for step in range(steps_here):
+                rows_of, first_lane, _ = place(step)
+                rest = rest[:, : width - first_lane]
+                full[width + step * INPUTS : width + (step + 1) * INPUTS, width + first_lane :] = rest
+                rest -= start[rows_of, : width - first_lane]
+            to_columns(range(2 * steps_here))
 
         for q in range(span // pair):
             at = slice(q * pair, (q + 1) * pair)
@@ -423,7 +447,8 @@
             pltpu.VMEM((4 * half, width), BF16),
             pltpu.VMEM((4 * half, width), BF16),
             pltpu.VMEM((LANES, span + LANES), F32),
-            pltpu.VMEM((span, span), F32),
+            pltpu.VMEM((width, 2 * width), F32),
+            pltpu.VMEM((width, width + LANES), F32),
             pltpu.VMEM((span, span), F32),
             pltpu.VMEM((columns, span), F32),
         ],
@@ -484,7 +509,7 @@
     even_pair = paired(even_pair, 2, 0)
     own_block = place_rows(wanted, arrived)
     own_block, first = lax.optimization_barrier((own_block, first))
-    next_two = shifted(own_block, "tm", -2)
+    ahead = [paired(own_block, 2, odd) for odd in (0, 1)]
     scale = 1.0 / math.sqrt(SENS_DEV * n_tiles * steps_here * lax.axis_size("tm"))
     place = lax.axis_index("tm").astype(jnp.int32).reshape(1)
     total = gram_image(place, first, second, even_pair, odd_pair, swapped, arrived, sketch, scale)
@@ -493,7 +518,9 @@
     last = tm_bits + sensor_bits - 1
     axes = ("tm", "sensor")
     total = reduce_scatter(total, axes, [[last]])
-    total, next_two = lax.optimization_barrier((total, next_two))
+    total, ahead = lax.optimization_barrier((total, ahead))
+    next_two = jnp.where(lax.rem(place[0] // 2, 2) == 0, ahead[0], ahead[1])
+    next_two = jnp.where(place[0] < lax.axis_size("tm") - 2, next_two, 0)
     next_one = crossed(jnp.where(lax.rem(place[0], 2) == 0, next_two, own_block), ("tm",), 1)
     ends, wide = hankel_ends(own_block, next_two, sketch)
     left = list(range(last))

time: 41.4 us -> 39.9 us (0.964)
  Pallas kernels: 13.4 us -> 11.1 us
  starting transfers between devices: 18.2 us -> 20 us
  waiting for transfers between devices: 8.04 us -> 7.14 us
    ppermute x2 -> x4, starting transfers between devices: 1.92 us -> 5.19 us  [paired(): return lax.ppermute(x, ('tm', 'sensor'), pairs)]
    ppermute x13, waiting for transfers between devices: 7.63 us -> 5.5 us  [crossed(): return lax.ppermute(x, axes, [(i, i ^ mask) for i in range(count)])]
    pallas_call x1, Pallas kernels: 5.46 us -> 3.37 us  [gram_image(): pl.pallas_call(kernel, in_specs=[smem] + [vmem] * (6 + tiles), out_specs=...]
    ppermute x2 -> x4, waiting for transfers between devices: 0.01 us -> 1.65 us  [paired(): return lax.ppermute(x, ('tm', 'sensor'), pairs)]
    ppermute x1 -> x0, starting transfers between devices: 1.29 us -> none  [shifted(): return lax.ppermute(x, axis, pairs)]
  transfers between devices with their start and end apart: 16 -> 17, of which waited for: 8 -> 7; matrix products, arithmetic and copies ran while one was open for 0% -> 0% of each run, Pallas kernels for 26% -> 21%
where the time goes in v5:
time: 39.9 us; the launch traced here: 39.8 us
  starting transfers between devices  20 us (50%)
  Pallas kernels  11.1 us (28%)
  waiting for transfers between devices  7.14 us (18%)
  between operations  0.79 us (2%)
  other arithmetic  0.72 us (2%)
    ppermute x13, starting transfers between devices, crossed(): return lax.ppermute(x, axes, [(i, i ^ mask) for i in range(count)])  14.8 us
    ppermute x13, waiting for transfers between devices, crossed(): return lax.ppermute(x, axes, [(i, i ^ mask) for i in range(count)])  5.5 us
    ppermute x4, starting transfers between devices, paired(): return lax.ppermute(x, ('tm', 'sensor'), pairs)  5.19 us
    pallas_call x1, Pallas kernels, gram_image(): pl.pallas_call(kernel, in_specs=[smem] + [vmem] * (6 + tiles), out_specs=...  3.37 us
    pallas_call x1, Pallas kernels, hankel_middle(): pl.pallas_call(kernel, in_specs=[vmem] * 3, out_specs=pl.BlockSpec(memory...  2.72 us
    pallas_call x1, Pallas kernels, pick_rows(): pl.pallas_call(kernel, in_specs=[pl.BlockSpec(memory_space=pltpu.HBM)] *...  2.54 us
    pallas_call x1, Pallas kernels, hankel_ends(): pl.pallas_call(kernel, in_specs=[vmem] * 3, out_specs=[vmem] * 2, out_sha...  1.94 us
    ppermute x4, waiting for transfers between devices, paired(): return lax.ppermute(x, ('tm', 'sensor'), pairs)  1.65 us
  transfers between devices with their start and end apart: 17, of which 7 were waited for; matrix products, arithmetic and copies ran while one was open for 0% of the time, Pallas kernels for 21%

profile of v5, /device:TPU:0, one launch (start us, length us, event | category | flops | bytes accessed | tf_op | source)
XLA Modules:
  0.0 39.8 jit_solution(2095550550674832216)
XLA Ops:
  0.6 2.5 %shard_map.59 = (bf16[144,512]{1,0:T(8,128)(2,1)S(1)}, bf16[144,512]{1,0:T(8,128)(2,1)S(1)}, bf16[144,512]{1,0:T(8,128)(2,1)S(1)}, bf16[144,512]{1,0:T(8,128)(2,1)S(1)}, s32[4,128]{1,0:T(4,128)S(1)}) custom-call(s32[4,128]{1,0:T(4,128)} %bitcast.50, s32[4,128]{1,0:T(4,128)} %bitcast.51, bf16[2048,512]{1,0:T(8,128)(2,1)} %state_hbm.1), custom_call_target="tpu_custom_call" | custom-call | flops 1073741824 | bytes 2097152 | tf_op jit(solution)/shard_map/pallas_call | solution.py:92
  3.2 0.5 %collective-permute-start = (bf16[144,512]{1,0:T(8,128)(2,1)S(1)}, bf16[144,512]{1,0:T(8,128)(2,1)S(1)}, u32[]{:S(2)}, u32[]{:S(2)}) collective-permute-start(bf16[144,512]{1,0:T(8,128)(2,1)S(1)} %get-tuple-element.29.refs_1_), channel_id=1, source_target_pairs={{0,1},{1,0},{2,3},{3,2},{4,5},{5,4},{6,7},{7,6},{8,9},{9,8},{10,11... | collective-permute-start | bytes 442376 | tf_op jit(solution)/shard_map/ppermute | solution.py:43
  3.7 2.6 %collective-permute-start.1 = (bf16[144,512]{1,0:T(8,128)(2,1)S(1)}, bf16[144,512]{1,0:T(8,128)(2,1)S(1)}, u32[]{:S(2)}, u32[]{:S(2)}) collective-permute-start(bf16[144,512]{1,0:T(8,128)(2,1)S(1)} %get-tuple-element.30.refs_2_), channel_id=1, source_target_pairs={{0,2},{1,3},{2,0},{3,1},{4,6},{5,7},{6,4},{7,5},{8,10},{9,11},{10,... | collective-permute-start | bytes 442376 | tf_op jit(solution)/shard_map/ppermute | solution.py:43
  6.3 0.1 collective-permute-start.2
  6.4 0.1 shard_map.61
  6.5 1.9 %collective-permute-start.3 = (bf16[256,512]{1,0:T(8,128)(2,1)S(1)}, bf16[256,512]{1,0:T(8,128)(2,1)S(1)}, u32[]{:S(2)}, u32[]{:S(2)}) collective-permute-start(bf16[256,512]{1,0:T(8,128)(2,1)S(1)} %get-tuple-element.35), channel_id=1, source_target_pairs={{0,8},{1,9},{2,10},{3,11},{4,12},{5,13},{6,14},{7,15},{8,0},{9,1},... | collective-permute-start | bytes 786440 | tf_op jit(solution)/shard_map/ppermute | solution.py:38
  8.3 0.1 collective-permute-start.4
  8.4 0.0 collective-permute-done.refs_1_
  8.4 1.5 %collective-permute-start.5 = (bf16[256,512]{1,0:T(8,128)(2,1)S(1)}, bf16[256,512]{1,0:T(8,128)(2,1)S(1)}, u32[]{:S(2)}, u32[]{:S(2)}) collective-permute-start(bf16[256,512]{1,0:T(8,128)(2,1)S(1)} %get-tuple-element.37), channel_id=1, source_target_pairs={{0,4},{4,0},{8,12},{12,8},{16,20},{20,16},{24,28},{28,24},{1,5},{5... | collective-permute-start | bytes 786440 | tf_op jit(solution)/shard_map/ppermute | solution.py:43
  9.9 1.1 %collective-permute-done.1.refs_2_ = bf16[144,512]{1,0:T(8,128)(2,1)S(1)} collective-permute-done((bf16[144,512]{1,0:T(8,128)(2,1)S(1)}, bf16[144,512]{1,0:T(8,128)(2,1)S(1)}, u32[]{:S(2)}, u32[]{:S(2)}) %collective-permute-start.1) | collective-permute-done | bytes 147488 | tf_op jit(solution)/shard_map/ppermute | solution.py:43
  11.0 2.6 %collective-permute-done.2.refs_3_ = bf16[144,512]{1,0:T(8,128)(2,1)S(1)} collective-permute-done((bf16[144,512]{1,0:T(8,128)(2,1)S(1)}, bf16[144,512]{1,0:T(8,128)(2,1)S(1)}, u32[]{:S(2)}, u32[]{:S(2)}) %collective-permute-start.2) | collective-permute-done | bytes 147488 | tf_op jit(solution)/shard_map/ppermute | solution.py:43
  13.6 0.4 %shard_map.60.first_ref = bf16[256,512]{1,0:T(8,128)(2,1)S(1)} custom-call(s32[4,128]{1,0:T(4,128)S(1)} %get-tuple-element.27.row_ref, bf16[144,512]{1,0:T(8,128)(2,1)S(1)} %get-tuple-element.28.refs_0_, bf16[144,512]{1,0:T(8,128)(2,1)S(1)} %collective-permute-done.refs_1_, bf16[144,512]{1,0:T(8,128)(2,1)S(1)} %collective-permute-done.1.refs_2_, ...), custom_call_target="tpu_custom_call" | custom-call | flops 20000000000 | tf_op jit(solution)/shard_map/pallas_call | solution.py:123
  14.1 0.4 %collective-permute-start.9 = (bf16[256,512]{1,0:T(8,128)(2,1)S(1)}, bf16[256,512]{1,0:T(8,128)(2,1)S(1)}, u32[]{:S(2)}, u32[]{:S(2)}) collective-permute-start(bf16[256,512]{1,0:T(8,128)(2,1)S(1)} %shard_map.60.first_ref), channel_id=1, source_target_pairs={{0,1},{1,0},{2,3},{3,2},{4,5},{5,4},{6,7},{7,6},{8,16},{9,17},{10,... | collective-permute-start | bytes 786440 | tf_op jit(solution)/shard_map/ppermute | solution.py:38
  14.5 2.8 %collective-permute-start.8 = (bf16[256,512]{1,0:T(8,128)(2,1)S(1)}, bf16[256,512]{1,0:T(8,128)(2,1)S(1)}, u32[]{:S(2)}, u32[]{:S(2)}) collective-permute-start(bf16[256,512]{1,0:T(8,128)(2,1)S(1)} %shard_map.60.first_ref), channel_id=1, source_target_pairs={{0,8},{1,9},{2,10},{3,11},{4,12},{5,13},{6,14},{7,15},{8,0},{9,1},... | collective-permute-start | bytes 786440 | tf_op jit(solution)/shard_map/ppermute | solution.py:38
  17.3 3.4 %shard_map.62 = f32[1024,128]{1,0:T(8,128)S(1)} custom-call(s32[1]{0:T(128)} %bitcast.place_ref, bf16[256,512]{1,0:T(8,128)(2,1)S(1)} %get-tuple-element.33.first_ref, bf16[256,512]{1,0:T(8,128)(2,1)S(1)} %get-tuple-element.34.second_ref, bf16[256,512]{1,0:T(8,128)(2,1)S(1)} %collective-permute-done.3.even_ref, ...), custom_call_target="tpu_custom_call" | custom-call | flops 5000000000 | tf_op jit(solution)/shard_map/pallas_call | solution.py:440
  20.8 0.1 collective-permute-start.6
  20.9 0.5 %collective-permute-start.7 = (f32[2,2,2,32,128]{4,3,2,1,0:T(8,128)S(1)}, f32[2,2,2,32,128]{4,3,2,1,0:T(8,128)S(1)}, u32[]{:S(2)}, u32[]{:S(2)}) collective-permute-start(f32[2,2,2,32,128]{4,3,2,1,0:T(8,128)S(1)} %get-tuple-element.58), channel_id=1, source_target_pairs={{0,1},{1,0},{2,3},{3,2},{4,5},{5,4},{6,7},{7,6},{8,9},{9,8},{10,11... | collective-permute-start | bytes 393224 | tf_op jit(solution)/shard_map/ppermute | solution.py:43
  21.4 0.8 %collective-permute-done.6 = f32[2,2,2,32,128]{4,3,2,1,0:T(8,128)S(1)} collective-permute-done((f32[2,2,2,32,128]{4,3,2,1,0:T(8,128)S(1)}, f32[2,2,2,32,128]{4,3,2,1,0:T(8,128)S(1)}, u32[]{:S(2)}, u32[]{:S(2)}) %collective-permute-start.6) | collective-permute-done | bytes 131104 | tf_op jit(solution)/shard_map/ppermute | solution.py:43
  22.2 0.2 collective-permute-done.7
  22.4 1.6 %collective-permute-done.8 = bf16[256,512]{1,0:T(8,128)(2,1)S(1)} collective-permute-done((bf16[256,512]{1,0:T(8,128)(2,1)S(1)}, bf16[256,512]{1,0:T(8,128)(2,1)S(1)}, u32[]{:S(2)}, u32[]{:S(2)}) %collective-permute-start.8) | collective-permute-done | bytes 262176 | tf_op jit(solution)/shard_map/ppermute | solution.py:38
  24.1 2.5 %collective-permute-start.12 = (f32[2,2,32,128]{3,2,1,0:T(8,128)S(1)}, f32[2,2,32,128]{3,2,1,0:T(8,128)S(1)}, u32[]{:S(2)}, u32[]{:S(2)}) collective-permute-start(f32[2,2,32,128]{3,2,1,0:T(8,128)S(1)} %get-tuple-element.54), channel_id=1, source_target_pairs={{0,6},{1,7},{2,4},{3,5},{4,2},{5,3},{6,0},{7,1},{8,14},{9,15},{10,... | collective-permute-start | bytes 196616 | tf_op jit(solution)/shard_map/ppermute | solution.py:43
  26.6 0.5 %collective-permute-start.11 = (f32[2,2,32,128]{3,2,1,0:T(8,128)S(1)}, f32[2,2,32,128]{3,2,1,0:T(8,128)S(1)}, u32[]{:S(2)}, u32[]{:S(2)}) collective-permute-start(f32[2,2,32,128]{3,2,1,0:T(8,128)S(1)} %get-tuple-element.55), channel_id=1, source_target_pairs={{0,4},{1,5},{2,6},{3,7},{4,0},{5,1},{6,2},{7,3},{8,12},{9,13},{10,... | collective-permute-start | bytes 196616 | tf_op jit(solution)/shard_map/ppermute | solution.py:43
  27.1 0.5 %collective-permute-start.10 = (f32[2,2,32,128]{3,2,1,0:T(8,128)S(1)}, f32[2,2,32,128]{3,2,1,0:T(8,128)S(1)}, u32[]{:S(2)}, u32[]{:S(2)}) collective-permute-start(f32[2,2,32,128]{3,2,1,0:T(8,128)S(1)} %get-tuple-element.56), channel_id=1, source_target_pairs={{0,2},{1,3},{2,0},{3,1},{4,6},{5,7},{6,4},{7,5},{8,10},{9,11},{10,... | collective-permute-start | bytes 196616 | tf_op jit(solution)/shard_map/ppermute | solution.py:43
  27.7 1.5 %collective-permute-start.16 = (bf16[256,512]{1,0:T(8,128)(2,1)S(1)}, bf16[256,512]{1,0:T(8,128)(2,1)S(1)}, u32[]{:S(2)}, u32[]{:S(2)}) collective-permute-start(bf16[256,512]{1,0:T(8,128)(2,1)S(1)} %get-tuple-element.52), channel_id=1, source_target_pairs={{0,4},{4,0},{8,12},{12,8},{16,20},{20,16},{24,28},{28,24},{1,5},{5... | collective-permute-start | bytes 786440 | tf_op jit(solution)/shard_map/ppermute | solution.py:43
  29.3 1.9 %shard_map.63 = (f32[32,256,128]{2,1,0:T(8,128)S(1)}, bf16[1152,1024]{1,0:T(8,128)(2,1)S(1)}) custom-call(bf16[256,512]{1,0:T(8,128)(2,1)S(1)} %shard_map.60.first_ref, bf16[256,512]{1,0:T(8,128)(2,1)S(1)} %get-tuple-element.53.last_ref, bf16[1024,128]{1,0:T(8,128)(2,1)S(1)} %copy-done), custom_call_target="tpu_custom_call" | custom-call | flops 2500000000 | tf_op jit(solution)/shard_map/pallas_call | solution.py:197
  31.2 0.4 %collective-permute-done.11 = f32[2,2,32,128]{3,2,1,0:T(8,128)S(1)} collective-permute-done((f32[2,2,32,128]{3,2,1,0:T(8,128)S(1)}, f32[2,2,32,128]{3,2,1,0:T(8,128)S(1)}, u32[]{:S(2)}, u32[]{:S(2)}) %collective-permute-start.11) | collective-permute-done | bytes 65568 | tf_op jit(solution)/shard_map/ppermute | solution.py:43
  31.7 2.6 %collective-permute-start.15 = (f32[32,128]{1,0:T(8,128)S(1)}, f32[32,128]{1,0:T(8,128)S(1)}, u32[]{:S(2)}, u32[]{:S(2)}) collective-permute-start(f32[32,128]{1,0:T(8,128)S(1)} %get-tuple-element.59), channel_id=1, source_target_pairs={{0,24},{1,25},{2,26},{3,27},{4,28},{5,29},{6,30},{7,31},{8,16},{9,... | collective-permute-start | bytes 49160 | tf_op jit(solution)/shard_map/ppermute | solution.py:43
  34.3 0.7 %collective-permute-start.14 = (f32[32,128]{1,0:T(8,128)S(1)}, f32[32,128]{1,0:T(8,128)S(1)}, u32[]{:S(2)}, u32[]{:S(2)}) collective-permute-start(f32[32,128]{1,0:T(8,128)S(1)} %get-tuple-element.60), channel_id=1, source_target_pairs={{0,16},{1,17},{2,18},{3,19},{4,20},{5,21},{6,22},{7,23},{8,24},{9,... | collective-permute-start | bytes 49160 | tf_op jit(solution)/shard_map/ppermute | solution.py:43
  35.0 1.2 %collective-permute-start.13 = (f32[32,128]{1,0:T(8,128)S(1)}, f32[32,128]{1,0:T(8,128)S(1)}, u32[]{:S(2)}, u32[]{:S(2)}) collective-permute-start(f32[32,128]{1,0:T(8,128)S(1)} %get-tuple-element.61), channel_id=1, source_target_pairs={{0,8},{1,9},{2,10},{3,11},{4,12},{5,13},{6,14},{7,15},{8,0},{9,1},... | collective-permute-start | bytes 49160 | tf_op jit(solution)/shard_map/ppermute | solution.py:43
  36.1 0.3 collective-permute-done.16.middle_ref
  36.4 2.7 %shard_map.64 = f32[32,256,128]{2,1,0:T(8,128)} custom-call(bf16[256,512]{1,0:T(8,128)(2,1)S(1)} %collective-permute-done.16.middle_ref, bf16[1152,1024]{1,0:T(8,128)(2,1)S(1)} %get-tuple-element.46.wide_ref, f32[32,256,128]{2,1,0:T(8,128)S(1)} %get-tuple-element.47.ends_ref), custom_call_target="tpu_custom_call" | custom-call | flops 2500000000 | tf_op jit(solution)/shard_map/pallas_call | solution.py:230
  39.2 0.6 %fusion.3 = f32[32,128]{1,0:T(8,128)} fusion(f32[32,128]{1,0:T(8,128)S(1)} %collective-permute-done.15, f32[32,128]{1,0:T(8,128)S(1)} %collective-permute-done.14, f32[32,128]{1,0:T(8,128)S(1)} %collective-permute-done.13, f32[4,32,128]{2,1,0:T(8,128)S(1)} %bitcast.47, s32[]{:T(128)S(6)} %select_n.76), kind=kLoop, calls=%fused_computation.14 | loop fusion | flops 12288 | bytes 81924 | tf_op jit(solution)/shard_map/add | solution.py:493
  (18 shorter events, 0.2 us)
Async XLA Ops:
  3.2 5.2 %collective-permute-start = (bf16[144,512]{1,0:T(8,128)(2,1)S(1)}, bf16[144,512]{1,0:T(8,128)(2,1)S(1)}, u32[]{:S(2)}, u32[]{:S(2)}) collective-permute-start(bf16[144,512]{1,0:T(8,128)(2,1)S(1)} %get-tuple-element.29.refs_1_), channel_id=1, source_target_pairs={{0,1},{1,0},{2,3},{3,2},{4,5},{5,4},{6,7},{7,6},{8,9},{9,8},{10,11... | collective-permute-start | bytes 442376 | tf_op jit(solution)/shard_map/ppermute | solution.py:43
  3.7 7.3 %collective-permute-start.1 = (bf16[144,512]{1,0:T(8,128)(2,1)S(1)}, bf16[144,512]{1,0:T(8,128)(2,1)S(1)}, u32[]{:S(2)}, u32[]{:S(2)}) collective-permute-start(bf16[144,512]{1,0:T(8,128)(2,1)S(1)} %get-tuple-element.30.refs_2_), channel_id=1, source_target_pairs={{0,2},{1,3},{2,0},{3,1},{4,6},{5,7},{6,4},{7,5},{8,10},{9,11},{10,... | collective-permute-start | bytes 442376 | tf_op jit(solution)/shard_map/ppermute | solution.py:43
  6.3 7.3 %collective-permute-start.2 = (bf16[144,512]{1,0:T(8,128)(2,1)S(1)}, bf16[144,512]{1,0:T(8,128)(2,1)S(1)}, u32[]{:S(2)}, u32[]{:S(2)}) collective-permute-start(bf16[144,512]{1,0:T(8,128)(2,1)S(1)} %get-tuple-element.31.refs_3_), channel_id=1, source_target_pairs={{0,3},{1,2},{2,1},{3,0},{4,7},{5,6},{6,5},{7,4},{8,11},{9,10},{10,... | collective-permute-start | bytes 442376 | tf_op jit(solution)/shard_map/ppermute | solution.py:43
  6.5 10.9 %collective-permute-start.3 = (bf16[256,512]{1,0:T(8,128)(2,1)S(1)}, bf16[256,512]{1,0:T(8,128)(2,1)S(1)}, u32[]{:S(2)}, u32[]{:S(2)}) collective-permute-start(bf16[256,512]{1,0:T(8,128)(2,1)S(1)} %get-tuple-element.35), channel_id=1, source_target_pairs={{0,8},{1,9},{2,10},{3,11},{4,12},{5,13},{6,14},{7,15},{8,0},{9,1},... | collective-permute-start | bytes 786440 | tf_op jit(solution)/shard_map/ppermute | solution.py:38
  8.3 9.0 %collective-permute-start.4 = (bf16[256,512]{1,0:T(8,128)(2,1)S(1)}, bf16[256,512]{1,0:T(8,128)(2,1)S(1)}, u32[]{:S(2)}, u32[]{:S(2)}) collective-permute-start(bf16[256,512]{1,0:T(8,128)(2,1)S(1)} %get-tuple-element.36), channel_id=1, source_target_pairs={{0,1},{1,0},{2,3},{3,2},{4,5},{5,4},{6,7},{7,6},{8,16},{9,17},{10,... | collective-permute-start | bytes 786440 | tf_op jit(solution)/shard_map/ppermute | solution.py:38
  8.4 9.0 %collective-permute-start.5 = (bf16[256,512]{1,0:T(8,128)(2,1)S(1)}, bf16[256,512]{1,0:T(8,128)(2,1)S(1)}, u32[]{:S(2)}, u32[]{:S(2)}) collective-permute-start(bf16[256,512]{1,0:T(8,128)(2,1)S(1)} %get-tuple-element.37), channel_id=1, source_target_pairs={{0,4},{4,0},{8,12},{12,8},{16,20},{20,16},{24,28},{28,24},{1,5},{5... | collective-permute-start | bytes 786440 | tf_op jit(solution)/shard_map/ppermute | solution.py:43
  13.6 3.7 %copy-start = (bf16[1024,128]{1,0:T(8,128)(2,1)S(1)}, bf16[1024,128]{1,0:T(8,128)(2,1)}, u32[]{:S(2)}) copy-start(bf16[1024,128]{1,0:T(8,128)(2,1)} %sketch_ref.1) | copy-start | bytes 786436
  14.1 8.4 %collective-permute-start.9 = (bf16[256,512]{1,0:T(8,128)(2,1)S(1)}, bf16[256,512]{1,0:T(8,128)(2,1)S(1)}, u32[]{:S(2)}, u32[]{:S(2)}) collective-permute-start(bf16[256,512]{1,0:T(8,128)(2,1)S(1)} %shard_map.60.first_ref), channel_id=1, source_target_pairs={{0,1},{1,0},{2,3},{3,2},{4,5},{5,4},{6,7},{7,6},{8,16},{9,17},{10,... | collective-permute-start | bytes 786440 | tf_op jit(solution)/shard_map/ppermute | solution.py:38
  14.5 9.6 %collective-permute-start.8 = (bf16[256,512]{1,0:T(8,128)(2,1)S(1)}, bf16[256,512]{1,0:T(8,128)(2,1)S(1)}, u32[]{:S(2)}, u32[]{:S(2)}) collective-permute-start(bf16[256,512]{1,0:T(8,128)(2,1)S(1)} %shard_map.60.first_ref), channel_id=1, source_target_pairs={{0,8},{1,9},{2,10},{3,11},{4,12},{5,13},{6,14},{7,15},{8,0},{9,1},... | collective-permute-start | bytes 786440 | tf_op jit(solution)/shard_map/ppermute | solution.py:38
  20.8 1.4 %collective-permute-start.6 = (f32[2,2,2,32,128]{4,3,2,1,0:T(8,128)S(1)}, f32[2,2,2,32,128]{4,3,2,1,0:T(8,128)S(1)}, u32[]{:S(2)}, u32[]{:S(2)}) collective-permute-start(f32[2,2,2,32,128]{4,3,2,1,0:T(8,128)S(1)} %get-tuple-element.57), channel_id=1, source_target_pairs={{0,1},{1,0},{2,3},{3,2},{4,5},{5,4},{6,7},{7,6},{8,9},{9,8},{10,11... | collective-permute-start | bytes 393224 | tf_op jit(solution)/shard_map/ppermute | solution.py:43
  20.9 1.5 %collective-permute-start.7 = (f32[2,2,2,32,128]{4,3,2,1,0:T(8,128)S(1)}, f32[2,2,2,32,128]{4,3,2,1,0:T(8,128)S(1)}, u32[]{:S(2)}, u32[]{:S(2)}) collective-permute-start(f32[2,2,2,32,128]{4,3,2,1,0:T(8,128)S(1)} %get-tuple-element.58), channel_id=1, source_target_pairs={{0,1},{1,0},{2,3},{3,2},{4,5},{5,4},{6,7},{7,6},{8,9},{9,8},{10,11... | collective-permute-start | bytes 393224 | tf_op jit(solution)/shard_map/ppermute | solution.py:43
  24.1 7.1 %collective-permute-start.12 = (f32[2,2,32,128]{3,2,1,0:T(8,128)S(1)}, f32[2,2,32,128]{3,2,1,0:T(8,128)S(1)}, u32[]{:S(2)}, u32[]{:S(2)}) collective-permute-start(f32[2,2,32,128]{3,2,1,0:T(8,128)S(1)} %get-tuple-element.54), channel_id=1, source_target_pairs={{0,6},{1,7},{2,4},{3,5},{4,2},{5,3},{6,0},{7,1},{8,14},{9,15},{10,... | collective-permute-start | bytes 196616 | tf_op jit(solution)/shard_map/ppermute | solution.py:43
  26.6 5.0 %collective-permute-start.11 = (f32[2,2,32,128]{3,2,1,0:T(8,128)S(1)}, f32[2,2,32,128]{3,2,1,0:T(8,128)S(1)}, u32[]{:S(2)}, u32[]{:S(2)}) collective-permute-start(f32[2,2,32,128]{3,2,1,0:T(8,128)S(1)} %get-tuple-element.55), channel_id=1, source_target_pairs={{0,4},{1,5},{2,6},{3,7},{4,0},{5,1},{6,2},{7,3},{8,12},{9,13},{10,... | collective-permute-start | bytes 196616 | tf_op jit(solution)/shard_map/ppermute | solution.py:43
  27.1 4.5 %collective-permute-start.10 = (f32[2,2,32,128]{3,2,1,0:T(8,128)S(1)}, f32[2,2,32,128]{3,2,1,0:T(8,128)S(1)}, u32[]{:S(2)}, u32[]{:S(2)}) collective-permute-start(f32[2,2,32,128]{3,2,1,0:T(8,128)S(1)} %get-tuple-element.56), channel_id=1, source_target_pairs={{0,2},{1,3},{2,0},{3,1},{4,6},{5,7},{6,4},{7,5},{8,10},{9,11},{10,... | collective-permute-start | bytes 196616 | tf_op jit(solution)/shard_map/ppermute | solution.py:43
  27.7 8.7 %collective-permute-start.16 = (bf16[256,512]{1,0:T(8,128)(2,1)S(1)}, bf16[256,512]{1,0:T(8,128)(2,1)S(1)}, u32[]{:S(2)}, u32[]{:S(2)}) collective-permute-start(bf16[256,512]{1,0:T(8,128)(2,1)S(1)} %get-tuple-element.52), channel_id=1, source_target_pairs={{0,4},{4,0},{8,12},{12,8},{16,20},{20,16},{24,28},{28,24},{1,5},{5... | collective-permute-start | bytes 786440 | tf_op jit(solution)/shard_map/ppermute | solution.py:43
  31.7 7.5 %collective-permute-start.15 = (f32[32,128]{1,0:T(8,128)S(1)}, f32[32,128]{1,0:T(8,128)S(1)}, u32[]{:S(2)}, u32[]{:S(2)}) collective-permute-start(f32[32,128]{1,0:T(8,128)S(1)} %get-tuple-element.59), channel_id=1, source_target_pairs={{0,24},{1,25},{2,26},{3,27},{4,28},{5,29},{6,30},{7,31},{8,16},{9,... | collective-permute-start | bytes 49160 | tf_op jit(solution)/shard_map/ppermute | solution.py:43
  34.3 4.8 %collective-permute-start.14 = (f32[32,128]{1,0:T(8,128)S(1)}, f32[32,128]{1,0:T(8,128)S(1)}, u32[]{:S(2)}, u32[]{:S(2)}) collective-permute-start(f32[32,128]{1,0:T(8,128)S(1)} %get-tuple-element.60), channel_id=1, source_target_pairs={{0,16},{1,17},{2,18},{3,19},{4,20},{5,21},{6,22},{7,23},{8,24},{9,... | collective-permute-start | bytes 49160 | tf_op jit(solution)/shard_map/ppermute | solution.py:43
  35.0 4.2 %collective-permute-start.13 = (f32[32,128]{1,0:T(8,128)S(1)}, f32[32,128]{1,0:T(8,128)S(1)}, u32[]{:S(2)}, u32[]{:S(2)}) collective-permute-start(f32[32,128]{1,0:T(8,128)S(1)} %get-tuple-element.61), channel_id=1, source_target_pairs={{0,8},{1,9},{2,10},{3,11},{4,12},{5,13},{6,14},{7,15},{8,0},{9,1},... | collective-permute-start | bytes 49160 | tf_op jit(solution)/shard_map/ppermute | solution.py:43

commit v6 on v5

--- a/solution.py
+++ b/solution.py
@@ -85,10 +85,15 @@
         got = got.astype(BF16)
         for m in range(tiles):
             parts[m][:capacity, :] = got[m * capacity : (m + 1) * capacity]
-            filled = jnp.broadcast_to(row_ref[pl.ds(me ^ m, 1), :1], (TAIL, width)) >= 0
-            parts[m][capacity:, :] = jnp.where(filled, 1.0, 0.0).astype(BF16)
-
-    shapes = [(capacity + TAIL, width)] * tiles
+            if m % 2 == 0:
+                own, other = [
+                    jnp.broadcast_to(jnp.where(row_ref[pl.ds(me ^ n, 1), :1] >= 0, 1.0, 0.0), (TAIL, width))
+                    for n in (m, m + 1)
+                ]
+                upper_rows = lax.broadcasted_iota(jnp.int32, (TAIL, width), 0) < TAIL // 2
+                parts[m][capacity:, :] = jnp.where(upper_rows, own, other).astype(BF16)
+
+    shapes = [(capacity + (0 if m % 2 else TAIL), width) for m in range(tiles)]
     return pl.pallas_call(
         kernel,
         in_specs=[pl.BlockSpec(memory_space=pltpu.HBM)] * 3,
@@ -130,8 +135,7 @@
 
 def prepare(parts):
     tiles = len(parts)
-    capacity, width = parts[0].shape
-    capacity -= TAIL
+    capacity, width = parts[1].shape
     half = tiles * capacity // 2
 
     def kernel(*refs):
@@ -242,10 +246,10 @@
     return lax.dot_general(a, b, (((0,), (0,)), ((), ())), preferred_element_type=F32)
 
 
-def gram_image(place, first, second, even_pair, odd_pair, swap, parts, sketch, scale):
+def gram_image(place, first, second, even_pair, odd_pair, swap, marked, other, sketch, scale):
     half, width = first.shape
     span, columns = sketch.shape
-    tiles = len(parts)
+    tiles = 2 * len(marked)
     capacity = 2 * half // tiles
     places = lax.axis_size("tm")
     group = LANES // INPUTS
@@ -253,14 +257,23 @@
     groups = span // LANES
 
     def kernel(place_ref, first_ref, second_ref, even_ref, odd_ref, swap_ref, *refs):
-        part_refs = refs[:tiles]
-        sketch_ref, image_ref, own, left, right, lag, start, later, full, turned = refs[tiles:]
+        mark_refs = refs[: tiles // 2]
+        other_ref = refs[tiles // 2]
+        sketch_ref, image_ref, own, left, right, lag, start, later, full, turned = refs[tiles // 2 + 1 :]
         spot = place_ref[0]
         odd = lax.rem(spot, 2)
+
+        def mark_of(m):
+            if m % 2 == 0:
+                return mark_refs[m // 2][capacity : capacity + TAIL, :][:1]
+            at = m // 2 * TAIL
+            row = other_ref[at : at + TAIL, :][TAIL // 2 : TAIL // 2 + 1]
+            return jnp.concatenate([row] * (width // LANES), axis=1)
+
         for m in range(tiles):
             at = slice(m * capacity, (m + 1) * capacity)
             source, base = (first_ref, 0) if m < tiles // 2 else (second_ref, half)
-            keep = part_refs[m][capacity : capacity + TAIL, :][:1]
+            keep = mark_of(m)
             own[at, :] = source[m * capacity - base : (m + 1) * capacity - base, :] * keep
 
         upper = lax.rem(spot // 2, 2)
@@ -290,7 +303,7 @@
         def _():
             for m in range(tiles // 2, tiles):
                 at = slice(m * capacity - half, (m + 1) * capacity - half)
-                keep = part_refs[m][capacity : capacity + TAIL, :][:1]
+                keep = mark_of(m)
                 mine = swap_ref[at, :] * keep
                 right[at, :] = mine
                 left[half + m * capacity - half : half + (m + 1) * capacity - half, :] = mine
@@ -301,7 +314,7 @@
         def _():
             for m in range(tiles // 2):
                 at = slice(m * capacity, (m + 1) * capacity)
-                keep = part_refs[m][capacity : capacity + TAIL, :][:1]
+                keep = mark_of(m)
                 mine = swap_ref[at, :] * keep
                 left[at, :] = mine
                 right[half + m * capacity : half + (m + 1) * capacity, :] = mine
@@ -439,7 +452,7 @@
     smem = pl.BlockSpec(memory_space=pltpu.SMEM)
     return pl.pallas_call(
         kernel,
-        in_specs=[smem] + [vmem] * (6 + tiles),
+        in_specs=[smem] + [vmem] * (7 + tiles // 2),
         out_specs=vmem,
         out_shape=jax.ShapeDtypeStruct((span, columns), F32),
         scratch_shapes=[
@@ -454,7 +467,7 @@
         ],
         compiler_params=pltpu.CompilerParams(vmem_limit_bytes=18 * MIB),
         cost_estimate=costs(5e9),
-    )(place, first, second, even_pair, odd_pair, swap, *parts, sketch)
+    )(place, first, second, even_pair, odd_pair, swap, *marked, other, sketch)
 
 
 def reduce_scatter(total, axes, rounds, left=None, gate=None):
@@ -507,12 +520,15 @@
     swapped = crossed(swap, ("tm",), 1)
     odd_pair = paired(odd_pair, 2, 1)
     even_pair = paired(even_pair, 2, 0)
+    marked = arrived[::2]
+    other = jnp.concatenate([part[-TAIL:, :LANES] for part in marked])
+    other = crossed(other, ("sensor",), 1)
     own_block = place_rows(wanted, arrived)
     own_block, first = lax.optimization_barrier((own_block, first))
     ahead = [paired(own_block, 2, odd) for odd in (0, 1)]
     scale = 1.0 / math.sqrt(SENS_DEV * n_tiles * steps_here * lax.axis_size("tm"))
     place = lax.axis_index("tm").astype(jnp.int32).reshape(1)
-    total = gram_image(place, first, second, even_pair, odd_pair, swapped, arrived, sketch, scale)
+    total = gram_image(place, first, second, even_pair, odd_pair, swapped, marked, other, sketch, scale)
     tm_bits = int(math.log2(lax.axis_size("tm")))
     sensor_bits = int(math.log2(n_tiles))
     last = tm_bits + sensor_bits - 1

time: 39.9 us -> 39.2 us (0.982)
  waiting for transfers between devices: 7.14 us -> 6.19 us
    ppermute x4, waiting for transfers between devices: 1.65 us -> 0.64 us  [paired(): return lax.ppermute(x, ('tm', 'sensor'), pairs)]
    ppermute x13 -> x14, starting transfers between devices: 14.8 us -> 15.1 us  [crossed(): return lax.ppermute(x, axes, [(i, i ^ mask) for i in range(count)])]
    ppermute x13 -> x14, waiting for transfers between devices: 5.5 us -> 5.55 us  [crossed(): return lax.ppermute(x, axes, [(i, i ^ mask) for i in range(count)])]
  transfers between devices with their start and end apart: 17 -> 18, of which waited for: 7 -> 9; matrix products, arithmetic and copies ran while one was open for 0% -> 0% of each run, Pallas kernels for 21% -> 22%
where the time goes in v6:
time: 39.2 us; the launch traced here: 39 us
  starting transfers between devices  20.2 us (52%)
  Pallas kernels  11 us (28%)
  waiting for transfers between devices  6.19 us (16%)
  between operations  0.8 us (2%)
  other arithmetic  0.72 us (2%)
    ppermute x14, starting transfers between devices, crossed(): return lax.ppermute(x, axes, [(i, i ^ mask) for i in range(count)])  15.1 us
    ppermute x14, waiting for transfers between devices, crossed(): return lax.ppermute(x, axes, [(i, i ^ mask) for i in range(count)])  5.55 us
    ppermute x4, starting transfers between devices, paired(): return lax.ppermute(x, ('tm', 'sensor'), pairs)  5.11 us
    pallas_call x1, Pallas kernels, gram_image(): pl.pallas_call(kernel, in_specs=[smem] + [vmem] * (7 + tiles // 2), out_s...  3.36 us
    pallas_call x1, Pallas kernels, hankel_middle(): pl.pallas_call(kernel, in_specs=[vmem] * 3, out_specs=pl.BlockSpec(memory...  2.7 us
    pallas_call x1, Pallas kernels, pick_rows(): pl.pallas_call(kernel, in_specs=[pl.BlockSpec(memory_space=pltpu.HBM)] *...  2.54 us
    pallas_call x1, Pallas kernels, hankel_ends(): pl.pallas_call(kernel, in_specs=[vmem] * 3, out_specs=[vmem] * 2, out_sha...  1.94 us
  transfers between devices with their start and end apart: 18, of which 9 were waited for; matrix products, arithmetic and copies ran while one was open for 0% of the time, Pallas kernels for 22%

profile of v6, /device:TPU:0, one launch (start us, length us, event | category | flops | bytes accessed | tf_op | source)
XLA Modules:
  0.0 39.0 jit_solution(11637777658077217142)
XLA Ops:
  0.6 2.5 %shard_map.59 = (bf16[144,512]{1,0:T(8,128)(2,1)S(1)}, bf16[128,512]{1,0:T(8,128)(2,1)S(1)}, bf16[144,512]{1,0:T(8,128)(2,1)S(1)}, bf16[128,512]{1,0:T(8,128)(2,1)S(1)}, s32[4,128]{1,0:T(4,128)S(1)}) custom-call(s32[4,128]{1,0:T(4,128)} %bitcast.50, s32[4,128]{1,0:T(4,128)} %bitcast.51, bf16[2048,512]{1,0:T(8,128)(2,1)} %state_hbm.1), custom_call_target="tpu_custom_call" | custom-call | flops 1073741824 | bytes 2097152 | tf_op jit(solution)/shard_map/pallas_call | solution.py:97
  3.2 3.0 %collective-permute-start.1 = (bf16[144,512]{1,0:T(8,128)(2,1)S(1)}, bf16[144,512]{1,0:T(8,128)(2,1)S(1)}, u32[]{:S(2)}, u32[]{:S(2)}) collective-permute-start(bf16[144,512]{1,0:T(8,128)(2,1)S(1)} %get-tuple-element.30.refs_2_), channel_id=1, source_target_pairs={{0,2},{1,3},{2,0},{3,1},{4,6},{5,7},{6,4},{7,5},{8,10},{9,11},{10,... | collective-permute-start | bytes 442376 | tf_op jit(solution)/shard_map/ppermute | solution.py:43
  6.2 0.2 collective-permute-start.2
  6.4 0.1 shard_map.61
  6.5 2.1 %collective-permute-start.3 = (bf16[256,512]{1,0:T(8,128)(2,1)S(1)}, bf16[256,512]{1,0:T(8,128)(2,1)S(1)}, u32[]{:S(2)}, u32[]{:S(2)}) collective-permute-start(bf16[256,512]{1,0:T(8,128)(2,1)S(1)} %get-tuple-element.35), channel_id=1, source_target_pairs={{0,8},{1,9},{2,10},{3,11},{4,12},{5,13},{6,14},{7,15},{8,0},{9,1},... | collective-permute-start | bytes 786440 | tf_op jit(solution)/shard_map/ppermute | solution.py:38
  8.6 2.3 %collective-permute-done.1.refs_2_.refs_1_ = bf16[144,512]{1,0:T(8,128)(2,1)S(1)} collective-permute-done((bf16[144,512]{1,0:T(8,128)(2,1)S(1)}, bf16[144,512]{1,0:T(8,128)(2,1)S(1)}, u32[]{:S(2)}, u32[]{:S(2)}) %collective-permute-start.1) | collective-permute-done | bytes 147488 | tf_op jit(solution)/shard_map/ppermute | solution.py:43
  10.9 2.0 %collective-permute-start.5 = (bf16[256,512]{1,0:T(8,128)(2,1)S(1)}, bf16[256,512]{1,0:T(8,128)(2,1)S(1)}, u32[]{:S(2)}, u32[]{:S(2)}) collective-permute-start(bf16[256,512]{1,0:T(8,128)(2,1)S(1)} %get-tuple-element.37), channel_id=1, source_target_pairs={{0,4},{4,0},{8,12},{12,8},{16,20},{20,16},{24,28},{28,24},{1,5},{5... | collective-permute-start | bytes 786440 | tf_op jit(solution)/shard_map/ppermute | solution.py:43
  12.9 0.1 collective-permute-start.6
  13.0 0.4 %shard_map.60.first_ref = bf16[256,512]{1,0:T(8,128)(2,1)S(1)} custom-call(s32[4,128]{1,0:T(4,128)S(1)} %get-tuple-element.27.row_ref, bf16[144,512]{1,0:T(8,128)(2,1)S(1)} %get-tuple-element.28.refs_0_, bf16[128,512]{1,0:T(8,128)(2,1)S(1)} %collective-permute-done.refs_1_, bf16[144,512]{1,0:T(8,128)(2,1)S(1)} %collective-permute-done.1.refs_2_.refs_1_, ...), custom_call_target="tpu_custom_call" | custom-call | flops 20000000000 | tf_op jit(solution)/shard_map/pallas_call | solution.py:128
  13.4 0.5 %collective-permute-start.10 = (bf16[256,512]{1,0:T(8,128)(2,1)S(1)}, bf16[256,512]{1,0:T(8,128)(2,1)S(1)}, u32[]{:S(2)}, u32[]{:S(2)}) collective-permute-start(bf16[256,512]{1,0:T(8,128)(2,1)S(1)} %shard_map.60.first_ref), channel_id=1, source_target_pairs={{0,1},{1,0},{2,3},{3,2},{4,5},{5,4},{6,7},{7,6},{8,16},{9,17},{10,... | collective-permute-start | bytes 786440 | tf_op jit(solution)/shard_map/ppermute | solution.py:38
  13.9 0.2 collective-permute-done.6.refs_2_
  14.1 2.5 %collective-permute-start.9 = (bf16[256,512]{1,0:T(8,128)(2,1)S(1)}, bf16[256,512]{1,0:T(8,128)(2,1)S(1)}, u32[]{:S(2)}, u32[]{:S(2)}) collective-permute-start(bf16[256,512]{1,0:T(8,128)(2,1)S(1)} %shard_map.60.first_ref), channel_id=1, source_target_pairs={{0,8},{1,9},{2,10},{3,11},{4,12},{5,13},{6,14},{7,15},{8,0},{9,1},... | collective-permute-start | bytes 786440 | tf_op jit(solution)/shard_map/ppermute | solution.py:38
  16.6 0.9 %collective-permute-done.5.swap_ref = bf16[256,512]{1,0:T(8,128)(2,1)S(1)} collective-permute-done((bf16[256,512]{1,0:T(8,128)(2,1)S(1)}, bf16[256,512]{1,0:T(8,128)(2,1)S(1)}, u32[]{:S(2)}, u32[]{:S(2)}) %collective-permute-start.5) | collective-permute-done | bytes 262176 | tf_op jit(solution)/shard_map/ppermute | solution.py:43
  17.6 3.4 %shard_map.62 = f32[1024,128]{1,0:T(8,128)S(1)} custom-call(s32[1]{0:T(128)} %bitcast.place_ref, bf16[256,512]{1,0:T(8,128)(2,1)S(1)} %get-tuple-element.33.first_ref, bf16[256,512]{1,0:T(8,128)(2,1)S(1)} %get-tuple-element.34.second_ref, bf16[256,512]{1,0:T(8,128)(2,1)S(1)} %collective-permute-done.3.even_ref, ...), custom_call_target="tpu_custom_call" | custom-call | flops 5000000000 | tf_op jit(solution)/shard_map/pallas_call | solution.py:453
  21.0 0.1 collective-permute-start.7
  21.1 0.5 %collective-permute-start.8 = (f32[2,2,2,32,128]{4,3,2,1,0:T(8,128)S(1)}, f32[2,2,2,32,128]{4,3,2,1,0:T(8,128)S(1)}, u32[]{:S(2)}, u32[]{:S(2)}) collective-permute-start(f32[2,2,2,32,128]{4,3,2,1,0:T(8,128)S(1)} %get-tuple-element.58), channel_id=1, source_target_pairs={{0,1},{1,0},{2,3},{3,2},{4,5},{5,4},{6,7},{7,6},{8,9},{9,8},{10,11... | collective-permute-start | bytes 393224 | tf_op jit(solution)/shard_map/ppermute | solution.py:43
  21.6 0.8 %collective-permute-done.7 = f32[2,2,2,32,128]{4,3,2,1,0:T(8,128)S(1)} collective-permute-done((f32[2,2,2,32,128]{4,3,2,1,0:T(8,128)S(1)}, f32[2,2,2,32,128]{4,3,2,1,0:T(8,128)S(1)}, u32[]{:S(2)}, u32[]{:S(2)}) %collective-permute-start.7) | collective-permute-done | bytes 131104 | tf_op jit(solution)/shard_map/ppermute | solution.py:43
  22.4 0.2 collective-permute-done.8
  22.6 0.6 %collective-permute-done.9 = bf16[256,512]{1,0:T(8,128)(2,1)S(1)} collective-permute-done((bf16[256,512]{1,0:T(8,128)(2,1)S(1)}, bf16[256,512]{1,0:T(8,128)(2,1)S(1)}, u32[]{:S(2)}, u32[]{:S(2)}) %collective-permute-start.9) | collective-permute-done | bytes 262176 | tf_op jit(solution)/shard_map/ppermute | solution.py:38
  23.3 2.2 %collective-permute-start.13 = (f32[2,2,32,128]{3,2,1,0:T(8,128)S(1)}, f32[2,2,32,128]{3,2,1,0:T(8,128)S(1)}, u32[]{:S(2)}, u32[]{:S(2)}) collective-permute-start(f32[2,2,32,128]{3,2,1,0:T(8,128)S(1)} %get-tuple-element.54), channel_id=1, source_target_pairs={{0,6},{1,7},{2,4},{3,5},{4,2},{5,3},{6,0},{7,1},{8,14},{9,15},{10,... | collective-permute-start | bytes 196616 | tf_op jit(solution)/shard_map/ppermute | solution.py:43
  25.5 0.9 %collective-permute-start.12 = (f32[2,2,32,128]{3,2,1,0:T(8,128)S(1)}, f32[2,2,32,128]{3,2,1,0:T(8,128)S(1)}, u32[]{:S(2)}, u32[]{:S(2)}) collective-permute-start(f32[2,2,32,128]{3,2,1,0:T(8,128)S(1)} %get-tuple-element.55), channel_id=1, source_target_pairs={{0,4},{1,5},{2,6},{3,7},{4,0},{5,1},{6,2},{7,3},{8,12},{9,13},{10,... | collective-permute-start | bytes 196616 | tf_op jit(solution)/shard_map/ppermute | solution.py:43
  26.4 0.4 %collective-permute-start.11 = (f32[2,2,32,128]{3,2,1,0:T(8,128)S(1)}, f32[2,2,32,128]{3,2,1,0:T(8,128)S(1)}, u32[]{:S(2)}, u32[]{:S(2)}) collective-permute-start(f32[2,2,32,128]{3,2,1,0:T(8,128)S(1)} %get-tuple-element.56), channel_id=1, source_target_pairs={{0,2},{1,3},{2,0},{3,1},{4,6},{5,7},{6,4},{7,5},{8,10},{9,11},{10,... | collective-permute-start | bytes 196616 | tf_op jit(solution)/shard_map/ppermute | solution.py:43
  26.9 1.2 %collective-permute-start.17 = (bf16[256,512]{1,0:T(8,128)(2,1)S(1)}, bf16[256,512]{1,0:T(8,128)(2,1)S(1)}, u32[]{:S(2)}, u32[]{:S(2)}) collective-permute-start(bf16[256,512]{1,0:T(8,128)(2,1)S(1)} %get-tuple-element.52), channel_id=1, source_target_pairs={{0,4},{4,0},{8,12},{12,8},{16,20},{20,16},{24,28},{28,24},{1,5},{5... | collective-permute-start | bytes 786440 | tf_op jit(solution)/shard_map/ppermute | solution.py:43
  28.1 1.9 %shard_map.63 = (f32[32,256,128]{2,1,0:T(8,128)S(1)}, bf16[1152,1024]{1,0:T(8,128)(2,1)S(1)}) custom-call(bf16[256,512]{1,0:T(8,128)(2,1)S(1)} %shard_map.60.first_ref, bf16[256,512]{1,0:T(8,128)(2,1)S(1)} %get-tuple-element.53.last_ref, bf16[1024,128]{1,0:T(8,128)(2,1)S(1)} %copy-done), custom_call_target="tpu_custom_call" | custom-call | flops 2500000000 | tf_op jit(solution)/shard_map/pallas_call | solution.py:201
  30.1 0.4 %collective-permute-done.12 = f32[2,2,32,128]{3,2,1,0:T(8,128)S(1)} collective-permute-done((f32[2,2,32,128]{3,2,1,0:T(8,128)S(1)}, f32[2,2,32,128]{3,2,1,0:T(8,128)S(1)}, u32[]{:S(2)}, u32[]{:S(2)}) %collective-permute-start.12) | collective-permute-done | bytes 65568 | tf_op jit(solution)/shard_map/ppermute | solution.py:43
  30.5 0.1 collective-permute-done.11
  30.7 2.9 %collective-permute-start.16 = (f32[32,128]{1,0:T(8,128)S(1)}, f32[32,128]{1,0:T(8,128)S(1)}, u32[]{:S(2)}, u32[]{:S(2)}) collective-permute-start(f32[32,128]{1,0:T(8,128)S(1)} %get-tuple-element.59), channel_id=1, source_target_pairs={{0,24},{1,25},{2,26},{3,27},{4,28},{5,29},{6,30},{7,31},{8,16},{9,... | collective-permute-start | bytes 49160 | tf_op jit(solution)/shard_map/ppermute | solution.py:43
  33.6 0.5 %collective-permute-start.15 = (f32[32,128]{1,0:T(8,128)S(1)}, f32[32,128]{1,0:T(8,128)S(1)}, u32[]{:S(2)}, u32[]{:S(2)}) collective-permute-start(f32[32,128]{1,0:T(8,128)S(1)} %get-tuple-element.60), channel_id=1, source_target_pairs={{0,16},{1,17},{2,18},{3,19},{4,20},{5,21},{6,22},{7,23},{8,24},{9,... | collective-permute-start | bytes 49160 | tf_op jit(solution)/shard_map/ppermute | solution.py:43
  34.1 1.1 %collective-permute-start.14 = (f32[32,128]{1,0:T(8,128)S(1)}, f32[32,128]{1,0:T(8,128)S(1)}, u32[]{:S(2)}, u32[]{:S(2)}) collective-permute-start(f32[32,128]{1,0:T(8,128)S(1)} %get-tuple-element.61), channel_id=1, source_target_pairs={{0,8},{1,9},{2,10},{3,11},{4,12},{5,13},{6,14},{7,15},{8,0},{9,1},... | collective-permute-start | bytes 49160 | tf_op jit(solution)/shard_map/ppermute | solution.py:43
  35.2 0.5 %collective-permute-done.17.middle_ref = bf16[256,512]{1,0:T(8,128)(2,1)S(1)} collective-permute-done((bf16[256,512]{1,0:T(8,128)(2,1)S(1)}, bf16[256,512]{1,0:T(8,128)(2,1)S(1)}, u32[]{:S(2)}, u32[]{:S(2)}) %collective-permute-start.17) | collective-permute-done | bytes 262176 | tf_op jit(solution)/shard_map/ppermute | solution.py:43
  35.7 2.7 %shard_map.64 = f32[32,256,128]{2,1,0:T(8,128)} custom-call(bf16[256,512]{1,0:T(8,128)(2,1)S(1)} %collective-permute-done.17.middle_ref, bf16[1152,1024]{1,0:T(8,128)(2,1)S(1)} %get-tuple-element.46.wide_ref, f32[32,256,128]{2,1,0:T(8,128)S(1)} %get-tuple-element.47.ends_ref), custom_call_target="tpu_custom_call" | custom-call | flops 2500000000 | tf_op jit(solution)/shard_map/pallas_call | solution.py:234
  38.4 0.6 %fusion.3 = f32[32,128]{1,0:T(8,128)} fusion(f32[32,128]{1,0:T(8,128)S(1)} %collective-permute-done.16, f32[32,128]{1,0:T(8,128)S(1)} %collective-permute-done.15, f32[32,128]{1,0:T(8,128)S(1)} %collective-permute-done.14, f32[4,32,128]{2,1,0:T(8,128)S(1)} %bitcast.47, s32[]{:T(128)S(6)} %select_n.76), kind=kLoop, calls=%fused_computation.14 | loop fusion | flops 12288 | bytes 81924 | tf_op jit(solution)/shard_map/add | solution.py:506
  (23 shorter events, 0.2 us)
Async XLA Ops:
  3.2 7.7 %collective-permute-start.1 = (bf16[144,512]{1,0:T(8,128)(2,1)S(1)}, bf16[144,512]{1,0:T(8,128)(2,1)S(1)}, u32[]{:S(2)}, u32[]{:S(2)}) collective-permute-start(bf16[144,512]{1,0:T(8,128)(2,1)S(1)} %get-tuple-element.30.refs_2_), channel_id=1, source_target_pairs={{0,2},{1,3},{2,0},{3,1},{4,6},{5,7},{6,4},{7,5},{8,10},{9,11},{10,... | collective-permute-start | bytes 442376 | tf_op jit(solution)/shard_map/ppermute | solution.py:43
  6.2 6.7 %collective-permute-start = (bf16[128,512]{1,0:T(8,128)(2,1)S(1)}, bf16[128,512]{1,0:T(8,128)(2,1)S(1)}, u32[]{:S(2)}, u32[]{:S(2)}) collective-permute-start(bf16[128,512]{1,0:T(8,128)(2,1)S(1)} %get-tuple-element.29.refs_1_), channel_id=1, source_target_pairs={{0,1},{1,0},{2,3},{3,2},{4,5},{5,4},{6,7},{7,6},{8,9},{9,8},{10,11... | collective-permute-start | bytes 393224 | tf_op jit(solution)/shard_map/ppermute | solution.py:43
  6.2 6.7 %collective-permute-start.2 = (bf16[128,512]{1,0:T(8,128)(2,1)S(1)}, bf16[128,512]{1,0:T(8,128)(2,1)S(1)}, u32[]{:S(2)}, u32[]{:S(2)}) collective-permute-start(bf16[128,512]{1,0:T(8,128)(2,1)S(1)} %get-tuple-element.31.refs_3_), channel_id=1, source_target_pairs={{0,3},{1,2},{2,1},{3,0},{4,7},{5,6},{6,5},{7,4},{8,11},{9,10},{10,... | collective-permute-start | bytes 393224 | tf_op jit(solution)/shard_map/ppermute | solution.py:43
  6.5 10.1 %collective-permute-start.3 = (bf16[256,512]{1,0:T(8,128)(2,1)S(1)}, bf16[256,512]{1,0:T(8,128)(2,1)S(1)}, u32[]{:S(2)}, u32[]{:S(2)}) collective-permute-start(bf16[256,512]{1,0:T(8,128)(2,1)S(1)} %get-tuple-element.35), channel_id=1, source_target_pairs={{0,8},{1,9},{2,10},{3,11},{4,12},{5,13},{6,14},{7,15},{8,0},{9,1},... | collective-permute-start | bytes 786440 | tf_op jit(solution)/shard_map/ppermute | solution.py:38
  8.6 8.0 %collective-permute-start.4 = (bf16[256,512]{1,0:T(8,128)(2,1)S(1)}, bf16[256,512]{1,0:T(8,128)(2,1)S(1)}, u32[]{:S(2)}, u32[]{:S(2)}) collective-permute-start(bf16[256,512]{1,0:T(8,128)(2,1)S(1)} %get-tuple-element.36), channel_id=1, source_target_pairs={{0,1},{1,0},{2,3},{3,2},{4,5},{5,4},{6,7},{7,6},{8,16},{9,17},{10,... | collective-permute-start | bytes 786440 | tf_op jit(solution)/shard_map/ppermute | solution.py:38
  10.9 6.7 %collective-permute-start.5 = (bf16[256,512]{1,0:T(8,128)(2,1)S(1)}, bf16[256,512]{1,0:T(8,128)(2,1)S(1)}, u32[]{:S(2)}, u32[]{:S(2)}) collective-permute-start(bf16[256,512]{1,0:T(8,128)(2,1)S(1)} %get-tuple-element.37), channel_id=1, source_target_pairs={{0,4},{4,0},{8,12},{12,8},{16,20},{20,16},{24,28},{28,24},{1,5},{5... | collective-permute-start | bytes 786440 | tf_op jit(solution)/shard_map/ppermute | solution.py:43
  12.9 1.2 %collective-permute-start.6 = (bf16[32,128]{1,0:T(8,128)(2,1)S(1)}, bf16[32,128]{1,0:T(8,128)(2,1)S(1)}, u32[]{:S(2)}, u32[]{:S(2)}) collective-permute-start(bf16[32,128]{1,0:T(8,128)(2,1)S(1)} %pad_maximum_fusion), channel_id=1, source_target_pairs={{0,1},{1,0},{2,3},{3,2},{4,5},{5,4},{6,7},{7,6},{8,9},{9,8},{10,11... | collective-permute-start | bytes 24584 | tf_op jit(solution)/shard_map/ppermute | solution.py:43
  13.0 4.6 %copy-start = (bf16[1024,128]{1,0:T(8,128)(2,1)S(1)}, bf16[1024,128]{1,0:T(8,128)(2,1)}, u32[]{:S(2)}) copy-start(bf16[1024,128]{1,0:T(8,128)(2,1)} %sketch_ref.1) | copy-start | bytes 786436
  13.4 9.2 %collective-permute-start.10 = (bf16[256,512]{1,0:T(8,128)(2,1)S(1)}, bf16[256,512]{1,0:T(8,128)(2,1)S(1)}, u32[]{:S(2)}, u32[]{:S(2)}) collective-permute-start(bf16[256,512]{1,0:T(8,128)(2,1)S(1)} %shard_map.60.first_ref), channel_id=1, source_target_pairs={{0,1},{1,0},{2,3},{3,2},{4,5},{5,4},{6,7},{7,6},{8,16},{9,17},{10,... | collective-permute-start | bytes 786440 | tf_op jit(solution)/shard_map/ppermute | solution.py:38
  14.1 9.2 %collective-permute-start.9 = (bf16[256,512]{1,0:T(8,128)(2,1)S(1)}, bf16[256,512]{1,0:T(8,128)(2,1)S(1)}, u32[]{:S(2)}, u32[]{:S(2)}) collective-permute-start(bf16[256,512]{1,0:T(8,128)(2,1)S(1)} %shard_map.60.first_ref), channel_id=1, source_target_pairs={{0,8},{1,9},{2,10},{3,11},{4,12},{5,13},{6,14},{7,15},{8,0},{9,1},... | collective-permute-start | bytes 786440 | tf_op jit(solution)/shard_map/ppermute | solution.py:38
  21.0 1.4 %collective-permute-start.7 = (f32[2,2,2,32,128]{4,3,2,1,0:T(8,128)S(1)}, f32[2,2,2,32,128]{4,3,2,1,0:T(8,128)S(1)}, u32[]{:S(2)}, u32[]{:S(2)}) collective-permute-start(f32[2,2,2,32,128]{4,3,2,1,0:T(8,128)S(1)} %get-tuple-element.57), channel_id=1, source_target_pairs={{0,1},{1,0},{2,3},{3,2},{4,5},{5,4},{6,7},{7,6},{8,9},{9,8},{10,11... | collective-permute-start | bytes 393224 | tf_op jit(solution)/shard_map/ppermute | solution.py:43
  21.1 1.5 %collective-permute-start.8 = (f32[2,2,2,32,128]{4,3,2,1,0:T(8,128)S(1)}, f32[2,2,2,32,128]{4,3,2,1,0:T(8,128)S(1)}, u32[]{:S(2)}, u32[]{:S(2)}) collective-permute-start(f32[2,2,2,32,128]{4,3,2,1,0:T(8,128)S(1)} %get-tuple-element.58), channel_id=1, source_target_pairs={{0,1},{1,0},{2,3},{3,2},{4,5},{5,4},{6,7},{7,6},{8,9},{9,8},{10,11... | collective-permute-start | bytes 393224 | tf_op jit(solution)/shard_map/ppermute | solution.py:43
  23.3 6.8 %collective-permute-start.13 = (f32[2,2,32,128]{3,2,1,0:T(8,128)S(1)}, f32[2,2,32,128]{3,2,1,0:T(8,128)S(1)}, u32[]{:S(2)}, u32[]{:S(2)}) collective-permute-start(f32[2,2,32,128]{3,2,1,0:T(8,128)S(1)} %get-tuple-element.54), channel_id=1, source_target_pairs={{0,6},{1,7},{2,4},{3,5},{4,2},{5,3},{6,0},{7,1},{8,14},{9,15},{10,... | collective-permute-start | bytes 196616 | tf_op jit(solution)/shard_map/ppermute | solution.py:43
  25.5 5.0 %collective-permute-start.12 = (f32[2,2,32,128]{3,2,1,0:T(8,128)S(1)}, f32[2,2,32,128]{3,2,1,0:T(8,128)S(1)}, u32[]{:S(2)}, u32[]{:S(2)}) collective-permute-start(f32[2,2,32,128]{3,2,1,0:T(8,128)S(1)} %get-tuple-element.55), channel_id=1, source_target_pairs={{0,4},{1,5},{2,6},{3,7},{4,0},{5,1},{6,2},{7,3},{8,12},{9,13},{10,... | collective-permute-start | bytes 196616 | tf_op jit(solution)/shard_map/ppermute | solution.py:43
  26.4 4.3 %collective-permute-start.11 = (f32[2,2,32,128]{3,2,1,0:T(8,128)S(1)}, f32[2,2,32,128]{3,2,1,0:T(8,128)S(1)}, u32[]{:S(2)}, u32[]{:S(2)}) collective-permute-start(f32[2,2,32,128]{3,2,1,0:T(8,128)S(1)} %get-tuple-element.56), channel_id=1, source_target_pairs={{0,2},{1,3},{2,0},{3,1},{4,6},{5,7},{6,4},{7,5},{8,10},{9,11},{10,... | collective-permute-start | bytes 196616 | tf_op jit(solution)/shard_map/ppermute | solution.py:43
  26.9 8.8 %collective-permute-start.17 = (bf16[256,512]{1,0:T(8,128)(2,1)S(1)}, bf16[256,512]{1,0:T(8,128)(2,1)S(1)}, u32[]{:S(2)}, u32[]{:S(2)}) collective-permute-start(bf16[256,512]{1,0:T(8,128)(2,1)S(1)} %get-tuple-element.52), channel_id=1, source_target_pairs={{0,4},{4,0},{8,12},{12,8},{16,20},{20,16},{24,28},{28,24},{1,5},{5... | collective-permute-start | bytes 786440 | tf_op jit(solution)/shard_map/ppermute | solution.py:43
  30.7 7.7 %collective-permute-start.16 = (f32[32,128]{1,0:T(8,128)S(1)}, f32[32,128]{1,0:T(8,128)S(1)}, u32[]{:S(2)}, u32[]{:S(2)}) collective-permute-start(f32[32,128]{1,0:T(8,128)S(1)} %get-tuple-element.59), channel_id=1, source_target_pairs={{0,24},{1,25},{2,26},{3,27},{4,28},{5,29},{6,30},{7,31},{8,16},{9,... | collective-permute-start | bytes 49160 | tf_op jit(solution)/shard_map/ppermute | solution.py:43
  33.6 4.8 %collective-permute-start.15 = (f32[32,128]{1,0:T(8,128)S(1)}, f32[32,128]{1,0:T(8,128)S(1)}, u32[]{:S(2)}, u32[]{:S(2)}) collective-permute-start(f32[32,128]{1,0:T(8,128)S(1)} %get-tuple-element.60), channel_id=1, source_target_pairs={{0,16},{1,17},{2,18},{3,19},{4,20},{5,21},{6,22},{7,23},{8,24},{9,... | collective-permute-start | bytes 49160 | tf_op jit(solution)/shard_map/ppermute | solution.py:43
  34.1 4.3 %collective-permute-start.14 = (f32[32,128]{1,0:T(8,128)S(1)}, f32[32,128]{1,0:T(8,128)S(1)}, u32[]{:S(2)}, u32[]{:S(2)}) collective-permute-start(f32[32,128]{1,0:T(8,128)S(1)} %get-tuple-element.61), channel_id=1, source_target_pairs={{0,8},{1,9},{2,10},{3,11},{4,12},{5,13},{6,14},{7,15},{8,0},{9,1},... | collective-permute-start | bytes 49160 | tf_op jit(solution)/shard_map/ppermute | solution.py:43

commit v7 on v6

--- a/solution.py
+++ b/solution.py
@@ -517,6 +517,7 @@
     *parts, wanted = pick_rows(state_tiles, probe_cell[0], probe_row[0])
     arrived = [parts[0]] + [crossed(parts[m], ("sensor",), m) for m in range(1, n_tiles)]
     first, second, swap, even_pair, odd_pair = prepare(parts)
+    swap, arrived[1] = lax.optimization_barrier((swap, arrived[1]))
     swapped = crossed(swap, ("tm",), 1)
     odd_pair = paired(odd_pair, 2, 1)
     even_pair = paired(even_pair, 2, 0)
@@ -525,7 +526,7 @@
     other = crossed(other, ("sensor",), 1)
     own_block = place_rows(wanted, arrived)
     own_block, first = lax.optimization_barrier((own_block, first))
-    ahead = [paired(own_block, 2, odd) for odd in (0, 1)]
+    ahead = [paired(own_block, 2, odd) for odd in (1, 0)]
     scale = 1.0 / math.sqrt(SENS_DEV * n_tiles * steps_here * lax.axis_size("tm"))
     place = lax.axis_index("tm").astype(jnp.int32).reshape(1)
     total = gram_image(place, first, second, even_pair, odd_pair, swapped, marked, other, sketch, scale)
@@ -535,7 +536,7 @@
     axes = ("tm", "sensor")
     total = reduce_scatter(total, axes, [[last]])
     total, ahead = lax.optimization_barrier((total, ahead))
-    next_two = jnp.where(lax.rem(place[0] // 2, 2) == 0, ahead[0], ahead[1])
+    next_two = jnp.where(lax.rem(place[0] // 2, 2) == 0, ahead[1], ahead[0])
     next_two = jnp.where(place[0] < lax.axis_size("tm") - 2, next_two, 0)
     next_one = crossed(jnp.where(lax.rem(place[0], 2) == 0, next_two, own_block), ("tm",), 1)
     ends, wide = hankel_ends(own_block, next_two, sketch)

time: 39.2 us -> 38.3 us (0.977)
  starting transfers between devices: 20.2 us -> 19.5 us
    ppermute x4, starting transfers between devices: 5.11 us -> 4.5 us  [paired(): return lax.ppermute(x, ('tm', 'sensor'), pairs)]
    ppermute x4, waiting for transfers between devices: 0.64 us -> 0.12 us  [paired(): return lax.ppermute(x, ('tm', 'sensor'), pairs)]
  transfers between devices with their start and end apart: 18 -> 18, of which waited for: 9 -> 8; matrix products, arithmetic and copies ran while one was open for 0% -> 0% of each run, Pallas kernels for 22% -> 22%
where the time goes in v7:
time: 38.3 us; the launch traced here: 38.2 us
  starting transfers between devices  19.5 us (51%)
  Pallas kernels  11.1 us (29%)
  waiting for transfers between devices  6.01 us (16%)
  between operations  0.8 us (2%)
  other arithmetic  0.72 us (2%)
    ppermute x14, starting transfers between devices, crossed(): return lax.ppermute(x, axes, [(i, i ^ mask) for i in range(count)])  15 us
    ppermute x14, waiting for transfers between devices, crossed(): return lax.ppermute(x, axes, [(i, i ^ mask) for i in range(count)])  5.89 us
    ppermute x4, starting transfers between devices, paired(): return lax.ppermute(x, ('tm', 'sensor'), pairs)  4.5 us
    pallas_call x1, Pallas kernels, gram_image(): pl.pallas_call(kernel, in_specs=[smem] + [vmem] * (7 + tiles // 2), out_s...  3.36 us
    pallas_call x1, Pallas kernels, hankel_middle(): pl.pallas_call(kernel, in_specs=[vmem] * 3, out_specs=pl.BlockSpec(memory...  2.71 us
    pallas_call x1, Pallas kernels, pick_rows(): pl.pallas_call(kernel, in_specs=[pl.BlockSpec(memory_space=pltpu.HBM)] *...  2.54 us
    pallas_call x1, Pallas kernels, hankel_ends(): pl.pallas_call(kernel, in_specs=[vmem] * 3, out_specs=[vmem] * 2, out_sha...  1.94 us
  transfers between devices with their start and end apart: 18, of which 8 were waited for; matrix products, arithmetic and copies ran while one was open for 0% of the time, Pallas kernels for 22%

profile of v7, /device:TPU:0, one launch (start us, length us, event | category | flops | bytes accessed | tf_op | source)
XLA Modules:
  0.0 38.2 jit_solution(13616766952426930295)
XLA Ops:
  0.6 2.5 %shard_map.59 = (bf16[144,512]{1,0:T(8,128)(2,1)S(1)}, bf16[128,512]{1,0:T(8,128)(2,1)S(1)}, bf16[144,512]{1,0:T(8,128)(2,1)S(1)}, bf16[128,512]{1,0:T(8,128)(2,1)S(1)}, s32[4,128]{1,0:T(4,128)S(1)}) custom-call(s32[4,128]{1,0:T(4,128)} %bitcast.50, s32[4,128]{1,0:T(4,128)} %bitcast.51, bf16[2048,512]{1,0:T(8,128)(2,1)} %state_hbm.1), custom_call_target="tpu_custom_call" | custom-call | flops 1073741824 | bytes 2097152 | tf_op jit(solution)/shard_map/pallas_call | solution.py:97
  3.2 3.0 %collective-permute-start.1 = (bf16[144,512]{1,0:T(8,128)(2,1)S(1)}, bf16[144,512]{1,0:T(8,128)(2,1)S(1)}, u32[]{:S(2)}, u32[]{:S(2)}) collective-permute-start(bf16[144,512]{1,0:T(8,128)(2,1)S(1)} %get-tuple-element.32.refs_2_), channel_id=1, source_target_pairs={{0,2},{1,3},{2,0},{3,1},{4,6},{5,7},{6,4},{7,5},{8,10},{9,11},{10,... | collective-permute-start | bytes 442376 | tf_op jit(solution)/shard_map/ppermute | solution.py:43
  6.2 0.0 collective-permute-start
  6.2 0.2 collective-permute-start.2
  6.4 0.1 shard_map.60
  6.5 2.1 %collective-permute-start.3 = (bf16[256,512]{1,0:T(8,128)(2,1)S(1)}, bf16[256,512]{1,0:T(8,128)(2,1)S(1)}, u32[]{:S(2)}, u32[]{:S(2)}) collective-permute-start(bf16[256,512]{1,0:T(8,128)(2,1)S(1)} %get-tuple-element.39), channel_id=1, source_target_pairs={{0,8},{1,9},{2,10},{3,11},{4,12},{5,13},{6,14},{7,15},{8,0},{9,1},... | collective-permute-start | bytes 786440 | tf_op jit(solution)/shard_map/ppermute | solution.py:38
  8.6 0.0 collective-permute-start.4
  8.6 1.6 %collective-permute-start.5 = (bf16[256,512]{1,0:T(8,128)(2,1)S(1)}, bf16[256,512]{1,0:T(8,128)(2,1)S(1)}, u32[]{:S(2)}, u32[]{:S(2)}) collective-permute-start(bf16[256,512]{1,0:T(8,128)(2,1)S(1)} %get-tuple-element.41), channel_id=1, source_target_pairs={{0,4},{4,0},{8,12},{12,8},{16,20},{20,16},{24,28},{28,24},{1,5},{5... | collective-permute-start | bytes 786440 | tf_op jit(solution)/shard_map/ppermute | solution.py:43
  10.1 0.7 %collective-permute-done.1.refs_2_.refs_1_ = bf16[144,512]{1,0:T(8,128)(2,1)S(1)} collective-permute-done((bf16[144,512]{1,0:T(8,128)(2,1)S(1)}, bf16[144,512]{1,0:T(8,128)(2,1)S(1)}, u32[]{:S(2)}, u32[]{:S(2)}) %collective-permute-start.1) | collective-permute-done | bytes 147488 | tf_op jit(solution)/shard_map/ppermute | solution.py:43
  10.9 1.2 %collective-permute-done.2.refs_3_ = bf16[128,512]{1,0:T(8,128)(2,1)S(1)} collective-permute-done((bf16[128,512]{1,0:T(8,128)(2,1)S(1)}, bf16[128,512]{1,0:T(8,128)(2,1)S(1)}, u32[]{:S(2)}, u32[]{:S(2)}) %collective-permute-start.2) | collective-permute-done | bytes 131104 | tf_op jit(solution)/shard_map/ppermute | solution.py:43
  12.1 0.4 %shard_map.61.first_ref = bf16[256,512]{1,0:T(8,128)(2,1)S(1)} custom-call(s32[4,128]{1,0:T(4,128)S(1)} %get-tuple-element.29.row_ref, bf16[144,512]{1,0:T(8,128)(2,1)S(1)} %get-tuple-element.30.refs_0_, bf16[128,512]{1,0:T(8,128)(2,1)S(1)} %collective-permute-done.refs_1_, bf16[144,512]{1,0:T(8,128)(2,1)S(1)} %collective-permute-done.1.refs_2_.refs_1_, ...), custom_call_target="tpu_custom_call" | custom-call | flops 20000000000 | tf_op jit(solution)/shard_map/pallas_call | solution.py:128
  12.5 1.6 %collective-permute-start.10 = (bf16[256,512]{1,0:T(8,128)(2,1)S(1)}, bf16[256,512]{1,0:T(8,128)(2,1)S(1)}, u32[]{:S(2)}, u32[]{:S(2)}) collective-permute-start(bf16[256,512]{1,0:T(8,128)(2,1)S(1)} %shard_map.61.first_ref), channel_id=1, source_target_pairs={{0,8},{1,9},{2,10},{3,11},{4,12},{5,13},{6,14},{7,15},{8,0},{9,1},... | collective-permute-start | bytes 786440 | tf_op jit(solution)/shard_map/ppermute | solution.py:38
  14.2 0.8 %collective-permute-start.9 = (bf16[256,512]{1,0:T(8,128)(2,1)S(1)}, bf16[256,512]{1,0:T(8,128)(2,1)S(1)}, u32[]{:S(2)}, u32[]{:S(2)}) collective-permute-start(bf16[256,512]{1,0:T(8,128)(2,1)S(1)} %shard_map.61.first_ref), channel_id=1, source_target_pairs={{0,1},{1,0},{2,3},{3,2},{4,5},{5,4},{6,7},{7,6},{8,16},{9,17},{10,... | collective-permute-start | bytes 786440 | tf_op jit(solution)/shard_map/ppermute | solution.py:38
  15.0 0.1 collective-permute-done.3.even_ref
  15.1 2.2 %collective-permute-done.5.swap_ref = bf16[256,512]{1,0:T(8,128)(2,1)S(1)} collective-permute-done((bf16[256,512]{1,0:T(8,128)(2,1)S(1)}, bf16[256,512]{1,0:T(8,128)(2,1)S(1)}, u32[]{:S(2)}, u32[]{:S(2)}) %collective-permute-start.5) | collective-permute-done | bytes 262176 | tf_op jit(solution)/shard_map/ppermute | solution.py:43
  17.3 3.4 %shard_map.62 = f32[1024,128]{1,0:T(8,128)S(1)} custom-call(s32[1]{0:T(128)} %bitcast.place_ref, bf16[256,512]{1,0:T(8,128)(2,1)S(1)} %get-tuple-element.37.first_ref, bf16[256,512]{1,0:T(8,128)(2,1)S(1)} %get-tuple-element.38.second_ref, bf16[256,512]{1,0:T(8,128)(2,1)S(1)} %collective-permute-done.3.even_ref, ...), custom_call_target="tpu_custom_call" | custom-call | flops 5000000000 | tf_op jit(solution)/shard_map/pallas_call | solution.py:453
  20.7 0.1 collective-permute-start.7
  20.8 0.5 %collective-permute-start.8 = (f32[2,2,2,32,128]{4,3,2,1,0:T(8,128)S(1)}, f32[2,2,2,32,128]{4,3,2,1,0:T(8,128)S(1)}, u32[]{:S(2)}, u32[]{:S(2)}) collective-permute-start(f32[2,2,2,32,128]{4,3,2,1,0:T(8,128)S(1)} %get-tuple-element.62), channel_id=1, source_target_pairs={{0,1},{1,0},{2,3},{3,2},{4,5},{5,4},{6,7},{7,6},{8,9},{9,8},{10,11... | collective-permute-start | bytes 393224 | tf_op jit(solution)/shard_map/ppermute | solution.py:43
  21.3 0.8 %collective-permute-done.7 = f32[2,2,2,32,128]{4,3,2,1,0:T(8,128)S(1)} collective-permute-done((f32[2,2,2,32,128]{4,3,2,1,0:T(8,128)S(1)}, f32[2,2,2,32,128]{4,3,2,1,0:T(8,128)S(1)}, u32[]{:S(2)}, u32[]{:S(2)}) %collective-permute-start.7) | collective-permute-done | bytes 131104 | tf_op jit(solution)/shard_map/ppermute | solution.py:43
  22.2 0.2 collective-permute-done.8
  22.4 2.6 %collective-permute-start.13 = (f32[2,2,32,128]{3,2,1,0:T(8,128)S(1)}, f32[2,2,32,128]{3,2,1,0:T(8,128)S(1)}, u32[]{:S(2)}, u32[]{:S(2)}) collective-permute-start(f32[2,2,32,128]{3,2,1,0:T(8,128)S(1)} %get-tuple-element.58), channel_id=1, source_target_pairs={{0,6},{1,7},{2,4},{3,5},{4,2},{5,3},{6,0},{7,1},{8,14},{9,15},{10,... | collective-permute-start | bytes 196616 | tf_op jit(solution)/shard_map/ppermute | solution.py:43
  25.0 0.5 %collective-permute-start.12 = (f32[2,2,32,128]{3,2,1,0:T(8,128)S(1)}, f32[2,2,32,128]{3,2,1,0:T(8,128)S(1)}, u32[]{:S(2)}, u32[]{:S(2)}) collective-permute-start(f32[2,2,32,128]{3,2,1,0:T(8,128)S(1)} %get-tuple-element.59), channel_id=1, source_target_pairs={{0,4},{1,5},{2,6},{3,7},{4,0},{5,1},{6,2},{7,3},{8,12},{9,13},{10,... | collective-permute-start | bytes 196616 | tf_op jit(solution)/shard_map/ppermute | solution.py:43
  25.5 0.5 %collective-permute-start.11 = (f32[2,2,32,128]{3,2,1,0:T(8,128)S(1)}, f32[2,2,32,128]{3,2,1,0:T(8,128)S(1)}, u32[]{:S(2)}, u32[]{:S(2)}) collective-permute-start(f32[2,2,32,128]{3,2,1,0:T(8,128)S(1)} %get-tuple-element.60), channel_id=1, source_target_pairs={{0,2},{1,3},{2,0},{3,1},{4,6},{5,7},{6,4},{7,5},{8,10},{9,11},{10,... | collective-permute-start | bytes 196616 | tf_op jit(solution)/shard_map/ppermute | solution.py:43
  26.0 1.6 %collective-permute-start.17 = (bf16[256,512]{1,0:T(8,128)(2,1)S(1)}, bf16[256,512]{1,0:T(8,128)(2,1)S(1)}, u32[]{:S(2)}, u32[]{:S(2)}) collective-permute-start(bf16[256,512]{1,0:T(8,128)(2,1)S(1)} %get-tuple-element.56), channel_id=1, source_target_pairs={{0,4},{4,0},{8,12},{12,8},{16,20},{20,16},{24,28},{28,24},{1,5},{5... | collective-permute-start | bytes 786440 | tf_op jit(solution)/shard_map/ppermute | solution.py:43
  27.7 1.9 %shard_map.63 = (f32[32,256,128]{2,1,0:T(8,128)S(1)}, bf16[1152,1024]{1,0:T(8,128)(2,1)S(1)}) custom-call(bf16[256,512]{1,0:T(8,128)(2,1)S(1)} %shard_map.61.first_ref, bf16[256,512]{1,0:T(8,128)(2,1)S(1)} %get-tuple-element.57.last_ref, bf16[1024,128]{1,0:T(8,128)(2,1)S(1)} %copy-done), custom_call_target="tpu_custom_call" | custom-call | flops 2500000000 | tf_op jit(solution)/shard_map/pallas_call | solution.py:201
  29.6 0.4 collective-permute-done.12
  30.0 2.5 %collective-permute-start.16 = (f32[32,128]{1,0:T(8,128)S(1)}, f32[32,128]{1,0:T(8,128)S(1)}, u32[]{:S(2)}, u32[]{:S(2)}) collective-permute-start(f32[32,128]{1,0:T(8,128)S(1)} %get-tuple-element.63), channel_id=1, source_target_pairs={{0,24},{1,25},{2,26},{3,27},{4,28},{5,29},{6,30},{7,31},{8,16},{9,... | collective-permute-start | bytes 49160 | tf_op jit(solution)/shard_map/ppermute | solution.py:43
  32.6 0.9 %collective-permute-start.15 = (f32[32,128]{1,0:T(8,128)S(1)}, f32[32,128]{1,0:T(8,128)S(1)}, u32[]{:S(2)}, u32[]{:S(2)}) collective-permute-start(f32[32,128]{1,0:T(8,128)S(1)} %get-tuple-element.64), channel_id=1, source_target_pairs={{0,16},{1,17},{2,18},{3,19},{4,20},{5,21},{6,22},{7,23},{8,24},{9,... | collective-permute-start | bytes 49160 | tf_op jit(solution)/shard_map/ppermute | solution.py:43
  33.5 1.0 %collective-permute-start.14 = (f32[32,128]{1,0:T(8,128)S(1)}, f32[32,128]{1,0:T(8,128)S(1)}, u32[]{:S(2)}, u32[]{:S(2)}) collective-permute-start(f32[32,128]{1,0:T(8,128)S(1)} %get-tuple-element.65), channel_id=1, source_target_pairs={{0,8},{1,9},{2,10},{3,11},{4,12},{5,13},{6,14},{7,15},{8,0},{9,1},... | collective-permute-start | bytes 49160 | tf_op jit(solution)/shard_map/ppermute | solution.py:43
  34.5 0.3 collective-permute-done.17.middle_ref
  34.8 2.7 %shard_map.64 = f32[32,256,128]{2,1,0:T(8,128)} custom-call(bf16[256,512]{1,0:T(8,128)(2,1)S(1)} %collective-permute-done.17.middle_ref, bf16[1152,1024]{1,0:T(8,128)(2,1)S(1)} %get-tuple-element.50.wide_ref, f32[32,256,128]{2,1,0:T(8,128)S(1)} %get-tuple-element.51.ends_ref), custom_call_target="tpu_custom_call" | custom-call | flops 2500000000 | tf_op jit(solution)/shard_map/pallas_call | solution.py:234
  37.6 0.6 %fusion.3 = f32[32,128]{1,0:T(8,128)} fusion(f32[32,128]{1,0:T(8,128)S(1)} %collective-permute-done.16, f32[32,128]{1,0:T(8,128)S(1)} %collective-permute-done.15, f32[32,128]{1,0:T(8,128)S(1)} %collective-permute-done.14, f32[4,32,128]{2,1,0:T(8,128)S(1)} %bitcast.47, s32[]{:T(128)S(6)} %select_n.76), kind=kLoop, calls=%fused_computation.14 | loop fusion | flops 12288 | bytes 81924 | tf_op jit(solution)/shard_map/add | solution.py:506
  (23 shorter events, 0.2 us)
Async XLA Ops:
  3.2 7.7 %collective-permute-start.1 = (bf16[144,512]{1,0:T(8,128)(2,1)S(1)}, bf16[144,512]{1,0:T(8,128)(2,1)S(1)}, u32[]{:S(2)}, u32[]{:S(2)}) collective-permute-start(bf16[144,512]{1,0:T(8,128)(2,1)S(1)} %get-tuple-element.32.refs_2_), channel_id=1, source_target_pairs={{0,2},{1,3},{2,0},{3,1},{4,6},{5,7},{6,4},{7,5},{8,10},{9,11},{10,... | collective-permute-start | bytes 442376 | tf_op jit(solution)/shard_map/ppermute | solution.py:43
  6.2 2.4 %collective-permute-start = (bf16[128,512]{1,0:T(8,128)(2,1)S(1)}, bf16[128,512]{1,0:T(8,128)(2,1)S(1)}, u32[]{:S(2)}, u32[]{:S(2)}) collective-permute-start(bf16[128,512]{1,0:T(8,128)(2,1)S(1)} %get-tuple-element.31.refs_1_), channel_id=1, source_target_pairs={{0,1},{1,0},{2,3},{3,2},{4,5},{5,4},{6,7},{7,6},{8,9},{9,8},{10,11... | collective-permute-start | bytes 393224 | tf_op jit(solution)/shard_map/ppermute | solution.py:43
  6.2 5.9 %collective-permute-start.2 = (bf16[128,512]{1,0:T(8,128)(2,1)S(1)}, bf16[128,512]{1,0:T(8,128)(2,1)S(1)}, u32[]{:S(2)}, u32[]{:S(2)}) collective-permute-start(bf16[128,512]{1,0:T(8,128)(2,1)S(1)} %get-tuple-element.33.refs_3_), channel_id=1, source_target_pairs={{0,3},{1,2},{2,1},{3,0},{4,7},{5,6},{6,5},{7,4},{8,11},{9,10},{10,... | collective-permute-start | bytes 393224 | tf_op jit(solution)/shard_map/ppermute | solution.py:43
  6.5 8.6 %collective-permute-start.3 = (bf16[256,512]{1,0:T(8,128)(2,1)S(1)}, bf16[256,512]{1,0:T(8,128)(2,1)S(1)}, u32[]{:S(2)}, u32[]{:S(2)}) collective-permute-start(bf16[256,512]{1,0:T(8,128)(2,1)S(1)} %get-tuple-element.39), channel_id=1, source_target_pairs={{0,8},{1,9},{2,10},{3,11},{4,12},{5,13},{6,14},{7,15},{8,0},{9,1},... | collective-permute-start | bytes 786440 | tf_op jit(solution)/shard_map/ppermute | solution.py:38
  8.6 6.5 %collective-permute-start.4 = (bf16[256,512]{1,0:T(8,128)(2,1)S(1)}, bf16[256,512]{1,0:T(8,128)(2,1)S(1)}, u32[]{:S(2)}, u32[]{:S(2)}) collective-permute-start(bf16[256,512]{1,0:T(8,128)(2,1)S(1)} %get-tuple-element.40), channel_id=1, source_target_pairs={{0,1},{1,0},{2,3},{3,2},{4,5},{5,4},{6,7},{7,6},{8,16},{9,17},{10,... | collective-permute-start | bytes 786440 | tf_op jit(solution)/shard_map/ppermute | solution.py:38
  8.6 8.7 %collective-permute-start.5 = (bf16[256,512]{1,0:T(8,128)(2,1)S(1)}, bf16[256,512]{1,0:T(8,128)(2,1)S(1)}, u32[]{:S(2)}, u32[]{:S(2)}) collective-permute-start(bf16[256,512]{1,0:T(8,128)(2,1)S(1)} %get-tuple-element.41), channel_id=1, source_target_pairs={{0,4},{4,0},{8,12},{12,8},{16,20},{20,16},{24,28},{28,24},{1,5},{5... | collective-permute-start | bytes 786440 | tf_op jit(solution)/shard_map/ppermute | solution.py:43
  10.9 3.3 %collective-permute-start.6 = (bf16[32,128]{1,0:T(8,128)(2,1)S(1)}, bf16[32,128]{1,0:T(8,128)(2,1)S(1)}, u32[]{:S(2)}, u32[]{:S(2)}) collective-permute-start(bf16[32,128]{1,0:T(8,128)(2,1)S(1)} %pad_maximum_fusion), channel_id=1, source_target_pairs={{0,1},{1,0},{2,3},{3,2},{4,5},{5,4},{6,7},{7,6},{8,9},{9,8},{10,11... | collective-permute-start | bytes 24584 | tf_op jit(solution)/shard_map/ppermute | solution.py:43
  12.1 5.2 %copy-start = (bf16[1024,128]{1,0:T(8,128)(2,1)S(1)}, bf16[1024,128]{1,0:T(8,128)(2,1)}, u32[]{:S(2)}) copy-start(bf16[1024,128]{1,0:T(8,128)(2,1)} %sketch_ref.1) | copy-start | bytes 786436
  12.5 9.8 %collective-permute-start.10 = (bf16[256,512]{1,0:T(8,128)(2,1)S(1)}, bf16[256,512]{1,0:T(8,128)(2,1)S(1)}, u32[]{:S(2)}, u32[]{:S(2)}) collective-permute-start(bf16[256,512]{1,0:T(8,128)(2,1)S(1)} %shard_map.61.first_ref), channel_id=1, source_target_pairs={{0,8},{1,9},{2,10},{3,11},{4,12},{5,13},{6,14},{7,15},{8,0},{9,1},... | collective-permute-start | bytes 786440 | tf_op jit(solution)/shard_map/ppermute | solution.py:38
  14.2 8.2 %collective-permute-start.9 = (bf16[256,512]{1,0:T(8,128)(2,1)S(1)}, bf16[256,512]{1,0:T(8,128)(2,1)S(1)}, u32[]{:S(2)}, u32[]{:S(2)}) collective-permute-start(bf16[256,512]{1,0:T(8,128)(2,1)S(1)} %shard_map.61.first_ref), channel_id=1, source_target_pairs={{0,1},{1,0},{2,3},{3,2},{4,5},{5,4},{6,7},{7,6},{8,16},{9,17},{10,... | collective-permute-start | bytes 786440 | tf_op jit(solution)/shard_map/ppermute | solution.py:38
  20.7 1.4 %collective-permute-start.7 = (f32[2,2,2,32,128]{4,3,2,1,0:T(8,128)S(1)}, f32[2,2,2,32,128]{4,3,2,1,0:T(8,128)S(1)}, u32[]{:S(2)}, u32[]{:S(2)}) collective-permute-start(f32[2,2,2,32,128]{4,3,2,1,0:T(8,128)S(1)} %get-tuple-element.61), channel_id=1, source_target_pairs={{0,1},{1,0},{2,3},{3,2},{4,5},{5,4},{6,7},{7,6},{8,9},{9,8},{10,11... | collective-permute-start | bytes 393224 | tf_op jit(solution)/shard_map/ppermute | solution.py:43
  20.8 1.5 %collective-permute-start.8 = (f32[2,2,2,32,128]{4,3,2,1,0:T(8,128)S(1)}, f32[2,2,2,32,128]{4,3,2,1,0:T(8,128)S(1)}, u32[]{:S(2)}, u32[]{:S(2)}) collective-permute-start(f32[2,2,2,32,128]{4,3,2,1,0:T(8,128)S(1)} %get-tuple-element.62), channel_id=1, source_target_pairs={{0,1},{1,0},{2,3},{3,2},{4,5},{5,4},{6,7},{7,6},{8,9},{9,8},{10,11... | collective-permute-start | bytes 393224 | tf_op jit(solution)/shard_map/ppermute | solution.py:43
  22.4 7.2 %collective-permute-start.13 = (f32[2,2,32,128]{3,2,1,0:T(8,128)S(1)}, f32[2,2,32,128]{3,2,1,0:T(8,128)S(1)}, u32[]{:S(2)}, u32[]{:S(2)}) collective-permute-start(f32[2,2,32,128]{3,2,1,0:T(8,128)S(1)} %get-tuple-element.58), channel_id=1, source_target_pairs={{0,6},{1,7},{2,4},{3,5},{4,2},{5,3},{6,0},{7,1},{8,14},{9,15},{10,... | collective-permute-start | bytes 196616 | tf_op jit(solution)/shard_map/ppermute | solution.py:43
  25.0 5.0 %collective-permute-start.12 = (f32[2,2,32,128]{3,2,1,0:T(8,128)S(1)}, f32[2,2,32,128]{3,2,1,0:T(8,128)S(1)}, u32[]{:S(2)}, u32[]{:S(2)}) collective-permute-start(f32[2,2,32,128]{3,2,1,0:T(8,128)S(1)} %get-tuple-element.59), channel_id=1, source_target_pairs={{0,4},{1,5},{2,6},{3,7},{4,0},{5,1},{6,2},{7,3},{8,12},{9,13},{10,... | collective-permute-start | bytes 196616 | tf_op jit(solution)/shard_map/ppermute | solution.py:43
  25.5 4.5 %collective-permute-start.11 = (f32[2,2,32,128]{3,2,1,0:T(8,128)S(1)}, f32[2,2,32,128]{3,2,1,0:T(8,128)S(1)}, u32[]{:S(2)}, u32[]{:S(2)}) collective-permute-start(f32[2,2,32,128]{3,2,1,0:T(8,128)S(1)} %get-tuple-element.60), channel_id=1, source_target_pairs={{0,2},{1,3},{2,0},{3,1},{4,6},{5,7},{6,4},{7,5},{8,10},{9,11},{10,... | collective-permute-start | bytes 196616 | tf_op jit(solution)/shard_map/ppermute | solution.py:43
  26.0 8.8 %collective-permute-start.17 = (bf16[256,512]{1,0:T(8,128)(2,1)S(1)}, bf16[256,512]{1,0:T(8,128)(2,1)S(1)}, u32[]{:S(2)}, u32[]{:S(2)}) collective-permute-start(bf16[256,512]{1,0:T(8,128)(2,1)S(1)} %get-tuple-element.56), channel_id=1, source_target_pairs={{0,4},{4,0},{8,12},{12,8},{16,20},{20,16},{24,28},{28,24},{1,5},{5... | collective-permute-start | bytes 786440 | tf_op jit(solution)/shard_map/ppermute | solution.py:43
  30.0 7.5 %collective-permute-start.16 = (f32[32,128]{1,0:T(8,128)S(1)}, f32[32,128]{1,0:T(8,128)S(1)}, u32[]{:S(2)}, u32[]{:S(2)}) collective-permute-start(f32[32,128]{1,0:T(8,128)S(1)} %get-tuple-element.63), channel_id=1, source_target_pairs={{0,24},{1,25},{2,26},{3,27},{4,28},{5,29},{6,30},{7,31},{8,16},{9,... | collective-permute-start | bytes 49160 | tf_op jit(solution)/shard_map/ppermute | solution.py:43
  32.6 5.0 %collective-permute-start.15 = (f32[32,128]{1,0:T(8,128)S(1)}, f32[32,128]{1,0:T(8,128)S(1)}, u32[]{:S(2)}, u32[]{:S(2)}) collective-permute-start(f32[32,128]{1,0:T(8,128)S(1)} %get-tuple-element.64), channel_id=1, source_target_pairs={{0,16},{1,17},{2,18},{3,19},{4,20},{5,21},{6,22},{7,23},{8,24},{9,... | collective-permute-start | bytes 49160 | tf_op jit(solution)/shard_map/ppermute | solution.py:43
  33.5 4.1 %collective-permute-start.14 = (f32[32,128]{1,0:T(8,128)S(1)}, f32[32,128]{1,0:T(8,128)S(1)}, u32[]{:S(2)}, u32[]{:S(2)}) collective-permute-start(f32[32,128]{1,0:T(8,128)S(1)} %get-tuple-element.65), channel_id=1, source_target_pairs={{0,8},{1,9},{2,10},{3,11},{4,12},{5,13},{6,14},{7,15},{8,0},{9,1},... | collective-permute-start | bytes 49160 | tf_op jit(solution)/shard_map/ppermute | solution.py:43
